TPU v7x, 256 devices: a whole 4x4x8 slice. The times are simulated.
256 devices in a mesh: dp: 8 (over x, core), expert: 32 (over y, z).
Axes of the slice: x: 4, y: 4, z: 8, core: 2. Of those that a mesh axis runs over, the one named last changes fastest.
Arguments:
- tokens: bfloat16 [32768, 2048], P(('dp', 'expert')), may hold values from -6 to 6
- cotangent: bfloat16 [32768, 2048], P(('dp', 'expert')), may hold values from -1.5 to 1.5
- routing: int32 [32768, 2], P(('dp', 'expert')), may hold values from 0 to 19, all different within a row; in each aligned block of 128 rows (0 to 127, 128 to 255, ...) at most 16 rows name the same one
- gates: bfloat16 [32768, 2], P(('dp', 'expert')), may hold values from 0.19921875 to 1
- new_place: int32 [32], replicated, may hold values from 0 to 19, as said below
- old_place: int32 [20], replicated, may hold values from 0 to 19, each once
- weights: bfloat16 [3, 20, 2048, 768], P(None, None, ('dp', 'expert')), may hold values from -0.125 to 0.125
- first_moment: float32 [3, 20, 2048, 768], P(None, None, ('dp', 'expert')), may hold values from -6 to 6
- second_moment: float32 [3, 20, 2048, 768], P(None, None, ('dp', 'expert')), may hold values from 0.5 to 20
Outputs:
- input_grad: bfloat16 [32768, 2048], P(('dp', 'expert'))
- gate_grad: bfloat16 [32768, 2], P(('dp', 'expert'))
- slot_weights: bfloat16 [3, 32, 2048, 768], P(None, 'expert', 'dp')
- new_first: float32 [3, 20, 2048, 768], P(None, None, ('dp', 'expert'))
- new_second: float32 [3, 20, 2048, 768], P(None, None, ('dp', 'expert'))
Inputs may be any that keep to these rules, and one draw needn't show every extreme that they name: `routing`: A token's 2 experts differ; among the 128 tokens of one device no expert is named more than 16 times, a bound that some block reaches. `new_place`: every expert is served by one slot or more. `old_place`: each expert names exactly one row.
All inputs are finite; a program needn't handle non-finite values.
Results may differ from a plain program's by a relative error of at most 0.024.
Values may be sent and summed in bfloat16 or wider, within the bound.
No kernel may reach another device: no remote copies, remote signals or barrier semaphores. Data moves between devices by JAX's collectives and lax.ppermute only.
A program may use at most 128 MiB of HBM per device.

v0:
```python
import jax
import jax.numpy as jnp
from jax import lax
from jax.sharding import PartitionSpec as P

beta_one = 0.9
beta_two = 0.95
learn_rate = 0.02
adam_step = 10.0
adam_eps = 1e-08


def expert_rows(inputs, upstream, gate_vals, stacked):
    first_pre = jnp.dot(inputs, stacked[0], preferred_element_type=jnp.float32)
    second_pre = jnp.dot(inputs, stacked[1], preferred_element_type=jnp.float32)
    back_proj = jnp.dot(upstream, stacked[2], preferred_element_type=jnp.float32)
    sigmoid_h = jax.nn.sigmoid(first_pre)
    activated = first_pre * sigmoid_h * second_pre
    gate_part = jnp.sum(activated * back_proj, axis=1).astype(jnp.bfloat16)
    weighted = gate_vals[:, None] * back_proj
    grad_second = (weighted * first_pre * sigmoid_h).astype(jnp.bfloat16)
    grad_first = (weighted * second_pre * sigmoid_h * (1.0 + first_pre * (1.0 - sigmoid_h))).astype(
        jnp.bfloat16
    )
    scaled_act = (gate_vals[:, None] * activated).astype(jnp.bfloat16)
    input_part = (
        jnp.einsum("rh,dh->rd", grad_first, stacked[0], preferred_element_type=jnp.float32)
        + jnp.einsum("rh,dh->rd", grad_second, stacked[1], preferred_element_type=jnp.float32)
    ).astype(jnp.bfloat16)
    weight_grads = jnp.stack(
        [
            jnp.einsum("rd,rh->dh", inputs, grad_first, preferred_element_type=jnp.float32),
            jnp.einsum("rd,rh->dh", inputs, grad_second, preferred_element_type=jnp.float32),
            jnp.einsum("rd,rh->dh", upstream, scaled_act, preferred_element_type=jnp.float32),
        ]
    )
    return (input_part, gate_part, weight_grads)


def adam_update(grad, stored, first, second):
    new_first = beta_one * first + (1.0 - beta_one) * grad
    new_second = beta_two * second + (1.0 - beta_two) * grad * grad
    first_hat = new_first / (1.0 - beta_one**adam_step)
    second_hat = new_second / (1.0 - beta_two**adam_step)
    updated = (
        stored.astype(jnp.float32) - learn_rate * first_hat / (jnp.sqrt(second_hat) + adam_eps)
    ).astype(jnp.bfloat16)
    return (updated, new_first, new_second)


def body(
    tokens, cotangent, routing, gates, new_place, old_place, weights, first_moment, second_moment
):
    tok_count, feature_width = tokens.shape
    top_count = routing.shape[1]
    expert_count = weights.shape[1]
    block_rows = weights.shape[2]
    hidden = weights.shape[3]
    slot_count = lax.axis_size("expert")
    data_count = lax.axis_size("dp")
    capacity = 2 * tok_count * top_count // slot_count
    buffer_rows = slot_count * capacity
    source = lax.axis_index("expert")
    expert_ids = jnp.arange(expert_count, dtype=jnp.int32)
    slot_ids = jnp.arange(slot_count, dtype=jnp.int32)
    place_hot = (new_place[:, None] == expert_ids[None, :]).astype(jnp.int32)
    slot_state = (new_place[:, None] == old_place[None, :]).astype(jnp.bfloat16)
    gathered = lax.all_gather(weights, "dp", axis=2, tiled=True)
    shaped = gathered.reshape(3, expert_count, data_count, block_rows, hidden)
    outgoing = jnp.einsum(
        "se,cedrh->cdsrh", slot_state, shaped, preferred_element_type=jnp.float32
    ).astype(jnp.bfloat16)
    arrived = lax.all_to_all(outgoing, "expert", split_axis=2, concat_axis=2, tiled=True)
    stacked = arrived.reshape(3, feature_width, hidden)
    replica_count = jnp.sum(place_hot, axis=0)
    earlier = jnp.cumsum(place_hot, axis=0) - place_hot
    slot_rank = jnp.sum(earlier * place_hot, axis=1)
    wanted = source % replica_count
    chosen = place_hot * (slot_rank[:, None] == wanted[None, :]).astype(jnp.int32)
    target_slot = jnp.sum(chosen * slot_ids[:, None], axis=0)
    flat_experts = routing.reshape(-1)
    assign_hot = (flat_experts[:, None] == expert_ids[None, :]).astype(jnp.int32)
    position = jnp.sum((jnp.cumsum(assign_hot, axis=0) - assign_hot) * assign_hot, axis=1)
    destination = jnp.sum(assign_hot * target_slot[None, :], axis=1) * capacity + position
    assign_dest = (
        destination[:, None] == jnp.arange(buffer_rows, dtype=jnp.int32)[None, :]
    ).astype(jnp.bfloat16)
    token_dest = jnp.sum(assign_dest.reshape(tok_count, top_count, buffer_rows), axis=1)
    send_tokens = jnp.einsum(
        "tb,td->bd", token_dest, tokens, preferred_element_type=jnp.float32
    ).astype(jnp.bfloat16)
    send_upstream = jnp.einsum(
        "tb,td->bd", token_dest, cotangent, preferred_element_type=jnp.float32
    ).astype(jnp.bfloat16)
    send_gates = jnp.einsum(
        "ab,a->b", assign_dest, gates.reshape(-1), preferred_element_type=jnp.float32
    ).astype(jnp.bfloat16)
    recv_tokens, recv_upstream, recv_gates = (
        lax.all_to_all(
            send_tokens.reshape(slot_count, capacity, feature_width),
            "expert",
            split_axis=0,
            concat_axis=0,
            tiled=True,
        ),
        lax.all_to_all(
            send_upstream.reshape(slot_count, capacity, feature_width),
            "expert",
            split_axis=0,
            concat_axis=0,
            tiled=True,
        ),
        lax.all_to_all(
            send_gates.reshape(slot_count, capacity),
            "expert",
            split_axis=0,
            concat_axis=0,
            tiled=True,
        ),
    )
    input_part, gate_part, weight_grads = expert_rows(
        recv_tokens.reshape(buffer_rows, feature_width),
        recv_upstream.reshape(buffer_rows, feature_width),
        recv_gates.reshape(-1).astype(jnp.float32),
        stacked,
    )
    back_rows, back_gates = (
        lax.all_to_all(
            input_part.reshape(slot_count, capacity, feature_width),
            "expert",
            split_axis=0,
            concat_axis=0,
            tiled=True,
        ),
        lax.all_to_all(
            gate_part.reshape(slot_count, capacity),
            "expert",
            split_axis=0,
            concat_axis=0,
            tiled=True,
        ),
    )
    input_grad = jnp.einsum(
        "tb,bd->td",
        token_dest,
        back_rows.reshape(buffer_rows, feature_width),
        preferred_element_type=jnp.float32,
    ).astype(jnp.bfloat16)
    gate_grad = (
        jnp.einsum(
            "ab,b->a", assign_dest, back_gates.reshape(-1), preferred_element_type=jnp.float32
        )
        .astype(jnp.bfloat16)
        .reshape(tok_count, top_count)
    )
    summed = lax.psum_scatter(
        weight_grads.astype(jnp.bfloat16), "dp", scatter_dimension=1, tiled=True
    )
    pieces = summed.reshape(3, slot_count, block_rows, hidden)
    returned = lax.all_to_all(pieces, "expert", split_axis=1, concat_axis=1, tiled=True)
    grad_state = jnp.einsum(
        "se,csrh->cerh", slot_state, returned, preferred_element_type=jnp.float32
    )
    updated, new_first, new_second = adam_update(grad_state, weights, first_moment, second_moment)
    leaving = jnp.einsum(
        "se,cerh->csrh", slot_state, updated, preferred_element_type=jnp.float32
    ).astype(jnp.bfloat16)
    landed = lax.all_to_all(leaving, "expert", split_axis=1, concat_axis=1, tiled=True)
    slot_weights = landed.reshape(3, 1, slot_count * block_rows, hidden)
    return (input_grad, gate_grad, slot_weights, new_first, new_second)


def solution(mesh):
    placed = (
        P(("dp", "expert"), None),
        P(("dp", "expert"), None),
        P(("dp", "expert"), None),
        P(("dp", "expert"), None),
        P(),
        P(),
        P(None, None, ("dp", "expert"), None),
        P(None, None, ("dp", "expert"), None),
        P(None, None, ("dp", "expert"), None),
    )
    return jax.shard_map(
        body,
        mesh=mesh,
        in_specs=placed,
        out_specs=(
            P(("dp", "expert"), None),
            P(("dp", "expert"), None),
            P(None, "expert", "dp", None),
            P(None, None, ("dp", "expert"), None),
            P(None, None, ("dp", "expert"), None),
        ),
        check_vma=False,
    )
```

profile of v0, /device:TPU:2, one launch (start us, length us, event | category | flops | bytes accessed | tf_op | source)
XLA Modules:
  0.0 589.9 jit_solution(8080591321334625019)
XLA Ops:
  7.2 0.7 all-gather.2.cloned.1.call-update
  7.9 0.8 copy.69
  9.0 0.7 fusion.22
  9.8 0.6 reduce-window.6
  10.4 0.2 slice_reduce_fusion
  10.7 0.8 copy.73
  11.5 0.1 reshape.149
  11.7 0.9 fusion.19
  12.7 0.7 fusion.21
  13.5 0.3 fusion.10
  13.8 0.7 all_to_all.37
  14.5 11.5 %all-to-all-start = ((bf16[32,1,16]{2,1,0:T(2,128)(2,1)}), bf16[32,1,16]{2,1,0:T(2,128)(2,1)S(1)}, u32[]{:S(2)}, u32[]{:S(2)}) async-start(bf16[32,1,16]{2,1,0:T(2,128)(2,1)} %all_to_all.37), calls=%async_computation | async-start | bytes 32768 | tf_op jit(solution)/shard_map/all_to_all | solution.py:113
  26.2 0.1 fusion.12
  26.3 2.0 convolution_convert_fusion.3
  28.4 7.3 %all-to-all-done = bf16[32,1,16]{2,1,0:T(2,128)(2,1)S(1)} async-done(((bf16[32,1,16]{2,1,0:T(2,128)(2,1)}), bf16[32,1,16]{2,1,0:T(2,128)(2,1)S(1)}, u32[]{:S(2)}, u32[]{:S(2)}) %all-to-all-start) | async-done | bytes 1056 | tf_op jit(solution)/shard_map/all_to_all | solution.py:113
  35.7 4.2 all-to-all-start.3
  39.9 13.8 %all-gather.2.cloned.1.call-done = bf16[3,20,64,768]{3,2,1,0:T(8,128)(2,1)} async-done(((bf16[3,20,8,768]{3,2,1,0:T(8,128)(2,1)}), bf16[3,20,64,768]{3,2,1,0:T(8,128)(2,1)}) %all-gather.2.cloned.1.call-update) | async-done | bytes 5898256 | tf_op jit(solution)/shard_map/all_gather | solution.py:68
  53.7 6.1 %copy.75 = bf16[3,20,64,768]{3,1,2,0:T(8,128)(2,1)S(1)} copy(bf16[3,20,64,768]{3,2,1,0:T(8,128)(2,1)} %all-gather.2.cloned.1.call-done) | data formatting | bytes 11796480 | tf_op jit(solution)/shard_map/all_gather | solution.py:68
  59.8 5.3 convert_bitcast_fusion
  65.2 12.6 %copy.77 = bf16[3,8,32,8,768]{4,3,1,0,2:T(8,128)(2,1)} copy(bf16[3,8,32,8,768]{4,2,3,1,0:T(8,128)(2,1)} %convert_bitcast_fusion) | data formatting | bytes 18874368 | tf_op jit(solution)/shard_map/convert_element_type | solution.py:72
  77.8 11.2 %all-to-all-done.3 = bf16[32,16,2048]{2,1,0:T(8,128)(2,1)S(1)} async-done(((bf16[32,16,2048]{2,1,0:T(8,128)(2,1)}), bf16[32,16,2048]{2,1,0:T(8,128)(2,1)S(1)}, u32[]{:S(2)}, u32[]{:S(2)}) %all-to-all-start.3) | async-done | bytes 2097184 | tf_op jit(solution)/shard_map/all_to_all | solution.py:99
  89.0 6.0 %all-to-all-start.2 = ((bf16[3,8,32,8,768]{4,3,1,0,2:T(8,128)(2,1)}), bf16[3,8,32,8,768]{4,3,1,0,2:T(8,128)(2,1)}, u32[]{:S(2)}, u32[]{:S(2)}) async-start(bf16[3,8,32,8,768]{4,3,1,0,2:T(8,128)(2,1)} %copy.77), calls=%async_computation.2 | async-start | bytes 18874368 | tf_op jit(solution)/shard_map/all_to_all | solution.py:73
  95.0 2.0 convolution_convert_fusion.4
  97.0 208.6 %all-to-all-done.2 = bf16[3,8,32,8,768]{4,3,1,0,2:T(8,128)(2,1)} async-done(((bf16[3,8,32,8,768]{4,3,1,0,2:T(8,128)(2,1)}), bf16[3,8,32,8,768]{4,3,1,0,2:T(8,128)(2,1)}, u32[]{:S(2)}, u32[]{:S(2)}) %all-to-all-start.2) | async-done | bytes 9437216 | tf_op jit(solution)/shard_map/all_to_all | solution.py:73
  305.7 13.5 %all-to-all-start.1 = ((bf16[32,16,2048]{2,1,0:T(8,128)(2,1)}), bf16[32,16,2048]{2,1,0:T(8,128)(2,1)}, u32[]{:S(2)}, u32[]{:S(2)}) async-start(bf16[32,16,2048]{2,1,0:T(8,128)(2,1)} %bitcast.2), calls=%async_computation.1 | async-start | bytes 4194304 | tf_op jit(solution)/shard_map/all_to_all | solution.py:106
  319.2 0.3 reduce-scatter.2.cloned.1.call-start
  319.6 4.2 fusion.32
  323.7 0.2 copy.102
  324.0 0.2 copy.103
  324.2 2.1 copy.101
  326.3 0.3 copy-done.7
  326.6 2.9 fusion.33
  329.5 3.0 fusion.34
  332.5 36.1 %all-to-all-done.1 = bf16[32,16,2048]{2,1,0:T(8,128)(2,1)} async-done(((bf16[32,16,2048]{2,1,0:T(8,128)(2,1)}), bf16[32,16,2048]{2,1,0:T(8,128)(2,1)}, u32[]{:S(2)}, u32[]{:S(2)}) %all-to-all-start.1) | async-done | bytes 2097184 | tf_op jit(solution)/shard_map/all_to_all | solution.py:106
  368.7 4.7 fusion.2
  373.4 4.0 multiply_reduce_fusion
  377.4 1.8 fusion.1
  379.3 1.8 fusion
  381.1 4.6 pad_maximum_fusion
  385.8 0.7 convert_element_type.112
  386.5 6.1 %all-to-all-start.5 = ((bf16[32,1,16]{2,1,0:T(2,128)(2,1)}), bf16[32,1,16]{2,1,0:T(2,128)(2,1)S(1)}, u32[]{:S(2)}, u32[]{:S(2)}) async-start(bf16[32,1,16]{2,1,0:T(2,128)(2,1)} %convert_element_type.112), calls=%async_computation.5 | async-start | bytes 32768 | tf_op jit(solution)/shard_map/all_to_all | solution.py:135
  392.6 48.3 %reduce-scatter.2.cloned.1.call-done = bf16[3,256,768]{2,1,0:T(8,128)(2,1)} async-done(((bf16[3,2048,768]{2,1,0:T(8,128)(2,1)}), bf16[3,256,768]{2,1,0:T(8,128)(2,1)}) %reduce-scatter.2.cloned.1.call-update) | async-done | bytes 1179664 | tf_op jit(solution)/shard_map/reduce_scatter | solution.py:156
  440.9 2.4 copy.84
  443.2 10.1 %all-to-all-start.6 = ((bf16[3,32,8,768]{3,2,0,1:T(8,128)(2,1)}), bf16[3,32,8,768]{3,2,0,1:T(8,128)(2,1)S(1)}, u32[]{:S(2)}, u32[]{:S(2)}) async-start(bf16[3,32,8,768]{3,2,0,1:T(8,128)(2,1)} %copy.84), calls=%async_computation.7 | async-start | bytes 2359296 | tf_op jit(solution)/shard_map/all_to_all | solution.py:160
  453.3 4.1 fusion.35
  457.5 3.2 add_convert_fusion
  460.7 25.1 %all-to-all-done.6 = bf16[3,32,8,768]{3,2,0,1:T(8,128)(2,1)S(1)} async-done(((bf16[3,32,8,768]{3,2,0,1:T(8,128)(2,1)}), bf16[3,32,8,768]{3,2,0,1:T(8,128)(2,1)S(1)}, u32[]{:S(2)}, u32[]{:S(2)}) %all-to-all-start.6) | async-done | bytes 1179680 | tf_op jit(solution)/shard_map/all_to_all | solution.py:160
  485.7 1.0 copy-done.6
  486.7 5.6 all-to-all-start.4
  492.4 3.8 fusion.4
  496.2 1.4 fusion.5
  497.6 0.4 copy-done.4
  498.0 1.7 copy.89
  499.7 43.0 %all-to-all-done.4 = bf16[32,16,2048]{2,1,0:T(8,128)(2,1)S(1)} async-done(((bf16[32,16,2048]{2,1,0:T(8,128)(2,1)}), bf16[32,16,2048]{2,1,0:T(8,128)(2,1)S(1)}, u32[]{:S(2)}, u32[]{:S(2)}) %all-to-all-start.4) | async-done | bytes 2097184 | tf_op jit(solution)/shard_map/all_to_all | solution.py:128
  542.7 6.3 %all-to-all-start.7 = ((bf16[3,32,8,768]{3,2,0,1:T(8,128)(2,1)}), bf16[3,32,8,768]{3,2,0,1:T(8,128)(2,1)}, u32[]{:S(2)}, u32[]{:S(2)}) async-start(bf16[3,32,8,768]{3,2,0,1:T(8,128)(2,1)} %copy.89), calls=%async_computation.8 | async-start | bytes 2359296 | tf_op jit(solution)/shard_map/all_to_all | solution.py:168
  549.1 0.3 fusion.9
  549.4 0.2 reshape.145
  549.6 0.6 copy.91
  550.2 1.2 convolution_convert_fusion.5
  551.4 0.4 copy-done.5
  551.8 1.6 copy.93
  553.5 1.6 copy.94
  555.0 25.2 %all-to-all-done.7 = bf16[3,32,8,768]{3,2,0,1:T(8,128)(2,1)} async-done(((bf16[3,32,8,768]{3,2,0,1:T(8,128)(2,1)}), bf16[3,32,8,768]{3,2,0,1:T(8,128)(2,1)}, u32[]{:S(2)}, u32[]{:S(2)}) %all-to-all-start.7) | async-done | bytes 1179680 | tf_op jit(solution)/shard_map/all_to_all | solution.py:168
  580.2 2.4 copy.118
  (60 shorter events, 1.4 us)
Async XLA Ops:
  7.2 19.2 %copy-start = (bf16[128,2048]{1,0:T(8,128)(2,1)S(1)}, bf16[128,2048]{1,0:T(8,128)(2,1)}, u32[]{:S(2)}) copy-start(bf16[128,2048]{1,0:T(8,128)(2,1)} %param.9) | copy-start | bytes 1572868
  7.2 46.5 %all-gather.2.cloned.1.call-start = ((), (), s32[]{:S(2)}) async-start(), calls=%async_computation.9 | async-start | bytes 6635520 | tf_op jit(solution)/shard_map/all_gather | solution.py:68
  14.5 21.2 %all-to-all-start = ((bf16[32,1,16]{2,1,0:T(2,128)(2,1)}), bf16[32,1,16]{2,1,0:T(2,128)(2,1)S(1)}, u32[]{:S(2)}, u32[]{:S(2)}) async-start(bf16[32,1,16]{2,1,0:T(2,128)(2,1)} %all_to_all.37), calls=%async_computation | async-start | bytes 32768 | tf_op jit(solution)/shard_map/all_to_all | solution.py:113
  35.7 53.4 %all-to-all-start.3 = ((bf16[32,16,2048]{2,1,0:T(8,128)(2,1)}), bf16[32,16,2048]{2,1,0:T(8,128)(2,1)S(1)}, u32[]{:S(2)}, u32[]{:S(2)}) async-start(bf16[32,16,2048]{2,1,0:T(8,128)(2,1)} %bitcast.8), calls=%async_computation.3 | async-start | bytes 4194304 | tf_op jit(solution)/shard_map/all_to_all | solution.py:99
  39.9 20.0 %copy-start.13 = (s32[32]{0:T(128)S(1)}, s32[32]{0:T(128)}, u32[]{:S(2)}) copy-start(s32[32]{0:T(128)} %param.13) | copy-start | bytes 388
  39.9 20.0 %copy-start.14 = (s32[20]{0:T(128)S(1)}, s32[20]{0:T(128)}, u32[]{:S(2)}) copy-start(s32[20]{0:T(128)} %param.14) | copy-start | bytes 244
  77.8 17.2 %copy-start.12 = (bf16[128,2048]{1,0:T(8,128)(2,1)S(1)}, bf16[128,2048]{1,0:T(8,128)(2,1)}, u32[]{:S(2)}) copy-start(bf16[128,2048]{1,0:T(8,128)(2,1)} %param.10) | copy-start | bytes 1572868
  89.0 216.6 %all-to-all-start.2 = ((bf16[3,8,32,8,768]{4,3,1,0,2:T(8,128)(2,1)}), bf16[3,8,32,8,768]{4,3,1,0,2:T(8,128)(2,1)}, u32[]{:S(2)}, u32[]{:S(2)}) async-start(bf16[3,8,32,8,768]{4,3,1,0,2:T(8,128)(2,1)} %copy.77), calls=%async_computation.2 | async-start | bytes 18874368 | tf_op jit(solution)/shard_map/all_to_all | solution.py:73
  305.7 63.0 %all-to-all-start.1 = ((bf16[32,16,2048]{2,1,0:T(8,128)(2,1)}), bf16[32,16,2048]{2,1,0:T(8,128)(2,1)}, u32[]{:S(2)}, u32[]{:S(2)}) async-start(bf16[32,16,2048]{2,1,0:T(8,128)(2,1)} %bitcast.2), calls=%async_computation.1 | async-start | bytes 4194304 | tf_op jit(solution)/shard_map/all_to_all | solution.py:106
  319.2 121.7 %reduce-scatter.2.cloned.1.call-start = ((), (), s32[]{:S(2)}) async-start(), calls=%async_computation.10 | async-start | bytes 10616832 | tf_op jit(solution)/shard_map/reduce_scatter | solution.py:156
  324.0 2.7 copy-start.7
  324.2 5.4 copy-start.9
  368.7 4.7 copy-start.10
  368.7 4.7 copy-start.18
  368.7 4.7 copy-start.19
  377.4 1.9 copy-start.15
  377.4 1.9 copy-start.17
  386.5 56.7 %all-to-all-start.5 = ((bf16[32,1,16]{2,1,0:T(2,128)(2,1)}), bf16[32,1,16]{2,1,0:T(2,128)(2,1)S(1)}, u32[]{:S(2)}, u32[]{:S(2)}) async-start(bf16[32,1,16]{2,1,0:T(2,128)(2,1)} %convert_element_type.112), calls=%async_computation.5 | async-start | bytes 32768 | tf_op jit(solution)/shard_map/all_to_all | solution.py:135
  443.2 42.5 %all-to-all-start.6 = ((bf16[3,32,8,768]{3,2,0,1:T(8,128)(2,1)}), bf16[3,32,8,768]{3,2,0,1:T(8,128)(2,1)S(1)}, u32[]{:S(2)}, u32[]{:S(2)}) async-start(bf16[3,32,8,768]{3,2,0,1:T(8,128)(2,1)} %copy.84), calls=%async_computation.7 | async-start | bytes 2359296 | tf_op jit(solution)/shard_map/all_to_all | solution.py:160
  453.3 4.1 copy-start.8
  453.3 4.1 copy-start.16
  485.7 1.0 copy-start.6
  486.7 56.0 %all-to-all-start.4 = ((bf16[32,16,2048]{2,1,0:T(8,128)(2,1)}), bf16[32,16,2048]{2,1,0:T(8,128)(2,1)S(1)}, u32[]{:S(2)}, u32[]{:S(2)}) async-start(bf16[32,16,2048]{2,1,0:T(8,128)(2,1)} %bitcast.87), calls=%async_computation.4 | async-start | bytes 4194304 | tf_op jit(solution)/shard_map/all_to_all | solution.py:128
  492.4 3.8 copy-start.11
  496.2 1.4 copy-start.2
  496.2 1.8 copy-start.4
  542.7 37.5 %all-to-all-start.7 = ((bf16[3,32,8,768]{3,2,0,1:T(8,128)(2,1)}), bf16[3,32,8,768]{3,2,0,1:T(8,128)(2,1)}, u32[]{:S(2)}, u32[]{:S(2)}) async-start(bf16[3,32,8,768]{3,2,0,1:T(8,128)(2,1)} %copy.89), calls=%async_computation.8 | async-start | bytes 2359296 | tf_op jit(solution)/shard_map/all_to_all | solution.py:168
  550.2 1.6 copy-start.5
  551.8 1.6 copy-start.3
  551.8 30.8 %copy-start.1 = (bf16[128,2048]{1,0:T(8,128)(2,1)S(1)}, bf16[128,2048]{1,0:T(8,128)(2,1)}, u32[]{:S(2)}) copy-start(bf16[128,2048]{1,0:T(8,128)(2,1)} %param.9) | copy-start | bytes 1572868
Sparse Core Ops, SparseCore 0:
  9.9 43.8 all-gather.1
  385.9 54.9 reduce-scatter.1
where the time goes:
time: 594 us; the launch traced here: 590 us
  waiting for transfers between devices  419 us (71%)
  starting transfers between devices  63.6 us (11%)
  local copies, waits for them, and re-layouts  41.9 us (7%)
  matrix products  41.9 us (7%)
  between operations  14.9 us (3%)
  other arithmetic  8.21 us (1%)
    all_to_all x1, waiting for transfers between devices, body(): lax.all_to_all(outgoing, 'expert', split_axis=2, concat_axis=2, tiled=True)  209 us
    reduce_scatter x1, waiting for transfers between devices, body(): lax.psum_scatter(weight_grads.astype(jnp.bfloat16), 'dp', scatter_dimensi...  48.3 us
    all_to_all x1, waiting for transfers between devices, body(): lax.all_to_all(input_part.reshape(slot_count, capacity, feature_width), '...  43 us
    all_to_all x1, waiting for transfers between devices, body(): lax.all_to_all(send_upstream.reshape(slot_count, capacity, feature_width)...  36.1 us
    all_to_all x1, waiting for transfers between devices, body(): lax.all_to_all(leaving, 'expert', split_axis=1, concat_axis=1, tiled=True)  25.2 us
    all_to_all x1, waiting for transfers between devices, body(): lax.all_to_all(pieces, 'expert', split_axis=1, concat_axis=1, tiled=True)  25.1 us
    all_gather x1, waiting for transfers between devices, body(): gathered = lax.all_gather(weights, 'dp', axis=2, tiled=True)  13.8 us
    all_to_all x1, starting transfers between devices, body(): lax.all_to_all(send_upstream.reshape(slot_count, capacity, feature_width)...  13.5 us
  transfers between devices with their start and end apart: 10, of which 9 were waited for; matrix products, arithmetic and copies ran while one was open for 12% of the time, Pallas kernels for 0%

commit v1 on v0

v1 whole, which is shorter than its diff:
```python
import jax
import jax.numpy as jnp
from jax import lax
from jax.sharding import PartitionSpec as P

beta_one = 0.9
beta_two = 0.95
learn_rate = 0.02
adam_step = 10.0
adam_eps = 1e-08


def adam_update(grad, stored, first, second):
    new_first = beta_one * first + (1.0 - beta_one) * grad
    new_second = beta_two * second + (1.0 - beta_two) * grad * grad
    first_hat = new_first / (1.0 - beta_one**adam_step)
    second_hat = new_second / (1.0 - beta_two**adam_step)
    updated = (
        stored.astype(jnp.float32) - learn_rate * first_hat / (jnp.sqrt(second_hat) + adam_eps)
    ).astype(jnp.bfloat16)
    return (updated, new_first, new_second)


def body(
    tokens, cotangent, routing, gates, new_place, old_place, weights, first_moment, second_moment
):
    tok_count, feature_width = tokens.shape
    top_count = routing.shape[1]
    expert_count = weights.shape[1]
    block_rows = weights.shape[2]
    hidden = weights.shape[3]
    slot_count = lax.axis_size("expert")
    capacity = 2 * tok_count * top_count // slot_count
    buffer_rows = slot_count * capacity
    source = lax.axis_index("expert")
    expert_ids = jnp.arange(expert_count, dtype=jnp.int32)
    slot_ids = jnp.arange(slot_count, dtype=jnp.int32)
    place_hot = (new_place[:, None] == expert_ids[None, :]).astype(jnp.int32)
    slot_state = (new_place[:, None] == old_place[None, :]).astype(jnp.bfloat16)

    outgoing = jnp.einsum(
        "se,cerh->scrh", slot_state, weights, preferred_element_type=jnp.float32
    ).astype(jnp.bfloat16)
    arrived = lax.all_to_all(outgoing, "expert", split_axis=0, concat_axis=0, tiled=True)
    gate_w, up_w, down_w = [
        lax.all_gather(
            arrived[:, c].reshape(slot_count * block_rows, hidden), "dp", axis=0, tiled=True
        )
        for c in range(3)
    ]

    replica_count = jnp.sum(place_hot, axis=0)
    earlier = jnp.cumsum(place_hot, axis=0) - place_hot
    slot_rank = jnp.sum(earlier * place_hot, axis=1)
    wanted = source % replica_count
    chosen = place_hot * (slot_rank[:, None] == wanted[None, :]).astype(jnp.int32)
    target_slot = jnp.sum(chosen * slot_ids[:, None], axis=0)
    flat_experts = routing.reshape(-1)
    assign_hot = (flat_experts[:, None] == expert_ids[None, :]).astype(jnp.int32)
    position = jnp.sum((jnp.cumsum(assign_hot, axis=0) - assign_hot) * assign_hot, axis=1)
    destination = jnp.sum(assign_hot * target_slot[None, :], axis=1) * capacity + position
    assign_dest = (
        destination[:, None] == jnp.arange(buffer_rows, dtype=jnp.int32)[None, :]
    ).astype(jnp.bfloat16)
    split_dest = assign_dest.reshape(tok_count, top_count, buffer_rows)
    token_dest = jnp.sum(split_dest, axis=1)
    gated_dest = jnp.sum(split_dest * gates[:, :, None], axis=1)

    def dispatch(where, rows):
        sent = jnp.einsum(
            "tb,td->bd", where, rows, preferred_element_type=jnp.float32
        ).astype(jnp.bfloat16)
        return lax.all_to_all(
            sent.reshape(slot_count, capacity, feature_width),
            "expert",
            split_axis=0,
            concat_axis=0,
            tiled=True,
        ).reshape(buffer_rows, feature_width)

    inputs = dispatch(token_dest, tokens)
    upstream = dispatch(gated_dest, cotangent)

    first_pre = jnp.dot(inputs, gate_w, preferred_element_type=jnp.float32)
    second_pre = jnp.dot(inputs, up_w, preferred_element_type=jnp.float32)
    weighted = jnp.dot(upstream, down_w, preferred_element_type=jnp.float32)
    sigmoid_h = jax.nn.sigmoid(first_pre)
    activated = first_pre * sigmoid_h * second_pre
    gate_part = jnp.sum(activated * weighted, axis=1).astype(jnp.bfloat16)
    grad_second = (weighted * first_pre * sigmoid_h).astype(jnp.bfloat16)
    grad_first = (weighted * second_pre * sigmoid_h * (1.0 + first_pre * (1.0 - sigmoid_h))).astype(
        jnp.bfloat16
    )
    act_low = activated.astype(jnp.bfloat16)

    def weight_grad(rows, units):
        grad = jnp.einsum("rd,rh->dh", rows, units, preferred_element_type=jnp.float32)
        return lax.psum_scatter(
            grad.astype(jnp.bfloat16), "dp", scatter_dimension=0, tiled=True
        ).reshape(slot_count, 1, block_rows, hidden)

    pieces = jnp.concatenate(
        [
            weight_grad(inputs, grad_first),
            weight_grad(inputs, grad_second),
            weight_grad(upstream, act_low),
        ],
        axis=1,
    )
    input_part = (
        jnp.einsum("rh,dh->rd", grad_first, gate_w, preferred_element_type=jnp.float32)
        + jnp.einsum("rh,dh->rd", grad_second, up_w, preferred_element_type=jnp.float32)
    ).astype(jnp.bfloat16)
    back_rows = lax.all_to_all(
        input_part.reshape(slot_count, capacity, feature_width),
        "expert",
        split_axis=0,
        concat_axis=0,
        tiled=True,
    )
    back_gates = lax.all_to_all(
        gate_part.reshape(slot_count, capacity),
        "expert",
        split_axis=0,
        concat_axis=0,
        tiled=True,
    )
    input_grad = jnp.einsum(
        "tb,bd->td",
        token_dest,
        back_rows.reshape(buffer_rows, feature_width),
        preferred_element_type=jnp.float32,
    ).astype(jnp.bfloat16)
    gate_sum = jnp.einsum(
        "ab,b->a", assign_dest, back_gates.reshape(-1), preferred_element_type=jnp.float32
    ).reshape(tok_count, top_count)
    gate_grad = (gate_sum / gates.astype(jnp.float32)).astype(jnp.bfloat16)

    returned = lax.all_to_all(pieces, "expert", split_axis=0, concat_axis=0, tiled=True)
    grad_state = jnp.einsum(
        "se,scrh->cerh", slot_state, returned, preferred_element_type=jnp.float32
    )
    updated, new_first, new_second = adam_update(grad_state, weights, first_moment, second_moment)
    leaving = jnp.einsum(
        "se,cerh->scrh", slot_state, updated, preferred_element_type=jnp.float32
    ).astype(jnp.bfloat16)
    landed = lax.all_to_all(leaving, "expert", split_axis=0, concat_axis=0, tiled=True)
    slot_weights = jnp.transpose(landed, (1, 0, 2, 3)).reshape(
        3, 1, slot_count * block_rows, hidden
    )
    return (input_grad, gate_grad, slot_weights, new_first, new_second)


def solution(mesh):
    placed = (
        P(("dp", "expert"), None),
        P(("dp", "expert"), None),
        P(("dp", "expert"), None),
        P(("dp", "expert"), None),
        P(),
        P(),
        P(None, None, ("dp", "expert"), None),
        P(None, None, ("dp", "expert"), None),
        P(None, None, ("dp", "expert"), None),
    )
    return jax.shard_map(
        body,
        mesh=mesh,
        in_specs=placed,
        out_specs=(
            P(("dp", "expert"), None),
            P(("dp", "expert"), None),
            P(None, "expert", "dp", None),
            P(None, None, ("dp", "expert"), None),
            P(None, None, ("dp", "expert"), None),
        ),
        check_vma=False,
    )
```

time: 594 us -> 437 us (0.74)
  waiting for transfers between devices: 419 us -> 269 us
  blocking collectives: 0 us -> 44.2 us
  local copies, waits for them, and re-layouts: 41.9 us -> 12.6 us
  starting transfers between devices: 63.6 us -> 38 us
  matrix products: 41.9 us -> 50.6 us
    all_to_all x6 -> x4, waiting for transfers between devices: 314 us -> 137 us  [the longest x2 86.7 us: dispatch(): lax.all_to_all(sent.reshape(slot_count, capacity, feature_width), 'expert...]
    all_to_all x0 -> x1, blocking collectives: none -> 44.2 us  [body(): lax.all_to_all(outgoing, 'expert', split_axis=0, concat_axis=0, tiled=True)]
    reduce_scatter x1 -> x3, waiting for transfers between devices: 48.3 us -> 89.1 us  [weight_grad(): lax.psum_scatter(grad.astype(jnp.bfloat16), 'dp', scatter_dimension=0, ti...]
    all_to_all x6 -> x4, starting transfers between devices: 51.5 us -> 26.2 us  [the longest x2 10.2 us: dispatch(): lax.all_to_all(sent.reshape(slot_count, capacity, feature_width), 'expert...]
    all_gather x1 -> x3, waiting for transfers between devices: 13.8 us -> 0.04 us  [body(): lax.all_gather(arrived[:, c].reshape(slot_count * block_rows, hidden), 'd...]
    convert_element_type x4 -> x3, local copies, waits for them, and re-layouts: 15 us -> 3.01 us  [the longest x1 1.66 us: body(): leaving = jnp.einsum('se,cerh->scrh', slot_state, updated, preferred_elem...]
    dot_general x14 -> x13, matrix products: 40.4 us -> 49.1 us  [the longest x3 14.3 us: weight_grad(): jnp.einsum('rd,rh->dh', rows, units, preferred_element_type=jnp.float32)]
    all_gather x1 -> x0, local copies, waits for them, and re-layouts: 6.1 us -> none  [body(): gathered = lax.all_gather(weights, 'dp', axis=2, tiled=True)]
  transfers between devices with their start and end apart: 10 -> 12, of which waited for: 9 -> 8; matrix products, arithmetic and copies ran while one was open for 12% -> 14% of each run, Pallas kernels for 0% -> 0%
where the time goes in v1:
time: 437 us; the launch traced here: 434 us
  waiting for transfers between devices  269 us (62%)
  matrix products  50.6 us (12%)
  blocking collectives  44.2 us (10%)
  starting transfers between devices  38 us (9%)
  between operations  14.4 us (3%)
  local copies, waits for them, and re-layouts  12.6 us (3%)
  other arithmetic  4.47 us (1%)
    reduce_scatter x3, waiting for transfers between devices, weight_grad(): lax.psum_scatter(grad.astype(jnp.bfloat16), 'dp', scatter_dimension=0, ti...  89.1 us
    all_to_all x2, waiting for transfers between devices, dispatch(): lax.all_to_all(sent.reshape(slot_count, capacity, feature_width), 'expert...  86.7 us
    all_to_all x1, blocking collectives, body(): lax.all_to_all(outgoing, 'expert', split_axis=0, concat_axis=0, tiled=True)  44.2 us
    all_to_all x1, waiting for transfers between devices, body(): lax.all_to_all(input_part.reshape(slot_count, capacity, feature_width), '...  42.1 us
    all_to_all x1, waiting for transfers between devices, body(): lax.all_to_all(leaving, 'expert', split_axis=0, concat_axis=0, tiled=True)  25.6 us
    all_to_all x1, waiting for transfers between devices, body(): lax.all_to_all(pieces, 'expert', split_axis=0, concat_axis=0, tiled=True)  24.2 us
    dot_general x3, matrix products, weight_grad(): jnp.einsum('rd,rh->dh', rows, units, preferred_element_type=jnp.float32)  14.3 us
    all_to_all x2, starting transfers between devices, dispatch(): lax.all_to_all(sent.reshape(slot_count, capacity, feature_width), 'expert...  10.2 us
  transfers between devices with their start and end apart: 12, of which 8 were waited for; matrix products, arithmetic and copies ran while one was open for 14% of the time, Pallas kernels for 0%

profile of v1, /device:TPU:2, one launch (start us, length us, event | category | flops | bytes accessed | tf_op | source)
XLA Modules:
  0.0 433.6 jit_solution(12476758268169267142)
XLA Ops:
  7.2 1.7 convolution_convert_fusion.7
  8.9 0.7 copy.81
  9.6 44.2 %all_to_all.36 = bf16[32,3,8,768]{3,2,1,0:T(8,128)(2,1)S(1)} all-to-all(bf16[32,3,8,768]{3,2,1,0:T(8,128)(2,1)S(1)} %copy.81), channel_id=1, replica_groups=mesh['dp'=8,'expert'=32] {'expert'}, dimensions={0} | all-to-all | bytes 2359296 | tf_op jit(solution)/shard_map/all_to_all | solution.py:44
  53.8 1.0 slice_bitcast_fusion.1
  55.0 0.7 all-gather.6.cloned.1.call-update
  55.7 0.1 copy.75
  55.8 0.1 eq.117
  55.9 0.1 eq.106
  56.1 0.1 fusion.22
  56.1 0.1 reduce_window_sum.26
  56.2 0.6 reduce-window.6
  56.8 0.2 slice_reduce_fusion
  57.0 0.1 broadcast_add_fusion
  57.2 0.2 fusion.19
  57.4 0.1 and_select_fusion
  57.5 0.1 fusion.21
  57.6 0.1 select_reduce_fusion
  57.7 0.1 add.47
  57.8 0.1 copy.78
  57.9 0.2 fusion.13
  58.1 2.1 convolution_convert_fusion.3
  60.1 4.1 all-to-all-start.2
  64.3 0.7 all-gather.4.cloned.1.call-update
  65.0 2.1 convolution_convert_fusion.4
  67.1 46.8 %all-to-all-done.2 = bf16[32,16,2048]{2,1,0:T(8,128)(2,1)S(1)} async-done(((bf16[32,16,2048]{2,1,0:T(8,128)(2,1)}), bf16[32,16,2048]{2,1,0:T(8,128)(2,1)S(1)}, u32[]{:S(2)}, u32[]{:S(2)}) %all-to-all-start.2) | async-done | bytes 2097184 | tf_op jit(solution)/shard_map/all_to_all | solution.py:73
  113.9 6.1 %all-to-all-start = ((bf16[32,16,2048]{2,1,0:T(8,128)(2,1)}), bf16[32,16,2048]{2,1,0:T(8,128)(2,1)}, u32[]{:S(2)}, u32[]{:S(2)}) async-start(bf16[32,16,2048]{2,1,0:T(8,128)(2,1)} %bitcast.1), calls=%async_computation | async-start | bytes 4194304 | tf_op jit(solution)/shard_map/all_to_all | solution.py:73
  120.0 0.0 reduce-scatter.8.cloned.1.call-start
  120.1 4.8 %fusion.40 = f32[512,768]{1,0:T(8,128)} fusion(bf16[512,2048]{1,0:T(8,128)(2,1)S(1)} %bitcast.88, bf16[2048,768]{1,0:T(8,128)(2,1)} %all-gather.8.cloned.1.call-done), kind=kOutput, calls=%fused_computation.80 | convolution fusion | flops 1610612736 | bytes 6815744 | tf_op jit(solution)/shard_map/dot_general | solution.py:84
  124.9 4.8 %fusion.39 = f32[512,768]{1,0:T(8,128)} fusion(bf16[512,2048]{1,0:T(8,128)(2,1)S(1)} %bitcast.89, bf16[2048,768]{1,0:T(8,128)(2,1)} %all-gather.6.cloned.1.call-done), kind=kOutput, calls=%fused_computation.79 | convolution fusion | flops 1610612736 | bytes 6815744 | tf_op jit(solution)/shard_map/dot_general | solution.py:85
  129.7 39.9 %all-to-all-done = bf16[32,16,2048]{2,1,0:T(8,128)(2,1)} async-done(((bf16[32,16,2048]{2,1,0:T(8,128)(2,1)}), bf16[32,16,2048]{2,1,0:T(8,128)(2,1)}, u32[]{:S(2)}, u32[]{:S(2)}) %all-to-all-start) | async-done | bytes 2097184 | tf_op jit(solution)/shard_map/all_to_all | solution.py:73
  169.6 6.1 %convolution_convert_fusion = bf16[2048,768]{1,0:T(8,128)(2,1)} fusion(bf16[512,2048]{1,0:T(8,128)(2,1)} %bitcast.2, f32[512,768]{1,0:T(8,128)} %fusion.39, f32[512,768]{1,0:T(8,128)} %fusion.40), kind=kOutput, calls=%fused_computation.1 | convolution fusion | flops 1614544896 | bytes 8388608 | tf_op jit(solution)/shard_map/rd,rh->dh/dot_general | solution.py:97
  175.8 0.2 reduce-scatter.6.cloned.1.call-start
  176.1 6.6 %multiply_reduce_fusion = (bf16[512]{0:T(512)(128)(2,1)S(1)}, bf16[512,768]{1,0:T(8,128)(2,1)}, bf16[512,768]{1,0:T(8,128)(2,1)S(1)}) fusion(f32[512,768]{1,0:T(8,128)} %fusion.39, f32[512,768]{1,0:T(8,128)} %fusion.40, bf16[512,2048]{1,0:T(8,128)(2,1)} %bitcast.2, bf16[2048,768]{1,0:T(8,128)(2,1)} %all-gather.4.cloned.1.call-done), kind=kOutput, calls=%fused_computation.14 | convolution fusion | flops 1617296896 | bytes 9962496 | tf_op jit(solution)/shard_map/dot_general | solution.py:86
  182.7 0.9 copy-done.13
  183.5 3.5 convolution_convert_fusion.1
  187.1 4.6 %convolution_convert_fusion.2 = bf16[2048,768]{1,0:T(8,128)(2,1)} fusion(bf16[512,2048]{1,0:T(8,128)(2,1)S(1)} %bitcast.91, bf16[512,768]{1,0:T(8,128)(2,1)} %get-tuple-element.32), kind=kOutput, calls=%fused_computation.3 | convolution fusion | flops 1612185600 | bytes 6029312 | tf_op jit(solution)/shard_map/rd,rh->dh/dot_general | solution.py:97
  191.8 0.7 convert_element_type.104
  192.5 6.0 %all-to-all-start.4 = ((bf16[32,1,16]{2,1,0:T(2,128)(2,1)}), bf16[32,1,16]{2,1,0:T(2,128)(2,1)S(1)}, u32[]{:S(2)}, u32[]{:S(2)}) async-start(bf16[32,1,16]{2,1,0:T(2,128)(2,1)} %convert_element_type.104), calls=%async_computation.4 | async-start | bytes 32768 | tf_op jit(solution)/shard_map/all_to_all | solution.py:121
  198.5 9.8 %reduce-scatter.8.cloned.1.call-done = bf16[256,768]{1,0:T(8,128)(2,1)} async-done(((bf16[2048,768]{1,0:T(8,128)(2,1)}), bf16[256,768]{1,0:T(8,128)(2,1)}) %reduce-scatter.8.cloned.1.call-update) | async-done | bytes 393232 | tf_op jit(solution)/shard_map/reduce_scatter | solution.py:98
  208.3 39.8 %reduce-scatter.6.cloned.1.call-done = bf16[256,768]{1,0:T(8,128)(2,1)} async-done(((bf16[2048,768]{1,0:T(8,128)(2,1)}), bf16[256,768]{1,0:T(8,128)(2,1)}) %reduce-scatter.6.cloned.1.call-update) | async-done | bytes 393232 | tf_op jit(solution)/shard_map/reduce_scatter | solution.py:98
  248.1 39.6 %reduce-scatter.4.cloned.1.call-done = bf16[256,768]{1,0:T(8,128)(2,1)} async-done(((bf16[2048,768]{1,0:T(8,128)(2,1)}), bf16[256,768]{1,0:T(8,128)(2,1)}) %reduce-scatter.4.cloned.1.call-update) | async-done | bytes 393232 | tf_op jit(solution)/shard_map/reduce_scatter | solution.py:98
  287.6 2.4 pad_maximum_fusion
  290.0 9.8 %all-to-all-start.5 = ((bf16[32,3,8,768]{3,2,1,0:T(8,128)(2,1)}), bf16[32,3,8,768]{3,2,1,0:T(8,128)(2,1)S(1)}, u32[]{:S(2)}, u32[]{:S(2)}) async-start(bf16[32,3,8,768]{3,2,1,0:T(8,128)(2,1)} %pad_maximum_fusion), calls=%async_computation.8 | async-start | bytes 2359296 | tf_op jit(solution)/shard_map/all_to_all | solution.py:139
  299.9 4.1 fusion.41
  304.0 3.2 add_convert_fusion
  307.2 24.2 %all-to-all-done.5 = bf16[32,3,8,768]{3,2,1,0:T(8,128)(2,1)S(1)} async-done(((bf16[32,3,8,768]{3,2,1,0:T(8,128)(2,1)}), bf16[32,3,8,768]{3,2,1,0:T(8,128)(2,1)S(1)}, u32[]{:S(2)}, u32[]{:S(2)}) %all-to-all-start.5) | async-done | bytes 1179680 | tf_op jit(solution)/shard_map/all_to_all | solution.py:139
  331.4 1.0 copy-done.5
  332.4 5.4 %all-to-all-start.3 = ((bf16[32,16,2048]{2,1,0:T(8,128)(2,1)}), bf16[32,16,2048]{2,1,0:T(8,128)(2,1)S(1)}, u32[]{:S(2)}, u32[]{:S(2)}) async-start(bf16[32,16,2048]{2,1,0:T(8,128)(2,1)} %bitcast.92), calls=%async_computation.3 | async-start | bytes 4194304 | tf_op jit(solution)/shard_map/all_to_all | solution.py:114
  337.8 3.8 fusion.1
  341.6 1.6 convolution_convert_fusion.6
  343.3 0.2 copy-done.3
  343.4 1.7 copy.96
  345.1 42.1 %all-to-all-done.3 = bf16[32,16,2048]{2,1,0:T(8,128)(2,1)S(1)} async-done(((bf16[32,16,2048]{2,1,0:T(8,128)(2,1)}), bf16[32,16,2048]{2,1,0:T(8,128)(2,1)S(1)}, u32[]{:S(2)}, u32[]{:S(2)}) %all-to-all-start.3) | async-done | bytes 2097184 | tf_op jit(solution)/shard_map/all_to_all | solution.py:114
  387.2 6.1 %all-to-all-start.6 = ((bf16[32,3,8,768]{3,2,1,0:T(8,128)(2,1)}), bf16[32,3,8,768]{3,2,1,0:T(8,128)(2,1)}, u32[]{:S(2)}, u32[]{:S(2)}) async-start(bf16[32,3,8,768]{3,2,1,0:T(8,128)(2,1)} %copy.96), calls=%async_computation.9 | async-start | bytes 2359296 | tf_op jit(solution)/shard_map/all_to_all | solution.py:147
  393.3 0.1 reduce.3
  393.4 0.1 reshape.150
  393.5 0.3 fusion.10
  393.8 0.5 fusion.35
  394.3 1.2 convolution_convert_fusion.5
  395.5 1.6 copy.99
  397.1 0.1 copy-done.2
  397.2 1.6 copy.100
  398.7 25.6 %all-to-all-done.6 = bf16[32,3,8,768]{3,2,1,0:T(8,128)(2,1)} async-done(((bf16[32,3,8,768]{3,2,1,0:T(8,128)(2,1)}), bf16[32,3,8,768]{3,2,1,0:T(8,128)(2,1)}, u32[]{:S(2)}, u32[]{:S(2)}) %all-to-all-start.6) | async-done | bytes 1179680 | tf_op jit(solution)/shard_map/all_to_all | solution.py:147
  424.3 2.4 copy.129
  (45 shorter events, 0.4 us)
Async XLA Ops:
  7.2 50.9 %copy-start = (bf16[128,2048]{1,0:T(8,128)(2,1)S(1)}, bf16[128,2048]{1,0:T(8,128)(2,1)}, u32[]{:S(2)}) copy-start(bf16[128,2048]{1,0:T(8,128)(2,1)} %param.9) | copy-start | bytes 1572868
  7.2 112.9 %all-gather.8.cloned.1.call-start = ((), (), s32[]{:S(2)}) async-start(), calls=%async_computation.12 | async-start | bytes 3538944 | tf_op jit(solution)/shard_map/all_gather | solution.py:46
  53.8 1.8 copy-start.11
  53.8 2.2 copy-start.8
  53.8 4.0 copy-start.10
  54.9 70.0 %all-gather.6.cloned.1.call-start = ((), (), s32[]{:S(2)}) async-start(), calls=%async_computation.11 | async-start | bytes 3538944 | tf_op jit(solution)/shard_map/all_gather | solution.py:46
  60.1 4.9 %copy-start.7 = (bf16[128,2048]{1,0:T(8,128)(2,1)S(1)}, bf16[128,2048]{1,0:T(8,128)(2,1)}, u32[]{:S(2)}) copy-start(bf16[128,2048]{1,0:T(8,128)(2,1)} %param.10) | copy-start | bytes 1572868
  60.1 53.8 %all-to-all-start.2 = ((bf16[32,16,2048]{2,1,0:T(8,128)(2,1)}), bf16[32,16,2048]{2,1,0:T(8,128)(2,1)S(1)}, u32[]{:S(2)}, u32[]{:S(2)}) async-start(bf16[32,16,2048]{2,1,0:T(8,128)(2,1)} %bitcast.5), calls=%async_computation.2 | async-start | bytes 4194304 | tf_op jit(solution)/shard_map/all_to_all | solution.py:73
  64.3 111.8 %all-gather.4.cloned.1.call-start = ((), (), s32[]{:S(2)}) async-start(), calls=%async_computation.10 | async-start | bytes 3538944 | tf_op jit(solution)/shard_map/all_gather | solution.py:46
  113.9 55.7 %all-to-all-start = ((bf16[32,16,2048]{2,1,0:T(8,128)(2,1)}), bf16[32,16,2048]{2,1,0:T(8,128)(2,1)}, u32[]{:S(2)}, u32[]{:S(2)}) async-start(bf16[32,16,2048]{2,1,0:T(8,128)(2,1)} %bitcast.1), calls=%async_computation | async-start | bytes 4194304 | tf_op jit(solution)/shard_map/all_to_all | solution.py:73
  120.0 88.3 %reduce-scatter.8.cloned.1.call-start = ((), (), s32[]{:S(2)}) async-start(), calls=%async_computation.15 | async-start | bytes 3538944 | tf_op jit(solution)/shard_map/reduce_scatter | solution.py:98
  175.8 72.2 %reduce-scatter.6.cloned.1.call-start = ((), (), s32[]{:S(2)}) async-start(), calls=%async_computation.14 | async-start | bytes 3538944 | tf_op jit(solution)/shard_map/reduce_scatter | solution.py:98
  182.7 0.9 copy-start.13
  187.1 100.6 %reduce-scatter.4.cloned.1.call-start = ((), (), s32[]{:S(2)}) async-start(), calls=%async_computation.13 | async-start | bytes 3538944 | tf_op jit(solution)/shard_map/reduce_scatter | solution.py:98
  192.5 97.5 %all-to-all-start.4 = ((bf16[32,1,16]{2,1,0:T(2,128)(2,1)}), bf16[32,1,16]{2,1,0:T(2,128)(2,1)S(1)}, u32[]{:S(2)}, u32[]{:S(2)}) async-start(bf16[32,1,16]{2,1,0:T(2,128)(2,1)} %convert_element_type.104), calls=%async_computation.4 | async-start | bytes 32768 | tf_op jit(solution)/shard_map/all_to_all | solution.py:121
  290.0 41.4 %all-to-all-start.5 = ((bf16[32,3,8,768]{3,2,1,0:T(8,128)(2,1)}), bf16[32,3,8,768]{3,2,1,0:T(8,128)(2,1)S(1)}, u32[]{:S(2)}, u32[]{:S(2)}) async-start(bf16[32,3,8,768]{3,2,1,0:T(8,128)(2,1)} %pad_maximum_fusion), calls=%async_computation.8 | async-start | bytes 2359296 | tf_op jit(solution)/shard_map/all_to_all | solution.py:139
  299.8 4.1 copy-start.12
  299.8 4.1 copy-start.14
  331.4 1.0 copy-start.5
  331.4 6.4 %copy-start.9 = (s32[20]{0:T(128)S(1)}, s32[20]{0:T(128)}, u32[]{:S(2)}) copy-start(s32[20]{0:T(128)} %param.14) | copy-start | bytes 244
  332.4 54.8 %all-to-all-start.3 = ((bf16[32,16,2048]{2,1,0:T(8,128)(2,1)}), bf16[32,16,2048]{2,1,0:T(8,128)(2,1)S(1)}, u32[]{:S(2)}, u32[]{:S(2)}) async-start(bf16[32,16,2048]{2,1,0:T(8,128)(2,1)} %bitcast.92), calls=%async_computation.3 | async-start | bytes 4194304 | tf_op jit(solution)/shard_map/all_to_all | solution.py:114
  337.8 3.8 copy-start.6
  341.6 1.7 copy-start.1
  341.6 1.8 copy-start.3
  387.2 37.1 %all-to-all-start.6 = ((bf16[32,3,8,768]{3,2,1,0:T(8,128)(2,1)}), bf16[32,3,8,768]{3,2,1,0:T(8,128)(2,1)}, u32[]{:S(2)}, u32[]{:S(2)}) async-start(bf16[32,3,8,768]{3,2,1,0:T(8,128)(2,1)} %copy.96), calls=%async_computation.9 | async-start | bytes 2359296 | tf_op jit(solution)/shard_map/all_to_all | solution.py:147
  393.5 2.0 copy-start.4
  395.5 1.6 copy-start.2
Sparse Core Ops, SparseCore 0:
  55.0 24.2 all-gather.7
  81.7 30.3 all-gather.5
  114.5 30.3 all-gather.3
  175.9 32.3 reduce-scatter.7
  210.7 37.3 reduce-scatter.5
  250.5 37.1 reduce-scatter.3

commit v2 on v1

--- a/solution.py
+++ b/solution.py
@@ -94,19 +94,19 @@
     act_low = activated.astype(jnp.bfloat16)
 
     def weight_grad(rows, units):
-        grad = jnp.einsum("rd,rh->dh", rows, units, preferred_element_type=jnp.float32)
-        return lax.psum_scatter(
-            grad.astype(jnp.bfloat16), "dp", scatter_dimension=0, tiled=True
-        ).reshape(slot_count, 1, block_rows, hidden)
+        return jnp.einsum("rd,rh->dh", rows, units, preferred_element_type=jnp.float32).astype(
+            jnp.bfloat16
+        )
 
-    pieces = jnp.concatenate(
+    weight_grads = jnp.stack(
         [
             weight_grad(inputs, grad_first),
             weight_grad(inputs, grad_second),
             weight_grad(upstream, act_low),
-        ],
-        axis=1,
+        ]
     )
+    summed = lax.psum_scatter(weight_grads, "dp", scatter_dimension=1, tiled=True)
+    pieces = jnp.transpose(summed.reshape(3, slot_count, block_rows, hidden), (1, 0, 2, 3))
     input_part = (
         jnp.einsum("rh,dh->rd", grad_first, gate_w, preferred_element_type=jnp.float32)
         + jnp.einsum("rh,dh->rd", grad_second, up_w, preferred_element_type=jnp.float32)
@@ -118,6 +118,7 @@
         concat_axis=0,
         tiled=True,
     )
+    pieces, back_rows = lax.optimization_barrier((pieces, back_rows))
     back_gates = lax.all_to_all(
         gate_part.reshape(slot_count, capacity),
         "expert",

time: 437 us -> 350 us (0.80)
  waiting for transfers between devices: 269 us -> 193 us
  matrix products: 50.6 us -> 42.5 us
    reduce_scatter x3 -> x1, waiting for transfers between devices: 89.1 us -> 41.1 us  [body(): lax.psum_scatter(weight_grads, 'dp', scatter_dimension=1, tiled=True)]
    all_to_all x1, waiting for transfers between devices: 42.1 us -> 6.25 us  [body(): lax.all_to_all(input_part.reshape(slot_count, capacity, feature_width), '...]
    all_to_all x1, waiting for transfers between devices: 24.2 us -> 30.3 us  [body(): lax.all_to_all(pieces, 'expert', split_axis=0, concat_axis=0, tiled=True)]
    dot_general x3, matrix products: 14.3 us -> 8.16 us  [weight_grad(): jnp.einsum('rd,rh->dh', rows, units, preferred_element_type=jnp.float32)]
    another operation x3 -> x4, other arithmetic: 0.7 us -> 5.48 us  [the longest x1 4.78 us: body(): jnp.stack([weight_grad(inputs, grad_first), weight_grad(inputs, grad_seco...]
  transfers between devices with their start and end apart: 12 -> 10, of which waited for: 8 -> 7; matrix products, arithmetic and copies ran while one was open for 14% -> 12% of each run, Pallas kernels for 0% -> 0%
where the time goes in v2:
time: 350 us; the launch traced here: 349 us
  waiting for transfers between devices  193 us (55%)
  blocking collectives  44.2 us (13%)
  matrix products  42.5 us (12%)
  starting transfers between devices  34.6 us (10%)
  between operations  14.1 us (4%)
  local copies, waits for them, and re-layouts  13.6 us (4%)
  other arithmetic  6.89 us (2%)
    all_to_all x2, waiting for transfers between devices, dispatch(): lax.all_to_all(sent.reshape(slot_count, capacity, feature_width), 'expert...  86.5 us
    all_to_all x1, blocking collectives, body(): lax.all_to_all(outgoing, 'expert', split_axis=0, concat_axis=0, tiled=True)  44.2 us
    reduce_scatter x1, waiting for transfers between devices, body(): lax.psum_scatter(weight_grads, 'dp', scatter_dimension=1, tiled=True)  41.1 us
    all_to_all x1, waiting for transfers between devices, body(): lax.all_to_all(pieces, 'expert', split_axis=0, concat_axis=0, tiled=True)  30.3 us
    all_to_all x1, waiting for transfers between devices, body(): lax.all_to_all(leaving, 'expert', split_axis=0, concat_axis=0, tiled=True)  25.1 us
    all_to_all x2, starting transfers between devices, dispatch(): lax.all_to_all(sent.reshape(slot_count, capacity, feature_width), 'expert...  10.2 us
    dot_general x3, matrix products, weight_grad(): jnp.einsum('rd,rh->dh', rows, units, preferred_element_type=jnp.float32)  8.16 us
  transfers between devices with their start and end apart: 10, of which 7 were waited for; matrix products, arithmetic and copies ran while one was open for 12% of the time, Pallas kernels for 0%

profile of v2, /device:TPU:2, one launch (start us, length us, event | category | flops | bytes accessed | tf_op | source)
XLA Modules:
  0.0 349.3 jit_solution(2714863727915391074)
XLA Ops:
  7.2 1.7 convolution_convert_fusion.7
  8.9 0.7 copy.75
  9.6 44.2 %all_to_all.36 = bf16[32,3,8,768]{3,2,1,0:T(8,128)(2,1)S(1)} all-to-all(bf16[32,3,8,768]{3,2,1,0:T(8,128)(2,1)S(1)} %copy.75), channel_id=1, replica_groups=mesh['dp'=8,'expert'=32] {'expert'}, dimensions={0} | all-to-all | bytes 2359296 | tf_op jit(solution)/shard_map/all_to_all | solution.py:44
  53.9 1.0 slice_bitcast_fusion.2
  54.9 0.0 all-gather.6.cloned.1.call-start
  55.0 0.7 all-gather.6.cloned.1.call-update
  55.7 0.1 copy.69
  55.8 0.1 eq.117
  55.9 0.1 eq.106
  56.1 0.1 fusion.25
  56.1 0.1 reduce_window_sum.26
  56.2 0.6 reduce-window.6
  56.8 0.2 slice_reduce_fusion
  57.0 0.1 broadcast_add_fusion
  57.2 0.2 fusion.22
  57.4 0.1 and_select_fusion
  57.5 0.1 fusion.24
  57.6 0.1 select_reduce_fusion
  57.7 0.1 add.43
  57.8 0.1 copy.72
  57.9 0.2 fusion.16
  58.1 2.1 convolution_convert_fusion.4
  60.2 4.1 %all-to-all-start = ((bf16[32,16,2048]{2,1,0:T(8,128)(2,1)}), bf16[32,16,2048]{2,1,0:T(8,128)(2,1)S(1)}, u32[]{:S(2)}, u32[]{:S(2)}) async-start(bf16[32,16,2048]{2,1,0:T(8,128)(2,1)} %bitcast.1), calls=%async_computation | async-start | bytes 4194304 | tf_op jit(solution)/shard_map/all_to_all | solution.py:73
  64.3 0.0 all-gather.4.cloned.1.call-start
  64.4 0.7 all-gather.4.cloned.1.call-update
  65.1 2.1 convolution_convert_fusion.3
  67.2 46.8 %all-to-all-done = bf16[32,16,2048]{2,1,0:T(8,128)(2,1)S(1)} async-done(((bf16[32,16,2048]{2,1,0:T(8,128)(2,1)}), bf16[32,16,2048]{2,1,0:T(8,128)(2,1)S(1)}, u32[]{:S(2)}, u32[]{:S(2)}) %all-to-all-start) | async-done | bytes 2097184 | tf_op jit(solution)/shard_map/all_to_all | solution.py:73
  113.9 6.1 %all-to-all-start.1 = ((bf16[32,16,2048]{2,1,0:T(8,128)(2,1)}), bf16[32,16,2048]{2,1,0:T(8,128)(2,1)}, u32[]{:S(2)}, u32[]{:S(2)}) async-start(bf16[32,16,2048]{2,1,0:T(8,128)(2,1)} %bitcast.3), calls=%async_computation.1 | async-start | bytes 4194304 | tf_op jit(solution)/shard_map/all_to_all | solution.py:73
  120.0 0.2 reduce-scatter.2.cloned.1.call-start
  120.3 4.9 %fusion.43 = f32[512,768]{1,0:T(8,128)} fusion(bf16[512,2048]{1,0:T(8,128)(2,1)S(1)} %bitcast.90, bf16[2048,768]{1,0:T(8,128)(2,1)} %all-gather.8.cloned.1.call-done), kind=kOutput, calls=%fused_computation.84 | convolution fusion | flops 1610612736 | bytes 6815744 | tf_op jit(solution)/shard_map/dot_general | solution.py:84
  125.2 4.8 %fusion.42 = f32[512,768]{1,0:T(8,128)} fusion(bf16[512,2048]{1,0:T(8,128)(2,1)S(1)} %bitcast.91, bf16[2048,768]{1,0:T(8,128)(2,1)} %all-gather.6.cloned.1.call-done), kind=kOutput, calls=%fused_computation.83 | convolution fusion | flops 1610612736 | bytes 6815744 | tf_op jit(solution)/shard_map/dot_general | solution.py:85
  130.0 39.7 %all-to-all-done.1 = bf16[32,16,2048]{2,1,0:T(8,128)(2,1)} async-done(((bf16[32,16,2048]{2,1,0:T(8,128)(2,1)}), bf16[32,16,2048]{2,1,0:T(8,128)(2,1)}, u32[]{:S(2)}, u32[]{:S(2)}) %all-to-all-start.1) | async-done | bytes 2097184 | tf_op jit(solution)/shard_map/all_to_all | solution.py:73
  169.7 4.4 %fusion.2 = bf16[1,2048,768]{2,1,0:T(8,128)(2,1)S(1)} fusion(bf16[512,2048]{1,0:T(8,128)(2,1)} %bitcast.4, f32[512,768]{1,0:T(8,128)} %fusion.42, f32[512,768]{1,0:T(8,128)} %fusion.43), kind=kOutput, calls=%fused_computation.9 | convolution fusion | flops 1614544896 | bytes 8388608 | tf_op jit(solution)/shard_map/rd,rh->dh/dot_general | solution.py:97
  174.2 5.9 %multiply_reduce_fusion = (bf16[512]{0:T(512)(128)(2,1)S(1)}, bf16[512,768]{1,0:T(8,128)(2,1)S(1)}, bf16[512,768]{1,0:T(8,128)(2,1)S(1)}) fusion(f32[512,768]{1,0:T(8,128)} %fusion.42, f32[512,768]{1,0:T(8,128)} %fusion.43, bf16[512,2048]{1,0:T(8,128)(2,1)} %bitcast.4, bf16[2048,768]{1,0:T(8,128)(2,1)} %all-gather.4.cloned.1.call-done), kind=kOutput, calls=%fused_computation.18 | convolution fusion | flops 1617296896 | bytes 9962496 | tf_op jit(solution)/shard_map/dot_general | solution.py:86
  180.1 1.9 fusion.1
  182.0 1.9 fusion
  183.9 4.8 %pad_maximum_fusion = bf16[3,2048,768]{2,1,0:T(8,128)(2,1)} fusion(bf16[1,2048,768]{2,1,0:T(8,128)(2,1)S(1)} %fusion.2, bf16[1,2048,768]{2,1,0:T(8,128)(2,1)S(1)} %fusion.1, bf16[1,2048,768]{2,1,0:T(8,128)(2,1)S(1)} %fusion), kind=kLoop, calls=%fused_computation | loop fusion | flops 9437184 | bytes 18874368 | tf_op jit(solution)/shard_map/stack | solution.py:101
  188.7 1.9 copy-done.14
  190.6 3.1 fusion.44
  193.7 3.1 add_convert_fusion
  196.8 6.0 %all-to-all-start.3 = ((bf16[32,16,2048]{2,1,0:T(8,128)(2,1)}), bf16[32,16,2048]{2,1,0:T(8,128)(2,1)S(1)}, u32[]{:S(2)}, u32[]{:S(2)}) async-start(bf16[32,16,2048]{2,1,0:T(8,128)(2,1)} %bitcast.94), calls=%async_computation.4 | async-start | bytes 4194304 | tf_op jit(solution)/shard_map/all_to_all | solution.py:114
  202.8 41.1 %reduce-scatter.2.cloned.1.call-done = bf16[3,256,768]{2,1,0:T(8,128)(2,1)} async-done(((bf16[3,2048,768]{2,1,0:T(8,128)(2,1)}), bf16[3,256,768]{2,1,0:T(8,128)(2,1)}) %reduce-scatter.2.cloned.1.call-update) | async-done | bytes 1179664 | tf_op jit(solution)/shard_map/reduce_scatter | solution.py:108
  243.9 2.4 copy_bitcast_fusion.1
  246.3 6.2 %all-to-all-done.3 = bf16[32,16,2048]{2,1,0:T(8,128)(2,1)S(1)} async-done(((bf16[32,16,2048]{2,1,0:T(8,128)(2,1)}), bf16[32,16,2048]{2,1,0:T(8,128)(2,1)S(1)}, u32[]{:S(2)}, u32[]{:S(2)}) %all-to-all-start.3) | async-done | bytes 2097184 | tf_op jit(solution)/shard_map/all_to_all | solution.py:114
  252.5 6.0 %all-to-all-start.5 = ((bf16[32,3,8,768]{3,2,1,0:T(8,128)(2,1)}), bf16[32,3,8,768]{3,2,1,0:T(8,128)(2,1)S(1)}, u32[]{:S(2)}, u32[]{:S(2)}) async-start(bf16[32,3,8,768]{3,2,1,0:T(8,128)(2,1)} %copy_bitcast_fusion.1), calls=%async_computation.6 | async-start | bytes 2359296 | tf_op jit(solution)/shard_map/all_to_all | solution.py:140
  258.5 0.7 convert_element_type.104
  259.2 30.3 %all-to-all-done.5 = bf16[32,3,8,768]{3,2,1,0:T(8,128)(2,1)S(1)} async-done(((bf16[32,3,8,768]{3,2,1,0:T(8,128)(2,1)}), bf16[32,3,8,768]{3,2,1,0:T(8,128)(2,1)S(1)}, u32[]{:S(2)}, u32[]{:S(2)}) %all-to-all-start.5) | async-done | bytes 1179680 | tf_op jit(solution)/shard_map/all_to_all | solution.py:140
  289.6 5.0 %all-to-all-start.4 = ((bf16[32,1,16]{2,1,0:T(2,128)(2,1)}), bf16[32,1,16]{2,1,0:T(2,128)(2,1)S(1)}, u32[]{:S(2)}, u32[]{:S(2)}) async-start(bf16[32,1,16]{2,1,0:T(2,128)(2,1)} %convert_element_type.104), calls=%async_computation.5 | async-start | bytes 32768 | tf_op jit(solution)/shard_map/all_to_all | solution.py:122
  294.6 3.4 fusion.4
  298.1 1.6 convolution_convert_fusion.6
  299.7 0.1 copy-done.4
  299.8 1.7 copy.88
  301.5 2.8 all-to-all-done.4
  304.3 7.0 %all-to-all-start.6 = ((bf16[32,3,8,768]{3,2,1,0:T(8,128)(2,1)}), bf16[32,3,8,768]{3,2,1,0:T(8,128)(2,1)S(1)}, u32[]{:S(2)}, u32[]{:S(2)}) async-start(bf16[32,3,8,768]{3,2,1,0:T(8,128)(2,1)} %copy.88), calls=%async_computation.7 | async-start | bytes 2359296 | tf_op jit(solution)/shard_map/all_to_all | solution.py:148
  311.3 0.1 reduce.3
  311.3 0.1 reshape.142
  311.4 0.3 fusion.13
  311.7 0.5 fusion.38
  312.2 1.2 convolution_convert_fusion.5
  313.5 1.6 copy.91
  315.0 0.1 copy-done.3
  315.1 1.6 copy.92
  316.7 25.1 %all-to-all-done.6 = bf16[32,3,8,768]{3,2,1,0:T(8,128)(2,1)S(1)} async-done(((bf16[32,3,8,768]{3,2,1,0:T(8,128)(2,1)}), bf16[32,3,8,768]{3,2,1,0:T(8,128)(2,1)S(1)}, u32[]{:S(2)}, u32[]{:S(2)}) %all-to-all-start.6) | async-done | bytes 1179680 | tf_op jit(solution)/shard_map/all_to_all | solution.py:148
  341.7 1.1 copy.122
  (48 shorter events, 0.3 us)
Async XLA Ops:
  7.2 50.9 %copy-start = (bf16[128,2048]{1,0:T(8,128)(2,1)S(1)}, bf16[128,2048]{1,0:T(8,128)(2,1)}, u32[]{:S(2)}) copy-start(bf16[128,2048]{1,0:T(8,128)(2,1)} %param.9) | copy-start | bytes 1572868
  7.2 113.1 %all-gather.8.cloned.1.call-start = ((), (), s32[]{:S(2)}) async-start(), calls=%async_computation.10 | async-start | bytes 3538944 | tf_op jit(solution)/shard_map/all_gather | solution.py:46
  53.8 1.8 copy-start.13
  53.8 2.2 copy-start.10
  53.8 4.0 %copy-start.12 = (bf16[128,2]{0,1:T(2,128)(2,1)S(1)}, bf16[128,2]{0,1:T(2,128)(2,1)}, u32[]{:S(2)}) copy-start(bf16[128,2]{0,1:T(2,128)(2,1)} %param.12) | copy-start | bytes 1540
  54.9 70.2 %all-gather.6.cloned.1.call-start = ((), (), s32[]{:S(2)}) async-start(), calls=%async_computation.9 | async-start | bytes 3538944 | tf_op jit(solution)/shard_map/all_gather | solution.py:46
  60.2 4.9 %copy-start.9 = (bf16[128,2048]{1,0:T(8,128)(2,1)S(1)}, bf16[128,2048]{1,0:T(8,128)(2,1)}, u32[]{:S(2)}) copy-start(bf16[128,2048]{1,0:T(8,128)(2,1)} %param.10) | copy-start | bytes 1572868
  60.2 53.8 %all-to-all-start = ((bf16[32,16,2048]{2,1,0:T(8,128)(2,1)}), bf16[32,16,2048]{2,1,0:T(8,128)(2,1)S(1)}, u32[]{:S(2)}, u32[]{:S(2)}) async-start(bf16[32,16,2048]{2,1,0:T(8,128)(2,1)} %bitcast.1), calls=%async_computation | async-start | bytes 4194304 | tf_op jit(solution)/shard_map/all_to_all | solution.py:73
  64.3 109.8 %all-gather.4.cloned.1.call-start = ((), (), s32[]{:S(2)}) async-start(), calls=%async_computation.8 | async-start | bytes 3538944 | tf_op jit(solution)/shard_map/all_gather | solution.py:46
  113.9 11.2 %copy-start.6 = (bf16[32,16,2048]{2,1,0:T(8,128)(2,1)}, bf16[32,16,2048]{2,1,0:T(8,128)(2,1)S(1)}, u32[]{:S(2)}) copy-start(bf16[32,16,2048]{2,1,0:T(8,128)(2,1)S(1)} %all-to-all-done) | copy-start | bytes 6291460
  113.9 55.7 %all-to-all-start.1 = ((bf16[32,16,2048]{2,1,0:T(8,128)(2,1)}), bf16[32,16,2048]{2,1,0:T(8,128)(2,1)}, u32[]{:S(2)}, u32[]{:S(2)}) async-start(bf16[32,16,2048]{2,1,0:T(8,128)(2,1)} %bitcast.3), calls=%async_computation.1 | async-start | bytes 4194304 | tf_op jit(solution)/shard_map/all_to_all | solution.py:73
  120.0 123.9 %reduce-scatter.2.cloned.1.call-start = ((), (), s32[]{:S(2)}) async-start(), calls=%async_computation.11 | async-start | bytes 10616832 | tf_op jit(solution)/shard_map/reduce_scatter | solution.py:108
  174.1 6.0 %copy-start.7 = (bf16[32,16,2048]{2,1,0:T(8,128)(2,1)S(1)}, bf16[32,16,2048]{2,1,0:T(8,128)(2,1)}, u32[]{:S(2)}) copy-start(bf16[32,16,2048]{2,1,0:T(8,128)(2,1)} %copy-done.6) | copy-start | bytes 6291460
  180.1 1.9 copy-start.16
  180.1 1.9 copy-start.18
  188.7 1.9 copy-start.14
  190.5 3.1 copy-start.15
  190.6 3.1 copy-start.17
  196.8 55.7 %all-to-all-start.3 = ((bf16[32,16,2048]{2,1,0:T(8,128)(2,1)}), bf16[32,16,2048]{2,1,0:T(8,128)(2,1)S(1)}, u32[]{:S(2)}, u32[]{:S(2)}) async-start(bf16[32,16,2048]{2,1,0:T(8,128)(2,1)} %bitcast.94), calls=%async_computation.4 | async-start | bytes 4194304 | tf_op jit(solution)/shard_map/all_to_all | solution.py:114
  246.3 48.3 %copy-start.11 = (s32[20]{0:T(128)S(1)}, s32[20]{0:T(128)}, u32[]{:S(2)}) copy-start(s32[20]{0:T(128)} %param.14) | copy-start | bytes 244
  252.5 37.0 %all-to-all-start.5 = ((bf16[32,3,8,768]{3,2,1,0:T(8,128)(2,1)}), bf16[32,3,8,768]{3,2,1,0:T(8,128)(2,1)S(1)}, u32[]{:S(2)}, u32[]{:S(2)}) async-start(bf16[32,3,8,768]{3,2,1,0:T(8,128)(2,1)} %copy_bitcast_fusion.1), calls=%async_computation.6 | async-start | bytes 2359296 | tf_op jit(solution)/shard_map/all_to_all | solution.py:140
  289.6 14.7 %all-to-all-start.4 = ((bf16[32,1,16]{2,1,0:T(2,128)(2,1)}), bf16[32,1,16]{2,1,0:T(2,128)(2,1)S(1)}, u32[]{:S(2)}, u32[]{:S(2)}) async-start(bf16[32,1,16]{2,1,0:T(2,128)(2,1)} %convert_element_type.104), calls=%async_computation.5 | async-start | bytes 32768 | tf_op jit(solution)/shard_map/all_to_all | solution.py:122
  294.6 3.5 copy-start.8
  298.1 1.6 copy-start.2
  298.1 1.7 copy-start.4
  304.3 37.4 %all-to-all-start.6 = ((bf16[32,3,8,768]{3,2,1,0:T(8,128)(2,1)}), bf16[32,3,8,768]{3,2,1,0:T(8,128)(2,1)S(1)}, u32[]{:S(2)}, u32[]{:S(2)}) async-start(bf16[32,3,8,768]{3,2,1,0:T(8,128)(2,1)} %copy.88), calls=%async_computation.7 | async-start | bytes 2359296 | tf_op jit(solution)/shard_map/all_to_all | solution.py:148
  311.4 2.0 copy-start.5
  313.5 1.6 copy-start.3
  315.1 27.7 %copy-start.1 = (bf16[128,2048]{1,0:T(8,128)(2,1)S(1)}, bf16[128,2048]{1,0:T(8,128)(2,1)}, u32[]{:S(2)}) copy-start(bf16[128,2048]{1,0:T(8,128)(2,1)} %param.9) | copy-start | bytes 1572868
Sparse Core Ops, SparseCore 0:
  55.0 24.2 all-gather.7
  81.7 30.3 all-gather.5
  114.5 30.3 all-gather.3
  188.8 55.0 reduce-scatter.1

commit v3 on v2

--- a/solution.py
+++ b/solution.py
@@ -1,6 +1,8 @@
 import jax
 import jax.numpy as jnp
 from jax import lax
+from jax.experimental import pallas as pl
+from jax.experimental.pallas import tpu as pltpu
 from jax.sharding import PartitionSpec as P
 
 beta_one = 0.9
@@ -8,6 +10,129 @@
 learn_rate = 0.02
 adam_step = 10.0
 adam_eps = 1e-08
+
+
+lane_count = 128
+vmem_bytes = 56 * 1024 * 1024
+
+
+def whole(shape):
+    return pl.BlockSpec(shape, lambda i: (0,) * len(shape), pipeline_mode=pl.Buffered(1))
+
+
+def grad_kernel(
+    depth_steps, x_ref, y_ref, down_ref, first_ref, second_ref, dw_ref, units_ref, gate_ref
+):
+    step = pl.program_id(0)
+    hidden = first_ref.shape[1]
+    part = 256
+    rows_depth = dw_ref.shape[1]
+
+    @pl.when(step == 0)
+    def _():
+        total = jnp.zeros((first_ref.shape[0], 1), jnp.float32)
+        for start in range(0, hidden, part):
+            cols = pl.ds(start, part)
+            weighted = jnp.dot(
+                y_ref[...], down_ref[:, cols], preferred_element_type=jnp.float32
+            )
+            first_pre = first_ref[:, cols]
+            second_pre = second_ref[:, cols]
+            sigmoid_h = jax.nn.sigmoid(first_pre)
+            gated = first_pre * sigmoid_h
+            activated = gated * second_pre
+            total = total + jnp.sum(activated * weighted, axis=1, keepdims=True)
+            grad_first = weighted * second_pre * sigmoid_h * (1.0 + first_pre * (1.0 - sigmoid_h))
+            units_ref[0, :, cols] = grad_first.astype(jnp.bfloat16)
+            units_ref[1, :, cols] = (weighted * gated).astype(jnp.bfloat16)
+            units_ref[2, :, cols] = activated.astype(jnp.bfloat16)
+        gate_ref[...] = jnp.broadcast_to(total, gate_ref.shape).astype(jnp.bfloat16)
+
+    which = step // depth_steps
+
+    def product(rows):
+        dw_ref[0] = lax.dot_general(
+            rows, units_ref[which], (((0,), (0,)), ((), ())), preferred_element_type=jnp.float32
+        ).astype(jnp.bfloat16)
+
+    @pl.when(which < 2)
+    def _():
+        product(x_ref[...])
+
+    @pl.when(which == 2)
+    def _():
+        place = pl.multiple_of(lax.rem(step, depth_steps) * rows_depth, rows_depth)
+        product(y_ref[:, pl.ds(place, rows_depth)])
+
+
+def unit_and_weight_grads(inputs, upstream, down_w, first_pre, second_pre):
+    rows, width = inputs.shape
+    hidden = down_w.shape[1]
+    depth = 512
+    steps = width // depth
+    return pl.pallas_call(
+        lambda *refs: grad_kernel(steps, *refs),
+        grid=(3 * steps,),
+        in_specs=[
+            pl.BlockSpec((rows, depth), lambda i: (0, lax.rem(i, steps))),
+            whole((rows, width)),
+            whole((width, hidden)),
+            whole((rows, hidden)),
+            whole((rows, hidden)),
+        ],
+        out_specs=[
+            pl.BlockSpec((1, depth, hidden), lambda i: (i // steps, lax.rem(i, steps), 0)),
+            whole((3, rows, hidden)),
+            whole((rows, lane_count)),
+        ],
+        out_shape=[
+            jax.ShapeDtypeStruct((3, width, hidden), jnp.bfloat16),
+            jax.ShapeDtypeStruct((3, rows, hidden), jnp.bfloat16),
+            jax.ShapeDtypeStruct((rows, lane_count), jnp.bfloat16),
+        ],
+        compiler_params=pltpu.CompilerParams(vmem_limit_bytes=vmem_bytes),
+        cost_estimate=pl.CostEstimate(
+            flops=8 * rows * width * hidden, bytes_accessed=24_000_000, transcendentals=rows * hidden
+        ),
+    )(inputs, upstream, down_w, first_pre, second_pre)
+
+
+def part_kernel(units_ref, gate_w_ref, up_w_ref, gate_ref, out_ref):
+    width = gate_w_ref.shape[0]
+    over_hidden = (((1,), (1,)), ((), ()))
+    for start in range(0, width, 512):
+        cols = pl.ds(start, 512)
+        out_ref[:, cols] = (
+            lax.dot_general(
+                units_ref[0], gate_w_ref[cols], over_hidden, preferred_element_type=jnp.float32
+            )
+            + lax.dot_general(
+                units_ref[1], up_w_ref[cols], over_hidden, preferred_element_type=jnp.float32
+            )
+        ).astype(jnp.bfloat16)
+    out_ref[:, pl.ds(width, lane_count)] = gate_ref[...]
+
+
+def input_parts(units, gate_w, up_w, gate_part):
+    rows = units.shape[1]
+    width, hidden = gate_w.shape
+    block = 256
+    return pl.pallas_call(
+        part_kernel,
+        grid=(rows // block,),
+        in_specs=[
+            pl.BlockSpec((2, block, hidden), lambda i: (0, i, 0)),
+            whole((width, hidden)),
+            whole((width, hidden)),
+            pl.BlockSpec((block, lane_count), lambda i: (i, 0)),
+        ],
+        out_specs=pl.BlockSpec((block, width + lane_count), lambda i: (i, 0)),
+        out_shape=jax.ShapeDtypeStruct((rows, width + lane_count), jnp.bfloat16),
+        compiler_params=pltpu.CompilerParams(vmem_limit_bytes=vmem_bytes),
+        cost_estimate=pl.CostEstimate(
+            flops=4 * rows * width * hidden, bytes_accessed=10_000_000, transcendentals=0
+        ),
+    )(units, gate_w, up_w, gate_part)
 
 
 def adam_update(grad, stored, first, second):
@@ -83,58 +208,26 @@
 
     first_pre = jnp.dot(inputs, gate_w, preferred_element_type=jnp.float32)
     second_pre = jnp.dot(inputs, up_w, preferred_element_type=jnp.float32)
-    weighted = jnp.dot(upstream, down_w, preferred_element_type=jnp.float32)
-    sigmoid_h = jax.nn.sigmoid(first_pre)
-    activated = first_pre * sigmoid_h * second_pre
-    gate_part = jnp.sum(activated * weighted, axis=1).astype(jnp.bfloat16)
-    grad_second = (weighted * first_pre * sigmoid_h).astype(jnp.bfloat16)
-    grad_first = (weighted * second_pre * sigmoid_h * (1.0 + first_pre * (1.0 - sigmoid_h))).astype(
-        jnp.bfloat16
-    )
-    act_low = activated.astype(jnp.bfloat16)
-
-    def weight_grad(rows, units):
-        return jnp.einsum("rd,rh->dh", rows, units, preferred_element_type=jnp.float32).astype(
-            jnp.bfloat16
-        )
-
-    weight_grads = jnp.stack(
-        [
-            weight_grad(inputs, grad_first),
-            weight_grad(inputs, grad_second),
-            weight_grad(upstream, act_low),
-        ]
+    weight_grads, units, gate_part = unit_and_weight_grads(
+        inputs, upstream, down_w, first_pre, second_pre
     )
     summed = lax.psum_scatter(weight_grads, "dp", scatter_dimension=1, tiled=True)
     pieces = jnp.transpose(summed.reshape(3, slot_count, block_rows, hidden), (1, 0, 2, 3))
-    input_part = (
-        jnp.einsum("rh,dh->rd", grad_first, gate_w, preferred_element_type=jnp.float32)
-        + jnp.einsum("rh,dh->rd", grad_second, up_w, preferred_element_type=jnp.float32)
-    ).astype(jnp.bfloat16)
-    back_rows = lax.all_to_all(
-        input_part.reshape(slot_count, capacity, feature_width),
+    input_part = input_parts(units, gate_w, up_w, gate_part)
+    back = lax.all_to_all(
+        input_part.reshape(slot_count, capacity, feature_width + lane_count),
         "expert",
         split_axis=0,
         concat_axis=0,
         tiled=True,
-    )
-    pieces, back_rows = lax.optimization_barrier((pieces, back_rows))
-    back_gates = lax.all_to_all(
-        gate_part.reshape(slot_count, capacity),
-        "expert",
-        split_axis=0,
-        concat_axis=0,
-        tiled=True,
-    )
+    ).reshape(buffer_rows, feature_width + lane_count)
+    pieces, back = lax.optimization_barrier((pieces, back))
     input_grad = jnp.einsum(
-        "tb,bd->td",
-        token_dest,
-        back_rows.reshape(buffer_rows, feature_width),
-        preferred_element_type=jnp.float32,
+        "tb,bd->td", token_dest, back[:, :feature_width], preferred_element_type=jnp.float32
     ).astype(jnp.bfloat16)
     gate_sum = jnp.einsum(
-        "ab,b->a", assign_dest, back_gates.reshape(-1), preferred_element_type=jnp.float32
-    ).reshape(tok_count, top_count)
+        "ab,bl->al", assign_dest, back[:, feature_width:], preferred_element_type=jnp.float32
+    )[:, 0].reshape(tok_count, top_count)
     gate_grad = (gate_sum / gates.astype(jnp.float32)).astype(jnp.bfloat16)
 
     returned = lax.all_to_all(pieces, "expert", split_axis=0, concat_axis=0, tiled=True)

time: 350 us -> 344 us (0.983)
  blocking collectives: 44.2 us -> 82.9 us
  waiting for transfers between devices: 193 us -> 159 us
  Pallas kernels: 0 us -> 26.9 us
  matrix products: 42.5 us -> 24.4 us
  starting transfers between devices: 34.6 us -> 20.6 us
  other arithmetic: 6.89 us -> 2.99 us
    all_to_all x0 -> x1, blocking collectives: none -> 38.6 us  [body(): lax.all_to_all(pieces, 'expert', split_axis=0, concat_axis=0, tiled=True)]
    all_to_all x3 -> x1, waiting for transfers between devices: 39.4 us -> 9.59 us  [body(): lax.all_to_all(input_part.reshape(slot_count, capacity, feature_width + l...]
    pallas_call x0 -> x2, Pallas kernels: none -> 26.9 us  [the longest x1 19.1 us: unit_and_weight_grads(): pl.pallas_call(lambda *refs: grad_kernel(steps, *refs), grid=(3 * steps,)...]
    dot_general x8 -> x2, matrix products: 21.8 us -> 4.21 us  [the longest x1 3.03 us: body(): jnp.einsum('tb,bd->td', token_dest, back[:, :feature_width], preferred_el...]
    all_to_all x3 -> x1, starting transfers between devices: 17 us -> 6.12 us  [body(): lax.all_to_all(input_part.reshape(slot_count, capacity, feature_width + l...]
    all_to_all x1, waiting for transfers between devices: 25.1 us -> 20 us  [body(): lax.all_to_all(leaving, 'expert', split_axis=0, concat_axis=0, tiled=True)]
    another operation x4 -> x3, other arithmetic: 5.48 us -> 0.7 us  [the longest x1 4.78 us: body(): jnp.stack([weight_grad(inputs, grad_first), weight_grad(inputs, grad_seco...]
  transfers between devices with their start and end apart: 10 -> 8, of which waited for: 7 -> 5; matrix products, arithmetic and copies ran while one was open for 12% -> 8% of each run, Pallas kernels for 0% -> 2%
where the time goes in v3:
time: 344 us; the launch traced here: 343 us
  waiting for transfers between devices  159 us (46%)
  blocking collectives  82.9 us (24%)
  Pallas kernels  26.9 us (8%)
  matrix products  24.4 us (7%)
  starting transfers between devices  20.6 us (6%)
  between operations  14 us (4%)
  local copies, waits for them, and re-layouts  12 us (3%)
    all_to_all x2, waiting for transfers between devices, dispatch(): lax.all_to_all(sent.reshape(slot_count, capacity, feature_width), 'expert...  86.5 us
    all_to_all x1, blocking collectives, body(): lax.all_to_all(outgoing, 'expert', split_axis=0, concat_axis=0, tiled=True)  44.2 us
    reduce_scatter x1, waiting for transfers between devices, body(): lax.psum_scatter(weight_grads, 'dp', scatter_dimension=1, tiled=True)  41.3 us
    all_to_all x1, blocking collectives, body(): lax.all_to_all(pieces, 'expert', split_axis=0, concat_axis=0, tiled=True)  38.6 us
    all_to_all x1, waiting for transfers between devices, body(): lax.all_to_all(leaving, 'expert', split_axis=0, concat_axis=0, tiled=True)  20 us
    pallas_call x1, Pallas kernels, unit_and_weight_grads(): pl.pallas_call(lambda *refs: grad_kernel(steps, *refs), grid=(3 * steps,)...  19.1 us
    all_to_all x2, starting transfers between devices, dispatch(): lax.all_to_all(sent.reshape(slot_count, capacity, feature_width), 'expert...  10.2 us
    all_to_all x1, waiting for transfers between devices, body(): lax.all_to_all(input_part.reshape(slot_count, capacity, feature_width + l...  9.59 us
  transfers between devices with their start and end apart: 8, of which 5 were waited for; matrix products, arithmetic and copies ran while one was open for 8% of the time, Pallas kernels for 2%

profile of v3, /device:TPU:2, one launch (start us, length us, event | category | flops | bytes accessed | tf_op | source)
XLA Modules:
  0.0 342.6 jit_solution(1191330367473428463)
XLA Ops:
  7.2 0.0 copy-start
  7.2 0.0 all-gather.6.cloned.1.call-start
  7.2 1.7 convolution_convert_fusion.4
  8.9 0.7 copy.77
  9.6 44.2 %all_to_all.30 = bf16[32,3,8,768]{3,2,1,0:T(8,128)(2,1)S(1)} all-to-all(bf16[32,3,8,768]{3,2,1,0:T(8,128)(2,1)S(1)} %copy.77), channel_id=1, replica_groups=mesh['dp'=8,'expert'=32] {'expert'}, dimensions={0} | all-to-all | bytes 2359296 | tf_op jit(solution)/shard_map/all_to_all | solution.py:169
  53.8 1.0 slice_bitcast_fusion
  54.9 0.0 all-gather.6.cloned.1.call-update
  54.9 0.0 all-gather.8.cloned.1.call-start
  55.0 0.7 all-gather.8.cloned.1.call-update
  55.7 0.0 copy-done.11
  55.7 0.1 copy.71
  55.8 0.1 eq.101
  55.9 0.1 eq.90
  56.1 0.6 reduce-window.6
  56.7 0.2 slice_reduce_fusion
  56.9 0.1 broadcast_add_fusion
  57.0 0.0 copy-done.8
  57.0 0.1 fusion.20
  57.1 0.1 reduce_window_sum.26
  57.2 0.2 fusion.17
  57.4 0.1 and_select_fusion
  57.5 0.1 fusion.19
  57.6 0.1 select_reduce_fusion
  57.7 0.1 add.35
  57.8 0.1 copy.74
  57.9 0.0 copy-done.10
  57.9 0.2 fusion.10
  58.1 0.0 copy-start.7
  58.1 2.1 convolution_convert_fusion.1
  60.2 4.1 %all-to-all-start = ((bf16[32,16,2048]{2,1,0:T(8,128)(2,1)}), bf16[32,16,2048]{2,1,0:T(8,128)(2,1)S(1)}, u32[]{:S(2)}, u32[]{:S(2)}) async-start(bf16[32,16,2048]{2,1,0:T(8,128)(2,1)} %bitcast.1), calls=%async_computation | async-start | bytes 4194304 | tf_op jit(solution)/shard_map/all_to_all | solution.py:198
  64.4 0.0 all-gather.4.cloned.1.call-start
  64.4 0.7 all-gather.4.cloned.1.call-update
  65.1 2.0 convolution_convert_fusion
  67.1 46.8 %all-to-all-done = bf16[32,16,2048]{2,1,0:T(8,128)(2,1)S(1)} async-done(((bf16[32,16,2048]{2,1,0:T(8,128)(2,1)}), bf16[32,16,2048]{2,1,0:T(8,128)(2,1)S(1)}, u32[]{:S(2)}, u32[]{:S(2)}) %all-to-all-start) | async-done | bytes 2097184 | tf_op jit(solution)/shard_map/all_to_all | solution.py:198
  114.0 6.1 %all-to-all-start.1 = ((bf16[32,16,2048]{2,1,0:T(8,128)(2,1)}), bf16[32,16,2048]{2,1,0:T(8,128)(2,1)}, u32[]{:S(2)}, u32[]{:S(2)}) async-start(bf16[32,16,2048]{2,1,0:T(8,128)(2,1)} %bitcast.3), calls=%async_computation.1 | async-start | bytes 4194304 | tf_op jit(solution)/shard_map/all_to_all | solution.py:198
  120.1 0.2 reduce-scatter.2.cloned.1.call-start
  120.3 0.0 all-gather.6.cloned.1.call-done.gate_w_ref
  120.3 4.9 %fusion.36.refs_3_ = f32[512,768]{1,0:T(8,128)} fusion(bf16[512,2048]{1,0:T(8,128)(2,1)S(1)} %bitcast.59, bf16[2048,768]{1,0:T(8,128)(2,1)} %all-gather.6.cloned.1.call-done.gate_w_ref), kind=kOutput, calls=%fused_computation.69 | convolution fusion | flops 1610612736 | bytes 6815744 | tf_op jit(solution)/shard_map/dot_general | solution.py:209
  125.2 4.9 %fusion.37.refs_4_ = f32[512,768]{1,0:T(8,128)} fusion(bf16[512,2048]{1,0:T(8,128)(2,1)S(1)} %bitcast.60, bf16[2048,768]{1,0:T(8,128)(2,1)} %all-gather.8.cloned.1.call-done.up_w_ref), kind=kOutput, calls=%fused_computation.70 | convolution fusion | flops 1610612736 | bytes 6815744 | tf_op jit(solution)/shard_map/dot_general | solution.py:210
  130.1 39.6 %all-to-all-done.1 = bf16[32,16,2048]{2,1,0:T(8,128)(2,1)} async-done(((bf16[32,16,2048]{2,1,0:T(8,128)(2,1)}), bf16[32,16,2048]{2,1,0:T(8,128)(2,1)}, u32[]{:S(2)}, u32[]{:S(2)}) %all-to-all-start.1) | async-done | bytes 2097184 | tf_op jit(solution)/shard_map/all_to_all | solution.py:198
  169.7 19.1 %shard_map.128 = (bf16[3,2048,768]{2,1,0:T(8,128)(2,1)}, bf16[3,512,768]{2,1,0:T(8,128)(2,1)}, bf16[512,128]{1,0:T(8,128)(2,1)}) custom-call(bf16[512,2048]{1,0:T(8,128)(2,1)} %bitcast.61, bf16[512,2048]{1,0:T(8,128)(2,1)} %bitcast.4.refs_1_, bf16[2048,768]{1,0:T(8,128)(2,1)} %all-gather.4.cloned.1.call-done.refs_2_, f32[512,768]{1,0:T(8,128)} %fusion.36.refs_3_, ...), custom_call_target="tpu_custom_call" | custom-call | flops 6442450944 | bytes 24000000 | tf_op jit(solution)/shard_map/pallas_call | solution.py:73
  188.8 0.0 reduce-scatter.2.cloned.1.call-update
  188.8 7.8 %shard_map.129 = bf16[512,2176]{1,0:T(8,128)(2,1)} custom-call(bf16[3,512,768]{2,1,0:T(8,128)(2,1)} %get-tuple-element.11.units_ref, bf16[2048,768]{1,0:T(8,128)(2,1)} %all-gather.6.cloned.1.call-done.gate_w_ref, bf16[2048,768]{1,0:T(8,128)(2,1)} %all-gather.8.cloned.1.call-done.up_w_ref, bf16[512,128]{1,0:T(8,128)(2,1)} %get-tuple-element.12.gate_ref), custom_call_target="tpu_custom_call" | custom-call | flops 3221225472 | bytes 10000000 | tf_op jit(solution)/shard_map/pallas_call | solution.py:120
  196.7 6.1 %all-to-all-start.3 = ((bf16[32,16,2176]{2,1,0:T(8,128)(2,1)}), bf16[32,16,2176]{2,1,0:T(8,128)(2,1)}, u32[]{:S(2)}, u32[]{:S(2)}) async-start(bf16[32,16,2176]{2,1,0:T(8,128)(2,1)} %bitcast.58), calls=%async_computation.4 | async-start | bytes 4456448 | tf_op jit(solution)/shard_map/all_to_all | solution.py:217
  202.8 41.3 %reduce-scatter.2.cloned.1.call-done = bf16[3,256,768]{2,1,0:T(8,128)(2,1)} async-done(((bf16[3,2048,768]{2,1,0:T(8,128)(2,1)}), bf16[3,256,768]{2,1,0:T(8,128)(2,1)}) %reduce-scatter.2.cloned.1.call-update) | async-done | bytes 1179664 | tf_op jit(solution)/shard_map/reduce_scatter | solution.py:214
  244.1 1.3 copy_bitcast_fusion.1
  245.4 0.0 copy-start.9
  245.4 9.6 %all-to-all-done.3 = bf16[32,16,2176]{2,1,0:T(8,128)(2,1)} async-done(((bf16[32,16,2176]{2,1,0:T(8,128)(2,1)}), bf16[32,16,2176]{2,1,0:T(8,128)(2,1)}, u32[]{:S(2)}, u32[]{:S(2)}) %all-to-all-start.3) | async-done | bytes 2228256 | tf_op jit(solution)/shard_map/all_to_all | solution.py:217
  255.0 38.6 %all_to_all.31 = bf16[32,3,8,768]{3,2,1,0:T(8,128)(2,1)S(1)} all-to-all(bf16[32,3,8,768]{3,2,1,0:T(8,128)(2,1)S(1)} %copy_bitcast_fusion.1), channel_id=1, replica_groups=mesh['dp'=8,'expert'=32] {'expert'}, dimensions={0} | all-to-all | bytes 2359296 | tf_op jit(solution)/shard_map/all_to_all | solution.py:233
  293.7 3.0 fusion.2
  296.7 1.6 convolution_convert_fusion.3
  298.3 0.0 copy-done.1
  298.3 1.7 copy.86
  300.0 3.9 %all-to-all-start.5 = ((bf16[32,3,8,768]{3,2,1,0:T(8,128)(2,1)}), bf16[32,3,8,768]{3,2,1,0:T(8,128)(2,1)S(1)}, u32[]{:S(2)}, u32[]{:S(2)}) async-start(bf16[32,3,8,768]{3,2,1,0:T(8,128)(2,1)} %copy.86), calls=%async_computation.6 | async-start | bytes 2359296 | tf_op jit(solution)/shard_map/all_to_all | solution.py:241
  303.9 0.1 copy.79
  304.1 1.2 convolution_reduce_fusion
  305.2 0.8 reshape_squeeze.15
  306.0 1.5 divide_convert_fusion
  307.5 1.3 copy.88
  308.8 3.0 convolution_convert_fusion.2
  311.9 1.6 copy.90
  313.4 1.6 copy.91
  315.0 20.0 %all-to-all-done.5 = bf16[32,3,8,768]{3,2,1,0:T(8,128)(2,1)S(1)} async-done(((bf16[32,3,8,768]{3,2,1,0:T(8,128)(2,1)}), bf16[32,3,8,768]{3,2,1,0:T(8,128)(2,1)S(1)}, u32[]{:S(2)}, u32[]{:S(2)}) %all-to-all-start.5) | async-done | bytes 1179680 | tf_op jit(solution)/shard_map/all_to_all | solution.py:241
  335.0 1.1 copy.117
  (26 shorter events, 0.1 us)
Async XLA Ops:
  7.2 50.9 %copy-start = (bf16[128,2048]{1,0:T(8,128)(2,1)S(1)}, bf16[128,2048]{1,0:T(8,128)(2,1)}, u32[]{:S(2)}) copy-start(bf16[128,2048]{1,0:T(8,128)(2,1)} %param.9) | copy-start | bytes 1572868
  7.2 113.1 %all-gather.6.cloned.1.call-start = ((), (), s32[]{:S(2)}) async-start(), calls=%async_computation.8 | async-start | bytes 3538944 | tf_op jit(solution)/shard_map/all_gather | solution.py:171
  53.8 1.8 copy-start.11
  53.8 3.2 copy-start.8
  53.8 4.0 %copy-start.10 = (bf16[128,2]{0,1:T(2,128)(2,1)S(1)}, bf16[128,2]{0,1:T(2,128)(2,1)}, u32[]{:S(2)}) copy-start(bf16[128,2]{0,1:T(2,128)(2,1)} %param.12) | copy-start | bytes 1540
  54.9 70.3 %all-gather.8.cloned.1.call-start = ((), (), s32[]{:S(2)}) async-start(), calls=%async_computation.9 | async-start | bytes 3538944 | tf_op jit(solution)/shard_map/all_gather | solution.py:171
  58.1 2.1 copy-start.7
  60.2 4.9 %copy-start.6 = (bf16[128,2048]{1,0:T(8,128)(2,1)S(1)}, bf16[128,2048]{1,0:T(8,128)(2,1)}, u32[]{:S(2)}) copy-start(bf16[128,2048]{1,0:T(8,128)(2,1)} %param.10) | copy-start | bytes 1572868
  60.2 53.8 %all-to-all-start = ((bf16[32,16,2048]{2,1,0:T(8,128)(2,1)}), bf16[32,16,2048]{2,1,0:T(8,128)(2,1)S(1)}, u32[]{:S(2)}, u32[]{:S(2)}) async-start(bf16[32,16,2048]{2,1,0:T(8,128)(2,1)} %bitcast.1), calls=%async_computation | async-start | bytes 4194304 | tf_op jit(solution)/shard_map/all_to_all | solution.py:198
  64.4 105.4 %all-gather.4.cloned.1.call-start = ((), (), s32[]{:S(2)}) async-start(), calls=%async_computation.7 | async-start | bytes 3538944 | tf_op jit(solution)/shard_map/all_gather | solution.py:171
  114.0 11.2 %copy-start.4 = (bf16[32,16,2048]{2,1,0:T(8,128)(2,1)}, bf16[32,16,2048]{2,1,0:T(8,128)(2,1)S(1)}, u32[]{:S(2)}) copy-start(bf16[32,16,2048]{2,1,0:T(8,128)(2,1)S(1)} %all-to-all-done) | copy-start | bytes 6291460
  114.0 55.7 %all-to-all-start.1 = ((bf16[32,16,2048]{2,1,0:T(8,128)(2,1)}), bf16[32,16,2048]{2,1,0:T(8,128)(2,1)}, u32[]{:S(2)}, u32[]{:S(2)}) async-start(bf16[32,16,2048]{2,1,0:T(8,128)(2,1)} %bitcast.3), calls=%async_computation.1 | async-start | bytes 4194304 | tf_op jit(solution)/shard_map/all_to_all | solution.py:198
  120.1 124.0 %reduce-scatter.2.cloned.1.call-start = ((), (), s32[]{:S(2)}) async-start(), calls=%async_computation.10 | async-start | bytes 10616832 | tf_op jit(solution)/shard_map/reduce_scatter | solution.py:214
  196.7 58.4 %all-to-all-start.3 = ((bf16[32,16,2176]{2,1,0:T(8,128)(2,1)}), bf16[32,16,2176]{2,1,0:T(8,128)(2,1)}, u32[]{:S(2)}, u32[]{:S(2)}) async-start(bf16[32,16,2176]{2,1,0:T(8,128)(2,1)} %bitcast.58), calls=%async_computation.4 | async-start | bytes 4456448 | tf_op jit(solution)/shard_map/all_to_all | solution.py:217
  245.4 48.3 %copy-start.9 = (s32[20]{0:T(128)S(1)}, s32[20]{0:T(128)}, u32[]{:S(2)}) copy-start(s32[20]{0:T(128)} %param.14) | copy-start | bytes 244
  255.0 38.7 %copy-start.3 = (f32[3,20,8,768]{3,2,1,0:T(8,128)S(1)}, f32[3,20,8,768]{3,2,1,0:T(8,128)}, u32[]{:S(2)}) copy-start(f32[3,20,8,768]{3,2,1,0:T(8,128)} %param.16) | copy-start | bytes 4423684
  293.7 3.0 copy-start.5
  296.7 1.6 copy-start.1
  300.0 35.0 %all-to-all-start.5 = ((bf16[32,3,8,768]{3,2,1,0:T(8,128)(2,1)}), bf16[32,3,8,768]{3,2,1,0:T(8,128)(2,1)S(1)}, u32[]{:S(2)}, u32[]{:S(2)}) async-start(bf16[32,3,8,768]{3,2,1,0:T(8,128)(2,1)} %copy.86), calls=%async_computation.6 | async-start | bytes 2359296 | tf_op jit(solution)/shard_map/all_to_all | solution.py:241
  308.8 3.0 copy-start.2
Sparse Core Ops, SparseCore 0:
  55.0 24.2 all-gather.5
  81.7 30.3 all-gather.7
  114.5 30.3 all-gather.3
  189.0 55.0 reduce-scatter.1

commit v4 on v3

--- a/solution.py
+++ b/solution.py
@@ -13,7 +13,7 @@
 
 
 lane_count = 128
-vmem_bytes = 56 * 1024 * 1024
+vmem_bytes = 40 * 1024 * 1024
 
 
 def whole(shape):
@@ -21,48 +21,65 @@
 
 
 def grad_kernel(
-    depth_steps, x_ref, y_ref, down_ref, first_ref, second_ref, dw_ref, units_ref, gate_ref
+    u_steps,
+    x_ref,
+    y_ref,
+    down_ref,
+    first_hbm,
+    second_hbm,
+    dw_ref,
+    units_ref,
+    gate_ref,
+    u_ref,
+    first_ref,
+    second_ref,
+    sems,
 ):
     step = pl.program_id(0)
-    hidden = first_ref.shape[1]
-    part = 256
-    rows_depth = dw_ref.shape[1]
+    rows, hidden = u_ref.shape
+    part = 128
+    fetch_first = pltpu.make_async_copy(first_hbm, first_ref, sems.at[0])
+    fetch_second = pltpu.make_async_copy(second_hbm, second_ref, sems.at[1])
 
     @pl.when(step == 0)
     def _():
-        total = jnp.zeros((first_ref.shape[0], 1), jnp.float32)
-        for start in range(0, hidden, part):
-            cols = pl.ds(start, part)
-            weighted = jnp.dot(
-                y_ref[...], down_ref[:, cols], preferred_element_type=jnp.float32
-            )
-            first_pre = first_ref[:, cols]
-            second_pre = second_ref[:, cols]
+        fetch_first.start()
+        fetch_second.start()
+        u_ref[...] = jnp.dot(y_ref[...], down_ref[...], preferred_element_type=jnp.float32)
+
+    @pl.when((step > 0) & (step < u_steps))
+    def _():
+        u_ref[...] += jnp.dot(y_ref[...], down_ref[...], preferred_element_type=jnp.float32)
+
+    @pl.when(step == u_steps - 1)
+    def _():
+        fetch_first.wait()
+        fetch_second.wait()
+        for start in range(0, rows, part):
+            span = pl.ds(start, part)
+            weighted = u_ref[span]
+            first_pre = first_ref[span]
+            second_pre = second_ref[span]
             sigmoid_h = jax.nn.sigmoid(first_pre)
             gated = first_pre * sigmoid_h
             activated = gated * second_pre
-            total = total + jnp.sum(activated * weighted, axis=1, keepdims=True)
+            total = jnp.sum(activated * weighted, axis=1, keepdims=True)
             grad_first = weighted * second_pre * sigmoid_h * (1.0 + first_pre * (1.0 - sigmoid_h))
-            units_ref[0, :, cols] = grad_first.astype(jnp.bfloat16)
-            units_ref[1, :, cols] = (weighted * gated).astype(jnp.bfloat16)
-            units_ref[2, :, cols] = activated.astype(jnp.bfloat16)
-        gate_ref[...] = jnp.broadcast_to(total, gate_ref.shape).astype(jnp.bfloat16)
-
-    which = step // depth_steps
-
-    def product(rows):
-        dw_ref[0] = lax.dot_general(
-            rows, units_ref[which], (((0,), (0,)), ((), ())), preferred_element_type=jnp.float32
+            units_ref[span, :hidden] = grad_first.astype(jnp.bfloat16)
+            units_ref[span, hidden : 2 * hidden] = (weighted * gated).astype(jnp.bfloat16)
+            units_ref[span, 2 * hidden :] = activated.astype(jnp.bfloat16)
+            gate_ref[span] = jnp.broadcast_to(total, (part, lane_count)).astype(jnp.bfloat16)
+
+    @pl.when(step >= u_steps)
+    def _():
+        both = jnp.dot(
+            x_ref[...].T, units_ref[:, : 2 * hidden], preferred_element_type=jnp.float32
         ).astype(jnp.bfloat16)
-
-    @pl.when(which < 2)
-    def _():
-        product(x_ref[...])
-
-    @pl.when(which == 2)
-    def _():
-        place = pl.multiple_of(lax.rem(step, depth_steps) * rows_depth, rows_depth)
-        product(y_ref[:, pl.ds(place, rows_depth)])
+        dw_ref[0] = both[:, :hidden]
+        dw_ref[1] = both[:, hidden:]
+        dw_ref[2] = jnp.dot(
+            y_ref[...].T, units_ref[:, 2 * hidden :], preferred_element_type=jnp.float32
+        ).astype(jnp.bfloat16)
 
 
 def unit_and_weight_grads(inputs, upstream, down_w, first_pre, second_pre):
@@ -72,23 +89,29 @@
     steps = width // depth
     return pl.pallas_call(
         lambda *refs: grad_kernel(steps, *refs),
-        grid=(3 * steps,),
+        grid=(2 * steps,),
         in_specs=[
+            pl.BlockSpec((rows, depth), lambda i: (0, jnp.maximum(i - steps, 0))),
             pl.BlockSpec((rows, depth), lambda i: (0, lax.rem(i, steps))),
-            whole((rows, width)),
-            whole((width, hidden)),
-            whole((rows, hidden)),
-            whole((rows, hidden)),
+            pl.BlockSpec((depth, hidden), lambda i: (jnp.minimum(i, steps - 1), 0)),
+            pl.BlockSpec(memory_space=pl.ANY),
+            pl.BlockSpec(memory_space=pl.ANY),
         ],
         out_specs=[
-            pl.BlockSpec((1, depth, hidden), lambda i: (i // steps, lax.rem(i, steps), 0)),
-            whole((3, rows, hidden)),
+            pl.BlockSpec((3, depth, hidden), lambda i: (0, jnp.maximum(i - steps, 0), 0)),
+            whole((rows, 3 * hidden)),
             whole((rows, lane_count)),
         ],
         out_shape=[
             jax.ShapeDtypeStruct((3, width, hidden), jnp.bfloat16),
-            jax.ShapeDtypeStruct((3, rows, hidden), jnp.bfloat16),
+            jax.ShapeDtypeStruct((rows, 3 * hidden), jnp.bfloat16),
             jax.ShapeDtypeStruct((rows, lane_count), jnp.bfloat16),
+        ],
+        scratch_shapes=[
+            pltpu.VMEM((rows, hidden), jnp.float32),
+            pltpu.VMEM((rows, hidden), jnp.float32),
+            pltpu.VMEM((rows, hidden), jnp.float32),
+            pltpu.SemaphoreType.DMA((2,)),
         ],
         compiler_params=pltpu.CompilerParams(vmem_limit_bytes=vmem_bytes),
         cost_estimate=pl.CostEstimate(
@@ -98,35 +121,41 @@
 
 
 def part_kernel(units_ref, gate_w_ref, up_w_ref, gate_ref, out_ref):
-    width = gate_w_ref.shape[0]
+    step = pl.program_id(0)
+    depth, hidden = gate_w_ref.shape
     over_hidden = (((1,), (1,)), ((), ()))
-    for start in range(0, width, 512):
-        cols = pl.ds(start, 512)
-        out_ref[:, cols] = (
-            lax.dot_general(
-                units_ref[0], gate_w_ref[cols], over_hidden, preferred_element_type=jnp.float32
-            )
-            + lax.dot_general(
-                units_ref[1], up_w_ref[cols], over_hidden, preferred_element_type=jnp.float32
-            )
-        ).astype(jnp.bfloat16)
-    out_ref[:, pl.ds(width, lane_count)] = gate_ref[...]
+
+    @pl.when(step == 0)
+    def _():
+        out_ref[:, pl.ds(out_ref.shape[1] - lane_count, lane_count)] = gate_ref[...]
+
+    out_ref[:, pl.ds(pl.multiple_of(step * depth, depth), depth)] = (
+        lax.dot_general(
+            units_ref[:, :hidden], gate_w_ref[...], over_hidden, preferred_element_type=jnp.float32
+        )
+        + lax.dot_general(
+            units_ref[:, hidden : 2 * hidden],
+            up_w_ref[...],
+            over_hidden,
+            preferred_element_type=jnp.float32,
+        )
+    ).astype(jnp.bfloat16)
 
 
 def input_parts(units, gate_w, up_w, gate_part):
-    rows = units.shape[1]
+    rows = units.shape[0]
     width, hidden = gate_w.shape
-    block = 256
+    depth = 512
     return pl.pallas_call(
         part_kernel,
-        grid=(rows // block,),
+        grid=(width // depth,),
         in_specs=[
-            pl.BlockSpec((2, block, hidden), lambda i: (0, i, 0)),
-            whole((width, hidden)),
-            whole((width, hidden)),
-            pl.BlockSpec((block, lane_count), lambda i: (i, 0)),
-        ],
-        out_specs=pl.BlockSpec((block, width + lane_count), lambda i: (i, 0)),
+            whole((rows, 3 * hidden)),
+            pl.BlockSpec((depth, hidden), lambda i: (i, 0)),
+            pl.BlockSpec((depth, hidden), lambda i: (i, 0)),
+            whole((rows, lane_count)),
+        ],
+        out_specs=whole((rows, width + lane_count)),
         out_shape=jax.ShapeDtypeStruct((rows, width + lane_count), jnp.bfloat16),
         compiler_params=pltpu.CompilerParams(vmem_limit_bytes=vmem_bytes),
         cost_estimate=pl.CostEstimate(
@@ -167,12 +196,6 @@
         "se,cerh->scrh", slot_state, weights, preferred_element_type=jnp.float32
     ).astype(jnp.bfloat16)
     arrived = lax.all_to_all(outgoing, "expert", split_axis=0, concat_axis=0, tiled=True)
-    gate_w, up_w, down_w = [
-        lax.all_gather(
-            arrived[:, c].reshape(slot_count * block_rows, hidden), "dp", axis=0, tiled=True
-        )
-        for c in range(3)
-    ]
 
     replica_count = jnp.sum(place_hot, axis=0)
     earlier = jnp.cumsum(place_hot, axis=0) - place_hot
@@ -191,20 +214,29 @@
     token_dest = jnp.sum(split_dest, axis=1)
     gated_dest = jnp.sum(split_dest * gates[:, :, None], axis=1)
 
-    def dispatch(where, rows):
-        sent = jnp.einsum(
-            "tb,td->bd", where, rows, preferred_element_type=jnp.float32
-        ).astype(jnp.bfloat16)
-        return lax.all_to_all(
-            sent.reshape(slot_count, capacity, feature_width),
-            "expert",
-            split_axis=0,
-            concat_axis=0,
-            tiled=True,
-        ).reshape(buffer_rows, feature_width)
-
-    inputs = dispatch(token_dest, tokens)
-    upstream = dispatch(gated_dest, cotangent)
+    def pack(where, rows):
+        return (
+            jnp.einsum("tb,td->bd", where, rows, preferred_element_type=jnp.float32)
+            .astype(jnp.bfloat16)
+            .reshape(slot_count, capacity, feature_width)
+        )
+
+    def dispatch(packed):
+        return lax.all_to_all(packed, "expert", split_axis=0, concat_axis=0, tiled=True).reshape(
+            buffer_rows, feature_width
+        )
+
+    arrived, packed_tokens, packed_upstream = lax.optimization_barrier(
+        (arrived, pack(token_dest, tokens), pack(gated_dest, cotangent))
+    )
+    gate_w, up_w, down_w = [
+        lax.all_gather(
+            arrived[:, c].reshape(slot_count * block_rows, hidden), "dp", axis=0, tiled=True
+        )
+        for c in range(3)
+    ]
+    inputs = dispatch(packed_tokens)
+    upstream = dispatch(packed_upstream)
 
     first_pre = jnp.dot(inputs, gate_w, preferred_element_type=jnp.float32)
     second_pre = jnp.dot(inputs, up_w, preferred_element_type=jnp.float32)

time: 344 us -> 343 us (level)
  blocking collectives: 82.9 us -> 38.6 us
  waiting for transfers between devices: 159 us -> 186 us
  starting transfers between devices: 20.6 us -> 33.4 us
  local copies, waits for them, and re-layouts: 12 us -> 24.5 us
  Pallas kernels: 26.9 us -> 18.2 us
    all_to_all x1 -> x0, blocking collectives: 44.2 us -> none  [body(): lax.all_to_all(outgoing, 'expert', split_axis=0, concat_axis=0, tiled=True)]
    all_to_all x2 -> x3, waiting for transfers between devices: 86.5 us -> 113 us  [the longest x2 88.8 us: dispatch(): lax.all_to_all(packed, 'expert', split_axis=0, concat_axis=0, tiled=True)]
    all_to_all x2 -> x3, starting transfers between devices: 10.2 us -> 22.9 us  [the longest x1 11.6 us: body(): lax.all_to_all(outgoing, 'expert', split_axis=0, concat_axis=0, tiled=True)]
    unnamed x30 -> x42, local copies, waits for them, and re-layouts: 4.64 us -> 16.2 us
    pallas_call x2, Pallas kernels: 26.9 us -> 18.2 us  [the longest x1 12.6 us: unit_and_weight_grads(): pl.pallas_call(lambda *refs: grad_kernel(steps, *refs), grid=(2 * steps,)...]
  transfers between devices with their start and end apart: 8 -> 9, of which waited for: 5 -> 6; matrix products, arithmetic and copies ran while one was open for 8% -> 8% of each run, Pallas kernels for 2% -> 2%
where the time goes in v4:
time: 343 us; the launch traced here: 342 us
  waiting for transfers between devices  186 us (54%)
  blocking collectives  38.6 us (11%)
  starting transfers between devices  33.4 us (10%)
  local copies, waits for them, and re-layouts  24.5 us (7%)
  matrix products  24.5 us (7%)
  Pallas kernels  18.2 us (5%)
  between operations  14 us (4%)
    all_to_all x2, waiting for transfers between devices, dispatch(): lax.all_to_all(packed, 'expert', split_axis=0, concat_axis=0, tiled=True)  88.8 us
    all_to_all x1, blocking collectives, body(): lax.all_to_all(pieces, 'expert', split_axis=0, concat_axis=0, tiled=True)  38.6 us
    reduce_scatter x1, waiting for transfers between devices, body(): lax.psum_scatter(weight_grads, 'dp', scatter_dimension=1, tiled=True)  37.9 us
    all_to_all x1, waiting for transfers between devices, body(): lax.all_to_all(outgoing, 'expert', split_axis=0, concat_axis=0, tiled=True)  24.6 us
    all_to_all x1, waiting for transfers between devices, body(): lax.all_to_all(leaving, 'expert', split_axis=0, concat_axis=0, tiled=True)  20 us
    unnamed x42, local copies, waits for them, and re-layouts  16.2 us
    all_to_all x1, waiting for transfers between devices, body(): lax.all_to_all(input_part.reshape(slot_count, capacity, feature_width + l...  13 us
    pallas_call x1, Pallas kernels, unit_and_weight_grads(): pl.pallas_call(lambda *refs: grad_kernel(steps, *refs), grid=(2 * steps,)...  12.6 us
  transfers between devices with their start and end apart: 9, of which 6 were waited for; matrix products, arithmetic and copies ran while one was open for 8% of the time, Pallas kernels for 2%

profile of v4, /device:TPU:2, one launch (start us, length us, event | category | flops | bytes accessed | tf_op | source)
XLA Modules:
  0.0 341.9 jit_solution(12431254886203248564)
XLA Ops:
  7.2 1.7 convolution_convert_fusion.4
  8.9 1.7 copy.77
  10.6 11.6 %all-to-all-start = ((bf16[32,3,8,768]{3,2,1,0:T(8,128)(2,1)}), bf16[32,3,8,768]{3,2,1,0:T(8,128)(2,1)S(1)}, u32[]{:S(2)}, u32[]{:S(2)}) async-start(bf16[32,3,8,768]{3,2,1,0:T(8,128)(2,1)} %copy.77), calls=%async_computation | async-start | bytes 2359296 | tf_op jit(solution)/shard_map/all_to_all | solution.py:198
  22.2 0.0 all-gather.8.cloned.1.call-start
  22.3 0.1 copy.71
  22.4 0.1 eq.101
  22.5 0.1 eq.90
  22.7 0.6 reduce-window.6
  23.3 0.2 slice_reduce_fusion
  23.5 0.1 broadcast_add_fusion
  23.7 0.1 fusion.20
  23.7 0.1 reduce_window_sum.26
  23.8 0.2 fusion.17
  24.0 0.1 and_select_fusion
  24.1 0.1 fusion.19
  24.2 0.1 select_reduce_fusion
  24.3 0.1 add.35
  24.4 0.1 copy.74
  24.5 0.2 fusion.10
  24.7 2.1 convolution_convert_fusion.1
  26.8 2.1 convolution_convert_fusion
  28.9 24.6 %all-to-all-done = bf16[32,3,8,768]{3,2,1,0:T(8,128)(2,1)S(1)} async-done(((bf16[32,3,8,768]{3,2,1,0:T(8,128)(2,1)}), bf16[32,3,8,768]{3,2,1,0:T(8,128)(2,1)S(1)}, u32[]{:S(2)}, u32[]{:S(2)}) %all-to-all-start) | async-done | bytes 1179680 | tf_op jit(solution)/shard_map/all_to_all | solution.py:198
  53.6 1.0 slice_bitcast_fusion
  54.6 0.0 all-gather.8.cloned.1.call-update
  54.6 0.0 all-gather.6.cloned.1.call-start
  54.7 0.7 all-gather.6.cloned.1.call-update
  55.4 5.2 %all-to-all-start.1 = ((bf16[32,16,2048]{2,1,0:T(8,128)(2,1)}), bf16[32,16,2048]{2,1,0:T(8,128)(2,1)S(1)}, u32[]{:S(2)}, u32[]{:S(2)}) async-start(bf16[32,16,2048]{2,1,0:T(8,128)(2,1)} %bitcast.62), calls=%async_computation.1 | async-start | bytes 4194304 | tf_op jit(solution)/shard_map/all_to_all | solution.py:225
  60.6 0.0 all-gather.4.cloned.1.call-start
  60.6 0.7 all-gather.4.cloned.1.call-update
  61.3 48.9 %all-to-all-done.1 = bf16[32,16,2048]{2,1,0:T(8,128)(2,1)S(1)} async-done(((bf16[32,16,2048]{2,1,0:T(8,128)(2,1)}), bf16[32,16,2048]{2,1,0:T(8,128)(2,1)S(1)}, u32[]{:S(2)}, u32[]{:S(2)}) %all-to-all-start.1) | async-done | bytes 2097184 | tf_op jit(solution)/shard_map/all_to_all | solution.py:225
  110.2 6.1 %all-to-all-start.2 = ((bf16[32,16,2048]{2,1,0:T(8,128)(2,1)}), bf16[32,16,2048]{2,1,0:T(8,128)(2,1)}, u32[]{:S(2)}, u32[]{:S(2)}) async-start(bf16[32,16,2048]{2,1,0:T(8,128)(2,1)} %bitcast.61), calls=%async_computation.2 | async-start | bytes 4194304 | tf_op jit(solution)/shard_map/all_to_all | solution.py:225
  116.4 0.0 reduce-scatter.2.cloned.1.call-start
  116.4 0.0 all-gather.8.cloned.1.call-done.up_w_ref
  116.4 4.8 %fusion.37.refs_4_ = f32[512,768]{1,0:T(8,128)} fusion(bf16[512,2048]{1,0:T(8,128)(2,1)S(1)} %bitcast.58, bf16[2048,768]{1,0:T(8,128)(2,1)} %all-gather.8.cloned.1.call-done.up_w_ref), kind=kOutput, calls=%fused_computation.70 | convolution fusion | flops 1610612736 | bytes 6815744 | tf_op jit(solution)/shard_map/dot_general | solution.py:242
  121.3 4.9 %fusion.36.refs_3_ = f32[512,768]{1,0:T(8,128)} fusion(bf16[512,2048]{1,0:T(8,128)(2,1)S(1)} %bitcast.59, bf16[2048,768]{1,0:T(8,128)(2,1)} %all-gather.6.cloned.1.call-done.gate_w_ref), kind=kOutput, calls=%fused_computation.69 | convolution fusion | flops 1610612736 | bytes 6815744 | tf_op jit(solution)/shard_map/dot_general | solution.py:241
  126.2 39.8 %all-to-all-done.2 = bf16[32,16,2048]{2,1,0:T(8,128)(2,1)} async-done(((bf16[32,16,2048]{2,1,0:T(8,128)(2,1)}), bf16[32,16,2048]{2,1,0:T(8,128)(2,1)}, u32[]{:S(2)}, u32[]{:S(2)}) %all-to-all-start.2) | async-done | bytes 2097184 | tf_op jit(solution)/shard_map/all_to_all | solution.py:225
  166.0 1.9 copy-done.3
  167.9 1.4 copy-done.6
  169.3 1.4 copy-done.7
  170.7 12.6 %shard_map.128 = (bf16[3,2048,768]{2,1,0:T(8,128)(2,1)}, bf16[512,2304]{1,0:T(8,128)(2,1)S(1)}, bf16[512,128]{1,0:T(8,128)(2,1)S(1)}) custom-call(bf16[512,2048]{1,0:T(8,128)(2,1)S(1)} %bitcast.60, bf16[512,2048]{1,0:T(8,128)(2,1)} %bitcast.5.refs_1_, bf16[2048,768]{1,0:T(8,128)(2,1)S(1)} %copy-done.3, f32[512,768]{1,0:T(8,128)S(1)} %copy-done.7, ...), custom_call_target="tpu_custom_call" | custom-call | flops 6442450944 | bytes 24000000 | tf_op jit(solution)/shard_map/pallas_call | solution.py:90
  183.4 1.4 copy-done.4
  184.8 1.6 copy-done.5
  186.4 1.9 copy-done.1
  188.3 1.9 copy-done.2
  190.2 5.6 %shard_map.129 = bf16[512,2176]{1,0:T(8,128)(2,1)} custom-call(bf16[512,2304]{1,0:T(8,128)(2,1)S(1)} %copy-done.5, bf16[2048,768]{1,0:T(8,128)(2,1)S(1)} %copy-done.2, bf16[2048,768]{1,0:T(8,128)(2,1)S(1)} %copy-done.1, bf16[512,128]{1,0:T(8,128)(2,1)S(1)} %get-tuple-element.18.gate_ref), custom_call_target="tpu_custom_call" | custom-call | flops 3221225472 | bytes 10000000 | tf_op jit(solution)/shard_map/pallas_call | solution.py:149
  195.8 6.3 %all-to-all-start.3 = ((bf16[32,16,2176]{2,1,0:T(8,128)(2,1)}), bf16[32,16,2176]{2,1,0:T(8,128)(2,1)}, u32[]{:S(2)}, u32[]{:S(2)}) async-start(bf16[32,16,2176]{2,1,0:T(8,128)(2,1)} %bitcast.11), calls=%async_computation.4 | async-start | bytes 4456448 | tf_op jit(solution)/shard_map/all_to_all | solution.py:249
  202.1 37.9 %reduce-scatter.2.cloned.1.call-done = bf16[3,256,768]{2,1,0:T(8,128)(2,1)} async-done(((bf16[3,2048,768]{2,1,0:T(8,128)(2,1)}), bf16[3,256,768]{2,1,0:T(8,128)(2,1)}) %reduce-scatter.2.cloned.1.call-update) | async-done | bytes 1179664 | tf_op jit(solution)/shard_map/reduce_scatter | solution.py:246
  240.0 1.3 copy_bitcast_fusion.1
  241.3 13.0 %all-to-all-done.3 = bf16[32,16,2176]{2,1,0:T(8,128)(2,1)} async-done(((bf16[32,16,2176]{2,1,0:T(8,128)(2,1)}), bf16[32,16,2176]{2,1,0:T(8,128)(2,1)}, u32[]{:S(2)}, u32[]{:S(2)}) %all-to-all-start.3) | async-done | bytes 2228256 | tf_op jit(solution)/shard_map/all_to_all | solution.py:249
  254.3 38.6 %all_to_all.30 = bf16[32,3,8,768]{3,2,1,0:T(8,128)(2,1)S(1)} all-to-all(bf16[32,3,8,768]{3,2,1,0:T(8,128)(2,1)S(1)} %copy_bitcast_fusion.1), channel_id=1, replica_groups=mesh['dp'=8,'expert'=32] {'expert'}, dimensions={0} | all-to-all | bytes 2359296 | tf_op jit(solution)/shard_map/all_to_all | solution.py:265
  293.0 3.0 fusion.2
  296.0 1.6 convolution_convert_fusion.3
  297.6 1.7 copy.86
  299.3 3.9 %all-to-all-start.5 = ((bf16[32,3,8,768]{3,2,1,0:T(8,128)(2,1)}), bf16[32,3,8,768]{3,2,1,0:T(8,128)(2,1)S(1)}, u32[]{:S(2)}, u32[]{:S(2)}) async-start(bf16[32,3,8,768]{3,2,1,0:T(8,128)(2,1)} %copy.86), calls=%async_computation.6 | async-start | bytes 2359296 | tf_op jit(solution)/shard_map/all_to_all | solution.py:273
  303.2 0.1 copy.79
  303.4 1.2 convolution_reduce_fusion
  304.5 0.8 reshape_squeeze.15
  305.3 1.5 divide_convert_fusion
  306.8 1.3 copy.88
  308.1 3.0 convolution_convert_fusion.2
  311.2 1.6 copy.90
  312.7 1.6 copy.91
  314.3 20.0 %all-to-all-done.5 = bf16[32,3,8,768]{3,2,1,0:T(8,128)(2,1)S(1)} async-done(((bf16[32,3,8,768]{3,2,1,0:T(8,128)(2,1)}), bf16[32,3,8,768]{3,2,1,0:T(8,128)(2,1)S(1)}, u32[]{:S(2)}, u32[]{:S(2)}) %all-to-all-start.5) | async-done | bytes 1179680 | tf_op jit(solution)/shard_map/all_to_all | solution.py:273
  334.3 1.1 copy.117
  (39 shorter events, 0.2 us)
Async XLA Ops:
  7.2 17.6 %copy-start = (bf16[128,2048]{1,0:T(8,128)(2,1)S(1)}, bf16[128,2048]{1,0:T(8,128)(2,1)}, u32[]{:S(2)}) copy-start(bf16[128,2048]{1,0:T(8,128)(2,1)} %param.9) | copy-start | bytes 1572868
  10.6 11.7 %copy-start.17 = (s32[128,2]{0,1:T(2,128)S(1)}, s32[128,2]{0,1:T(2,128)}, u32[]{:S(2)}) copy-start(s32[128,2]{0,1:T(2,128)} %param.11) | copy-start | bytes 3076
  10.6 13.1 %copy-start.14 = (s32[32]{0:T(128)S(1)}, s32[32]{0:T(128)}, u32[]{:S(2)}) copy-start(s32[32]{0:T(128)} %param.13) | copy-start | bytes 388
  10.6 13.9 %copy-start.16 = (bf16[128,2]{0,1:T(2,128)(2,1)S(1)}, bf16[128,2]{0,1:T(2,128)(2,1)}, u32[]{:S(2)}) copy-start(bf16[128,2]{0,1:T(2,128)(2,1)} %param.12) | copy-start | bytes 1540
  10.6 43.0 %all-to-all-start = ((bf16[32,3,8,768]{3,2,1,0:T(8,128)(2,1)}), bf16[32,3,8,768]{3,2,1,0:T(8,128)(2,1)S(1)}, u32[]{:S(2)}, u32[]{:S(2)}) async-start(bf16[32,3,8,768]{3,2,1,0:T(8,128)(2,1)} %copy.77), calls=%async_computation | async-start | bytes 2359296 | tf_op jit(solution)/shard_map/all_to_all | solution.py:198
  22.2 94.2 %all-gather.8.cloned.1.call-start = ((), (), s32[]{:S(2)}) async-start(), calls=%async_computation.9 | async-start | bytes 3538944 | tf_op jit(solution)/shard_map/all_gather | solution.py:233
  22.7 4.1 %copy-start.12 = (bf16[128,2048]{1,0:T(8,128)(2,1)S(1)}, bf16[128,2048]{1,0:T(8,128)(2,1)}, u32[]{:S(2)}) copy-start(bf16[128,2048]{1,0:T(8,128)(2,1)} %param.10) | copy-start | bytes 1572868
  24.7 2.1 copy-start.13
  54.6 66.7 %all-gather.6.cloned.1.call-start = ((), (), s32[]{:S(2)}) async-start(), calls=%async_computation.8 | async-start | bytes 3538944 | tf_op jit(solution)/shard_map/all_gather | solution.py:233
  55.4 54.9 %all-to-all-start.1 = ((bf16[32,16,2048]{2,1,0:T(8,128)(2,1)}), bf16[32,16,2048]{2,1,0:T(8,128)(2,1)S(1)}, u32[]{:S(2)}, u32[]{:S(2)}) async-start(bf16[32,16,2048]{2,1,0:T(8,128)(2,1)} %bitcast.62), calls=%async_computation.1 | async-start | bytes 4194304 | tf_op jit(solution)/shard_map/all_to_all | solution.py:225
  60.6 105.5 %all-gather.4.cloned.1.call-start = ((), (), s32[]{:S(2)}) async-start(), calls=%async_computation.7 | async-start | bytes 3538944 | tf_op jit(solution)/shard_map/all_gather | solution.py:233
  110.2 55.8 %all-to-all-start.2 = ((bf16[32,16,2048]{2,1,0:T(8,128)(2,1)}), bf16[32,16,2048]{2,1,0:T(8,128)(2,1)}, u32[]{:S(2)}, u32[]{:S(2)}) async-start(bf16[32,16,2048]{2,1,0:T(8,128)(2,1)} %bitcast.61), calls=%async_computation.2 | async-start | bytes 4194304 | tf_op jit(solution)/shard_map/all_to_all | solution.py:225
  116.4 123.6 %reduce-scatter.2.cloned.1.call-start = ((), (), s32[]{:S(2)}) async-start(), calls=%async_computation.10 | async-start | bytes 10616832 | tf_op jit(solution)/shard_map/reduce_scatter | solution.py:246
  166.0 1.9 copy-start.3
  167.9 1.4 copy-start.6
  169.3 1.4 copy-start.7
  183.3 1.4 copy-start.4
  184.7 1.7 copy-start.5
  186.4 1.9 copy-start.1
  188.3 1.9 copy-start.2
  195.8 58.5 %all-to-all-start.3 = ((bf16[32,16,2176]{2,1,0:T(8,128)(2,1)}), bf16[32,16,2176]{2,1,0:T(8,128)(2,1)}, u32[]{:S(2)}, u32[]{:S(2)}) async-start(bf16[32,16,2176]{2,1,0:T(8,128)(2,1)} %bitcast.11), calls=%async_computation.4 | async-start | bytes 4456448 | tf_op jit(solution)/shard_map/all_to_all | solution.py:249
  241.3 51.6 %copy-start.15 = (s32[20]{0:T(128)S(1)}, s32[20]{0:T(128)}, u32[]{:S(2)}) copy-start(s32[20]{0:T(128)} %param.14) | copy-start | bytes 244
  254.3 38.7 %copy-start.10 = (f32[3,20,8,768]{3,2,1,0:T(8,128)S(1)}, f32[3,20,8,768]{3,2,1,0:T(8,128)}, u32[]{:S(2)}) copy-start(f32[3,20,8,768]{3,2,1,0:T(8,128)} %param.16) | copy-start | bytes 4423684
  293.0 3.0 copy-start.11
  296.0 1.6 copy-start.8
  299.3 35.0 %all-to-all-start.5 = ((bf16[32,3,8,768]{3,2,1,0:T(8,128)(2,1)}), bf16[32,3,8,768]{3,2,1,0:T(8,128)(2,1)S(1)}, u32[]{:S(2)}, u32[]{:S(2)}) async-start(bf16[32,3,8,768]{3,2,1,0:T(8,128)(2,1)} %copy.86), calls=%async_computation.6 | async-start | bytes 2359296 | tf_op jit(solution)/shard_map/all_to_all | solution.py:273
  308.1 3.0 copy-start.9
Sparse Core Ops, SparseCore 0:
  54.7 25.8 all-gather.7
  83.1 30.3 all-gather.5
  115.9 30.3 all-gather.3
  184.9 55.0 reduce-scatter.1

commit v5 on v4

--- a/solution.py
+++ b/solution.py
@@ -13,7 +13,7 @@
 
 
 lane_count = 128
-vmem_bytes = 40 * 1024 * 1024
+vmem_bytes = 60 * 1024 * 1024
 
 
 def whole(shape):

time: 343 us -> 336 us (0.980)
  local copies, waits for them, and re-layouts: 24.5 us -> 13 us
  Pallas kernels: 18.2 us -> 22.8 us
    unnamed x42 -> x30, local copies, waits for them, and re-layouts: 16.2 us -> 4.65 us
  transfers between devices with their start and end apart: 9 -> 9, of which waited for: 6 -> 6; matrix products, arithmetic and copies ran while one was open for 8% -> 9% of each run, Pallas kernels for 2% -> 2%
where the time goes in v5:
time: 336 us; the launch traced here: 335 us
  waiting for transfers between devices  186 us (55%)
  blocking collectives  38.6 us (11%)
  starting transfers between devices  33.2 us (10%)
  matrix products  24.4 us (7%)
  Pallas kernels  22.8 us (7%)
  between operations  14 us (4%)
  local copies, waits for them, and re-layouts  13 us (4%)
    all_to_all x2, waiting for transfers between devices, dispatch(): lax.all_to_all(packed, 'expert', split_axis=0, concat_axis=0, tiled=True)  88.8 us
    reduce_scatter x1, waiting for transfers between devices, body(): lax.psum_scatter(weight_grads, 'dp', scatter_dimension=1, tiled=True)  41 us
    all_to_all x1, blocking collectives, body(): lax.all_to_all(pieces, 'expert', split_axis=0, concat_axis=0, tiled=True)  38.6 us
    all_to_all x1, waiting for transfers between devices, body(): lax.all_to_all(outgoing, 'expert', split_axis=0, concat_axis=0, tiled=True)  24.7 us
    all_to_all x1, waiting for transfers between devices, body(): lax.all_to_all(leaving, 'expert', split_axis=0, concat_axis=0, tiled=True)  20 us
    pallas_call x1, Pallas kernels, unit_and_weight_grads(): pl.pallas_call(lambda *refs: grad_kernel(steps, *refs), grid=(2 * steps,)...  14.7 us
    all_to_all x1, starting transfers between devices, body(): lax.all_to_all(outgoing, 'expert', split_axis=0, concat_axis=0, tiled=True)  11.6 us
    all_to_all x2, starting transfers between devices, dispatch(): lax.all_to_all(packed, 'expert', split_axis=0, concat_axis=0, tiled=True)  11.3 us
  transfers between devices with their start and end apart: 9, of which 6 were waited for; matrix products, arithmetic and copies ran while one was open for 9% of the time, Pallas kernels for 2%

profile of v5, /device:TPU:2, one launch (start us, length us, event | category | flops | bytes accessed | tf_op | source)
XLA Modules:
  0.0 334.8 jit_solution(6917812929783401171)
XLA Ops:
  7.2 0.0 copy-start
  7.2 1.7 convolution_convert_fusion.4
  8.9 1.7 copy.77
  10.6 11.6 %all-to-all-start = ((bf16[32,3,8,768]{3,2,1,0:T(8,128)(2,1)}), bf16[32,3,8,768]{3,2,1,0:T(8,128)(2,1)S(1)}, u32[]{:S(2)}, u32[]{:S(2)}) async-start(bf16[32,3,8,768]{3,2,1,0:T(8,128)(2,1)} %copy.77), calls=%async_computation | async-start | bytes 2359296 | tf_op jit(solution)/shard_map/all_to_all | solution.py:198
  22.2 0.0 all-gather.8.cloned.1.call-start
  22.3 0.1 copy.71
  22.4 0.1 eq.101
  22.5 0.1 eq.90
  22.7 0.0 copy-start.6
  22.7 0.6 reduce-window.6
  23.3 0.2 slice_reduce_fusion
  23.5 0.1 broadcast_add_fusion
  23.7 0.0 copy-done.8
  23.7 0.1 fusion.20
  23.7 0.1 reduce_window_sum.26
  23.8 0.2 fusion.17
  24.0 0.1 and_select_fusion
  24.1 0.1 fusion.19
  24.2 0.1 select_reduce_fusion
  24.3 0.1 add.35
  24.4 0.1 copy.74
  24.5 0.2 fusion.10
  24.7 0.0 copy-start.7
  24.7 2.0 convolution_convert_fusion.1
  26.8 2.1 convolution_convert_fusion
  28.8 24.7 %all-to-all-done = bf16[32,3,8,768]{3,2,1,0:T(8,128)(2,1)S(1)} async-done(((bf16[32,3,8,768]{3,2,1,0:T(8,128)(2,1)}), bf16[32,3,8,768]{3,2,1,0:T(8,128)(2,1)S(1)}, u32[]{:S(2)}, u32[]{:S(2)}) %all-to-all-start) | async-done | bytes 1179680 | tf_op jit(solution)/shard_map/all_to_all | solution.py:198
  53.6 1.0 slice_bitcast_fusion
  54.6 0.0 all-gather.8.cloned.1.call-update
  54.6 0.0 all-gather.6.cloned.1.call-start
  54.7 0.7 all-gather.6.cloned.1.call-update
  55.4 5.2 %all-to-all-start.1 = ((bf16[32,16,2048]{2,1,0:T(8,128)(2,1)}), bf16[32,16,2048]{2,1,0:T(8,128)(2,1)S(1)}, u32[]{:S(2)}, u32[]{:S(2)}) async-start(bf16[32,16,2048]{2,1,0:T(8,128)(2,1)} %bitcast.2), calls=%async_computation.1 | async-start | bytes 4194304 | tf_op jit(solution)/shard_map/all_to_all | solution.py:225
  60.6 0.0 all-gather.4.cloned.1.call-start
  60.6 0.7 all-gather.4.cloned.1.call-update
  61.3 48.9 %all-to-all-done.1 = bf16[32,16,2048]{2,1,0:T(8,128)(2,1)S(1)} async-done(((bf16[32,16,2048]{2,1,0:T(8,128)(2,1)}), bf16[32,16,2048]{2,1,0:T(8,128)(2,1)S(1)}, u32[]{:S(2)}, u32[]{:S(2)}) %all-to-all-start.1) | async-done | bytes 2097184 | tf_op jit(solution)/shard_map/all_to_all | solution.py:225
  110.2 6.1 %all-to-all-start.2 = ((bf16[32,16,2048]{2,1,0:T(8,128)(2,1)}), bf16[32,16,2048]{2,1,0:T(8,128)(2,1)}, u32[]{:S(2)}, u32[]{:S(2)}) async-start(bf16[32,16,2048]{2,1,0:T(8,128)(2,1)} %bitcast.3), calls=%async_computation.2 | async-start | bytes 4194304 | tf_op jit(solution)/shard_map/all_to_all | solution.py:225
  116.4 0.0 reduce-scatter.2.cloned.1.call-start
  116.4 0.0 all-gather.8.cloned.1.call-done.up_w_ref
  116.4 4.8 %fusion.37.refs_4_ = f32[512,768]{1,0:T(8,128)} fusion(bf16[512,2048]{1,0:T(8,128)(2,1)S(1)} %bitcast.59, bf16[2048,768]{1,0:T(8,128)(2,1)} %all-gather.8.cloned.1.call-done.up_w_ref), kind=kOutput, calls=%fused_computation.70 | convolution fusion | flops 1610612736 | bytes 6815744 | tf_op jit(solution)/shard_map/dot_general | solution.py:242
  121.3 4.9 %fusion.36.refs_3_ = f32[512,768]{1,0:T(8,128)} fusion(bf16[512,2048]{1,0:T(8,128)(2,1)S(1)} %bitcast.60, bf16[2048,768]{1,0:T(8,128)(2,1)} %all-gather.6.cloned.1.call-done.gate_w_ref), kind=kOutput, calls=%fused_computation.69 | convolution fusion | flops 1610612736 | bytes 6815744 | tf_op jit(solution)/shard_map/dot_general | solution.py:241
  126.2 39.8 %all-to-all-done.2 = bf16[32,16,2048]{2,1,0:T(8,128)(2,1)} async-done(((bf16[32,16,2048]{2,1,0:T(8,128)(2,1)}), bf16[32,16,2048]{2,1,0:T(8,128)(2,1)}, u32[]{:S(2)}, u32[]{:S(2)}) %all-to-all-start.2) | async-done | bytes 2097184 | tf_op jit(solution)/shard_map/all_to_all | solution.py:225
  166.0 14.7 %shard_map.128 = (bf16[3,2048,768]{2,1,0:T(8,128)(2,1)}, bf16[512,2304]{1,0:T(8,128)(2,1)}, bf16[512,128]{1,0:T(8,128)(2,1)}) custom-call(bf16[512,2048]{1,0:T(8,128)(2,1)} %bitcast.61, bf16[512,2048]{1,0:T(8,128)(2,1)} %bitcast.5.refs_1_, bf16[2048,768]{1,0:T(8,128)(2,1)} %all-gather.4.cloned.1.call-done.refs_2_, f32[512,768]{1,0:T(8,128)} %fusion.36.refs_3_, ...), custom_call_target="tpu_custom_call" | custom-call | flops 6442450944 | bytes 24000000 | tf_op jit(solution)/shard_map/pallas_call | solution.py:90
  180.8 0.0 reduce-scatter.2.cloned.1.call-update
  180.8 8.1 %shard_map.129 = bf16[512,2176]{1,0:T(8,128)(2,1)} custom-call(bf16[512,2304]{1,0:T(8,128)(2,1)} %get-tuple-element.17.units_ref, bf16[2048,768]{1,0:T(8,128)(2,1)} %all-gather.6.cloned.1.call-done.gate_w_ref, bf16[2048,768]{1,0:T(8,128)(2,1)} %all-gather.8.cloned.1.call-done.up_w_ref, bf16[512,128]{1,0:T(8,128)(2,1)} %get-tuple-element.18.gate_ref), custom_call_target="tpu_custom_call" | custom-call | flops 3221225472 | bytes 10000000 | tf_op jit(solution)/shard_map/pallas_call | solution.py:149
  188.8 6.1 %all-to-all-start.3 = ((bf16[32,16,2176]{2,1,0:T(8,128)(2,1)}), bf16[32,16,2176]{2,1,0:T(8,128)(2,1)}, u32[]{:S(2)}, u32[]{:S(2)}) async-start(bf16[32,16,2176]{2,1,0:T(8,128)(2,1)} %bitcast.58), calls=%async_computation.4 | async-start | bytes 4456448 | tf_op jit(solution)/shard_map/all_to_all | solution.py:249
  195.0 41.0 %reduce-scatter.2.cloned.1.call-done = bf16[3,256,768]{2,1,0:T(8,128)(2,1)} async-done(((bf16[3,2048,768]{2,1,0:T(8,128)(2,1)}), bf16[3,256,768]{2,1,0:T(8,128)(2,1)}) %reduce-scatter.2.cloned.1.call-update) | async-done | bytes 1179664 | tf_op jit(solution)/shard_map/reduce_scatter | solution.py:246
  236.0 1.3 copy_bitcast_fusion.1
  237.3 0.0 copy-start.9
  237.4 9.8 %all-to-all-done.3 = bf16[32,16,2176]{2,1,0:T(8,128)(2,1)} async-done(((bf16[32,16,2176]{2,1,0:T(8,128)(2,1)}), bf16[32,16,2176]{2,1,0:T(8,128)(2,1)}, u32[]{:S(2)}, u32[]{:S(2)}) %all-to-all-start.3) | async-done | bytes 2228256 | tf_op jit(solution)/shard_map/all_to_all | solution.py:249
  247.2 38.6 %all_to_all.30 = bf16[32,3,8,768]{3,2,1,0:T(8,128)(2,1)S(1)} all-to-all(bf16[32,3,8,768]{3,2,1,0:T(8,128)(2,1)S(1)} %copy_bitcast_fusion.1), channel_id=1, replica_groups=mesh['dp'=8,'expert'=32] {'expert'}, dimensions={0} | all-to-all | bytes 2359296 | tf_op jit(solution)/shard_map/all_to_all | solution.py:265
  285.8 3.0 fusion.2
  288.9 1.6 convolution_convert_fusion.3
  290.5 0.0 copy-done.1
  290.5 1.7 copy.86
  292.2 3.9 %all-to-all-start.5 = ((bf16[32,3,8,768]{3,2,1,0:T(8,128)(2,1)}), bf16[32,3,8,768]{3,2,1,0:T(8,128)(2,1)S(1)}, u32[]{:S(2)}, u32[]{:S(2)}) async-start(bf16[32,3,8,768]{3,2,1,0:T(8,128)(2,1)} %copy.86), calls=%async_computation.6 | async-start | bytes 2359296 | tf_op jit(solution)/shard_map/all_to_all | solution.py:273
  296.1 0.1 copy.79
  296.2 1.2 convolution_reduce_fusion
  297.4 0.8 reshape_squeeze.15
  298.2 1.5 divide_convert_fusion
  299.7 1.3 copy.88
  301.0 3.0 convolution_convert_fusion.2
  304.0 1.6 copy.90
  305.6 1.6 copy.91
  307.2 20.0 %all-to-all-done.5 = bf16[32,3,8,768]{3,2,1,0:T(8,128)(2,1)S(1)} async-done(((bf16[32,3,8,768]{3,2,1,0:T(8,128)(2,1)}), bf16[32,3,8,768]{3,2,1,0:T(8,128)(2,1)S(1)}, u32[]{:S(2)}, u32[]{:S(2)}) %all-to-all-start.5) | async-done | bytes 1179680 | tf_op jit(solution)/shard_map/all_to_all | solution.py:273
  327.2 1.1 copy.117
  (27 shorter events, 0.1 us)
Async XLA Ops:
  7.2 17.6 %copy-start = (bf16[128,2048]{1,0:T(8,128)(2,1)S(1)}, bf16[128,2048]{1,0:T(8,128)(2,1)}, u32[]{:S(2)}) copy-start(bf16[128,2048]{1,0:T(8,128)(2,1)} %param.9) | copy-start | bytes 1572868
  10.6 11.7 %copy-start.11 = (s32[128,2]{0,1:T(2,128)S(1)}, s32[128,2]{0,1:T(2,128)}, u32[]{:S(2)}) copy-start(s32[128,2]{0,1:T(2,128)} %param.11) | copy-start | bytes 3076
  10.6 13.1 %copy-start.8 = (s32[32]{0:T(128)S(1)}, s32[32]{0:T(128)}, u32[]{:S(2)}) copy-start(s32[32]{0:T(128)} %param.13) | copy-start | bytes 388
  10.6 13.9 %copy-start.10 = (bf16[128,2]{0,1:T(2,128)(2,1)S(1)}, bf16[128,2]{0,1:T(2,128)(2,1)}, u32[]{:S(2)}) copy-start(bf16[128,2]{0,1:T(2,128)(2,1)} %param.12) | copy-start | bytes 1540
  10.6 43.0 %all-to-all-start = ((bf16[32,3,8,768]{3,2,1,0:T(8,128)(2,1)}), bf16[32,3,8,768]{3,2,1,0:T(8,128)(2,1)S(1)}, u32[]{:S(2)}, u32[]{:S(2)}) async-start(bf16[32,3,8,768]{3,2,1,0:T(8,128)(2,1)} %copy.77), calls=%async_computation | async-start | bytes 2359296 | tf_op jit(solution)/shard_map/all_to_all | solution.py:198
  22.2 94.2 %all-gather.8.cloned.1.call-start = ((), (), s32[]{:S(2)}) async-start(), calls=%async_computation.9 | async-start | bytes 3538944 | tf_op jit(solution)/shard_map/all_gather | solution.py:233
  22.7 4.1 %copy-start.6 = (bf16[128,2048]{1,0:T(8,128)(2,1)S(1)}, bf16[128,2048]{1,0:T(8,128)(2,1)}, u32[]{:S(2)}) copy-start(bf16[128,2048]{1,0:T(8,128)(2,1)} %param.10) | copy-start | bytes 1572868
  24.7 2.1 copy-start.7
  54.6 66.7 %all-gather.6.cloned.1.call-start = ((), (), s32[]{:S(2)}) async-start(), calls=%async_computation.8 | async-start | bytes 3538944 | tf_op jit(solution)/shard_map/all_gather | solution.py:233
  55.4 54.9 %all-to-all-start.1 = ((bf16[32,16,2048]{2,1,0:T(8,128)(2,1)}), bf16[32,16,2048]{2,1,0:T(8,128)(2,1)S(1)}, u32[]{:S(2)}, u32[]{:S(2)}) async-start(bf16[32,16,2048]{2,1,0:T(8,128)(2,1)} %bitcast.2), calls=%async_computation.1 | async-start | bytes 4194304 | tf_op jit(solution)/shard_map/all_to_all | solution.py:225
  60.6 105.5 %all-gather.4.cloned.1.call-start = ((), (), s32[]{:S(2)}) async-start(), calls=%async_computation.7 | async-start | bytes 3538944 | tf_op jit(solution)/shard_map/all_gather | solution.py:233
  110.2 11.1 %copy-start.4 = (bf16[32,16,2048]{2,1,0:T(8,128)(2,1)}, bf16[32,16,2048]{2,1,0:T(8,128)(2,1)S(1)}, u32[]{:S(2)}) copy-start(bf16[32,16,2048]{2,1,0:T(8,128)(2,1)S(1)} %all-to-all-done.1) | copy-start | bytes 6291460
  110.2 55.8 %all-to-all-start.2 = ((bf16[32,16,2048]{2,1,0:T(8,128)(2,1)}), bf16[32,16,2048]{2,1,0:T(8,128)(2,1)}, u32[]{:S(2)}, u32[]{:S(2)}) async-start(bf16[32,16,2048]{2,1,0:T(8,128)(2,1)} %bitcast.3), calls=%async_computation.2 | async-start | bytes 4194304 | tf_op jit(solution)/shard_map/all_to_all | solution.py:225
  116.4 119.6 %reduce-scatter.2.cloned.1.call-start = ((), (), s32[]{:S(2)}) async-start(), calls=%async_computation.10 | async-start | bytes 10616832 | tf_op jit(solution)/shard_map/reduce_scatter | solution.py:246
  188.8 58.4 %all-to-all-start.3 = ((bf16[32,16,2176]{2,1,0:T(8,128)(2,1)}), bf16[32,16,2176]{2,1,0:T(8,128)(2,1)}, u32[]{:S(2)}, u32[]{:S(2)}) async-start(bf16[32,16,2176]{2,1,0:T(8,128)(2,1)} %bitcast.58), calls=%async_computation.4 | async-start | bytes 4456448 | tf_op jit(solution)/shard_map/all_to_all | solution.py:249
  237.3 48.5 %copy-start.9 = (s32[20]{0:T(128)S(1)}, s32[20]{0:T(128)}, u32[]{:S(2)}) copy-start(s32[20]{0:T(128)} %param.14) | copy-start | bytes 244
  247.2 38.7 %copy-start.3 = (f32[3,20,8,768]{3,2,1,0:T(8,128)S(1)}, f32[3,20,8,768]{3,2,1,0:T(8,128)}, u32[]{:S(2)}) copy-start(f32[3,20,8,768]{3,2,1,0:T(8,128)} %param.16) | copy-start | bytes 4423684
  285.8 3.0 copy-start.5
  288.9 1.6 copy-start.1
  292.2 35.0 %all-to-all-start.5 = ((bf16[32,3,8,768]{3,2,1,0:T(8,128)(2,1)}), bf16[32,3,8,768]{3,2,1,0:T(8,128)(2,1)S(1)}, u32[]{:S(2)}, u32[]{:S(2)}) async-start(bf16[32,3,8,768]{3,2,1,0:T(8,128)(2,1)} %copy.86), calls=%async_computation.6 | async-start | bytes 2359296 | tf_op jit(solution)/shard_map/all_to_all | solution.py:273
  301.0 3.0 copy-start.2
Sparse Core Ops, SparseCore 0:
  54.7 25.8 all-gather.7
  83.1 30.3 all-gather.5
  115.9 30.3 all-gather.3
  180.9 55.0 reduce-scatter.1

commit v6 on v5

v6 whole, which is shorter than its diff:
```python
import jax
import jax.numpy as jnp
from jax import lax
from jax.experimental import pallas as pl
from jax.experimental.pallas import tpu as pltpu
from jax.sharding import PartitionSpec as P

beta_one = 0.9
beta_two = 0.95
learn_rate = 0.02
adam_step = 10.0
adam_eps = 1e-08


lane_count = 128
vmem_bytes = 60 * 1024 * 1024


def whole(shape):
    return pl.BlockSpec(shape, lambda i: (0,) * len(shape), pipeline_mode=pl.Buffered(1))


def flat_rows(ref):
    return ref[...].reshape(-1, ref.shape[-1])


def grad_kernel(
    steps,
    x_ref,
    y_ref,
    gate_w_ref,
    up_w_ref,
    down_w_ref,
    dw_ref,
    units_ref,
    gate_ref,
    first_ref,
    second_ref,
    u_ref,
):
    step = pl.program_id(0)
    rows, hidden = u_ref.shape
    part = 128
    products = ((first_ref, x_ref, gate_w_ref), (second_ref, x_ref, up_w_ref), (u_ref, y_ref, down_w_ref))

    @pl.when(step == 0)
    def _():
        for total, left, right in products:
            total[...] = jnp.dot(
                flat_rows(left), flat_rows(right), preferred_element_type=jnp.float32
            )

    @pl.when((step > 0) & (step < steps))
    def _():
        for total, left, right in products:
            total[...] += jnp.dot(
                flat_rows(left), flat_rows(right), preferred_element_type=jnp.float32
            )

    @pl.when(step == steps - 1)
    def _():
        for start in range(0, rows, part):
            span = pl.ds(start, part)
            weighted = u_ref[span]
            first_pre = first_ref[span]
            second_pre = second_ref[span]
            sigmoid_h = jax.nn.sigmoid(first_pre)
            gated = first_pre * sigmoid_h
            activated = gated * second_pre
            total = jnp.sum(activated * weighted, axis=1, keepdims=True)
            grad_first = weighted * second_pre * sigmoid_h * (1.0 + first_pre * (1.0 - sigmoid_h))
            units_ref[span, :hidden] = grad_first.astype(jnp.bfloat16)
            units_ref[span, hidden : 2 * hidden] = (weighted * gated).astype(jnp.bfloat16)
            units_ref[span, 2 * hidden :] = activated.astype(jnp.bfloat16)
            gate_ref[span] = jnp.broadcast_to(total, (part, lane_count)).astype(jnp.bfloat16)

    @pl.when(step >= steps)
    def _():
        both = jnp.dot(
            flat_rows(x_ref).T, units_ref[:, : 2 * hidden], preferred_element_type=jnp.float32
        ).astype(jnp.bfloat16)
        dw_ref[0] = both[:, :hidden]
        dw_ref[1] = both[:, hidden:]
        dw_ref[2] = jnp.dot(
            flat_rows(y_ref).T, units_ref[:, 2 * hidden :], preferred_element_type=jnp.float32
        ).astype(jnp.bfloat16)


def weight_block(stacked, matrix, depth, block_of):
    _, _, rows, hidden = stacked.shape
    return pl.BlockSpec((depth // rows, 1, rows, hidden), lambda i: (block_of(i), matrix, 0, 0))


def unit_and_weight_grads(received, stacked):
    sources, _, capacity, width = received.shape
    hidden = stacked.shape[3]
    rows = sources * capacity
    depth = 512
    steps = width // depth

    def row_block(which):
        return pl.BlockSpec(
            (sources, 1, capacity, depth), lambda i: (0, which, 0, lax.rem(i, steps))
        )

    return pl.pallas_call(
        lambda *refs: grad_kernel(steps, *refs),
        grid=(2 * steps,),
        in_specs=[row_block(0), row_block(1)]
        + [weight_block(stacked, c, depth, lambda i: jnp.minimum(i, steps - 1)) for c in range(3)],
        out_specs=[
            pl.BlockSpec((3, depth, hidden), lambda i: (0, jnp.maximum(i - steps, 0), 0)),
            whole((rows, 3 * hidden)),
            whole((rows, lane_count)),
        ],
        out_shape=[
            jax.ShapeDtypeStruct((3, width, hidden), jnp.bfloat16),
            jax.ShapeDtypeStruct((rows, 3 * hidden), jnp.bfloat16),
            jax.ShapeDtypeStruct((rows, lane_count), jnp.bfloat16),
        ],
        scratch_shapes=[pltpu.VMEM((rows, hidden), jnp.float32)] * 3,
        compiler_params=pltpu.CompilerParams(vmem_limit_bytes=vmem_bytes),
        cost_estimate=pl.CostEstimate(
            flops=12 * rows * width * hidden,
            bytes_accessed=30_000_000,
            transcendentals=rows * hidden,
        ),
    )(received, received, stacked, stacked, stacked)


def part_kernel(units_ref, gate_w_ref, up_w_ref, gate_ref, out_ref):
    step = pl.program_id(0)
    hidden = gate_w_ref.shape[-1]
    over_hidden = (((1,), (1,)), ((), ()))

    @pl.when(step == 0)
    def _():
        out_ref[:, pl.ds(out_ref.shape[1] - lane_count, lane_count)] = gate_ref[...]

    gate_w = flat_rows(gate_w_ref)
    depth = gate_w.shape[0]
    out_ref[:, pl.ds(pl.multiple_of(step * depth, depth), depth)] = (
        lax.dot_general(
            units_ref[:, :hidden], gate_w, over_hidden, preferred_element_type=jnp.float32
        )
        + lax.dot_general(
            units_ref[:, hidden : 2 * hidden],
            flat_rows(up_w_ref),
            over_hidden,
            preferred_element_type=jnp.float32,
        )
    ).astype(jnp.bfloat16)


def input_parts(units, stacked, gate_part):
    rows = units.shape[0]
    hidden = stacked.shape[3]
    width = stacked.shape[0] * stacked.shape[2]
    depth = 512
    return pl.pallas_call(
        part_kernel,
        grid=(width // depth,),
        in_specs=[
            whole((rows, 3 * hidden)),
            weight_block(stacked, 0, depth, lambda i: i),
            weight_block(stacked, 1, depth, lambda i: i),
            whole((rows, lane_count)),
        ],
        out_specs=whole((rows, width + lane_count)),
        out_shape=jax.ShapeDtypeStruct((rows, width + lane_count), jnp.bfloat16),
        compiler_params=pltpu.CompilerParams(vmem_limit_bytes=vmem_bytes),
        cost_estimate=pl.CostEstimate(
            flops=4 * rows * width * hidden, bytes_accessed=10_000_000, transcendentals=0
        ),
    )(units, stacked, stacked, gate_part)


def adam_kernel(
    new_place_ref,
    old_place_ref,
    returned_ref,
    stored_ref,
    first_ref,
    second_ref,
    new_first_ref,
    new_second_ref,
    leaving_ref,
    row_ref,
    state_ref,
):
    slots, experts = returned_ref.shape[0], stored_ref.shape[1]
    first_scale = learn_rate / (1.0 - beta_one**adam_step)
    second_scale = 1.0 / (1.0 - beta_two**adam_step)
    for row in range(experts):
        row_ref[old_place_ref[row]] = row
    state_ref[...] = jnp.zeros_like(state_ref)
    for slot in range(slots):
        row = row_ref[new_place_ref[slot]]
        state_ref[row] = state_ref[row] + returned_ref[slot, 0].astype(jnp.float32)
    for row in range(experts):
        grad = state_ref[row]
        new_first = beta_one * first_ref[0, row] + (1.0 - beta_one) * grad
        new_second = beta_two * second_ref[0, row] + (1.0 - beta_two) * grad * grad
        new_first_ref[0, row] = new_first
        new_second_ref[0, row] = new_second
        state_ref[row] = stored_ref[0, row].astype(jnp.float32) - first_scale * new_first / (
            jnp.sqrt(second_scale * new_second) + adam_eps
        )
    for slot in range(slots):
        leaving_ref[slot, 0] = state_ref[row_ref[new_place_ref[slot]]].astype(jnp.bfloat16)


def adam_update(new_place, old_place, returned, stored, first, second):
    slots, matrices, rows, hidden = returned.shape
    experts = stored.shape[1]
    by_slot = pl.BlockSpec((slots, 1, rows, hidden), lambda i: (0, i, 0, 0))
    by_row = pl.BlockSpec((1, experts, rows, hidden), lambda i: (i, 0, 0, 0))
    scalars = pl.BlockSpec(memory_space=pltpu.SMEM)
    return pl.pallas_call(
        adam_kernel,
        grid=(matrices,),
        in_specs=[scalars, scalars, by_slot, by_row, by_row, by_row],
        out_specs=[by_row, by_row, by_slot],
        out_shape=[
            jax.ShapeDtypeStruct(first.shape, jnp.float32),
            jax.ShapeDtypeStruct(second.shape, jnp.float32),
            jax.ShapeDtypeStruct(returned.shape, jnp.bfloat16),
        ],
        scratch_shapes=[
            pltpu.SMEM((experts,), jnp.int32),
            pltpu.VMEM((experts, rows, hidden), jnp.float32),
        ],
        compiler_params=pltpu.CompilerParams(vmem_limit_bytes=vmem_bytes),
        cost_estimate=pl.CostEstimate(
            flops=20 * first.size, bytes_accessed=9_000_000, transcendentals=2 * first.size
        ),
    )(new_place, old_place, returned, stored, first, second)


def body(
    tokens, cotangent, routing, gates, new_place, old_place, weights, first_moment, second_moment
):
    tok_count, feature_width = tokens.shape
    top_count = routing.shape[1]
    expert_count = weights.shape[1]
    block_rows = weights.shape[2]
    hidden = weights.shape[3]
    slot_count = lax.axis_size("expert")
    capacity = 2 * tok_count * top_count // slot_count
    buffer_rows = slot_count * capacity
    source = lax.axis_index("expert")
    expert_ids = jnp.arange(expert_count, dtype=jnp.int32)
    slot_ids = jnp.arange(slot_count, dtype=jnp.int32)
    place_hot = (new_place[:, None] == expert_ids[None, :]).astype(jnp.int32)
    slot_state = (new_place[:, None] == old_place[None, :]).astype(jnp.bfloat16)

    outgoing = jnp.einsum(
        "se,cerh->scrh", slot_state, weights, preferred_element_type=jnp.float32
    ).astype(jnp.bfloat16)
    arrived = lax.all_to_all(outgoing, "expert", split_axis=0, concat_axis=0, tiled=True)

    replica_count = jnp.sum(place_hot, axis=0)
    earlier = jnp.cumsum(place_hot, axis=0) - place_hot
    slot_rank = jnp.sum(earlier * place_hot, axis=1)
    wanted = source % replica_count
    chosen = place_hot * (slot_rank[:, None] == wanted[None, :]).astype(jnp.int32)
    target_slot = jnp.sum(chosen * slot_ids[:, None], axis=0)
    flat_experts = routing.reshape(-1)
    assign_hot = (flat_experts[:, None] == expert_ids[None, :]).astype(jnp.int32)
    position = jnp.sum((jnp.cumsum(assign_hot, axis=0) - assign_hot) * assign_hot, axis=1)
    target = jnp.sum(assign_hot * target_slot[None, :], axis=1)
    destination = target * capacity + position
    assign_dest = (
        destination[:, None] == jnp.arange(buffer_rows, dtype=jnp.int32)[None, :]
    ).astype(jnp.bfloat16)
    token_dest = jnp.sum(assign_dest.reshape(tok_count, top_count, buffer_rows), axis=1)

    pair_rows = 2 * capacity
    first_row = (target * pair_rows + position).reshape(tok_count, top_count)
    row_of = jnp.concatenate([first_row, first_row + capacity])
    scale_of = jnp.concatenate([jnp.ones_like(gates), gates])
    message_rows = jnp.arange(slot_count * pair_rows, dtype=jnp.int32)
    both_dest = sum(
        jnp.where(row_of[:, k, None] == message_rows[None, :], scale_of[:, k, None], 0)
        for k in range(top_count)
    ).astype(jnp.bfloat16)
    packed = (
        jnp.einsum(
            "tb,td->bd",
            both_dest,
            jnp.concatenate([tokens, cotangent]),
            preferred_element_type=jnp.float32,
        )
        .astype(jnp.bfloat16)
        .reshape(slot_count, pair_rows, feature_width)
    )
    arrived, packed = lax.optimization_barrier((arrived, packed))
    stacked = lax.all_gather(
        jnp.transpose(arrived, (1, 0, 2, 3)).reshape(3, slot_count * block_rows, hidden),
        "dp",
        axis=0,
    )
    received = lax.all_to_all(packed, "expert", split_axis=0, concat_axis=0, tiled=True).reshape(
        slot_count, 2, capacity, feature_width
    )
    weight_grads, units, gate_part = unit_and_weight_grads(received, stacked)
    summed = lax.psum_scatter(weight_grads, "dp", scatter_dimension=1, tiled=True)
    pieces = jnp.transpose(summed.reshape(3, slot_count, block_rows, hidden), (1, 0, 2, 3))
    input_part = input_parts(units, stacked, gate_part)
    back = lax.all_to_all(
        input_part.reshape(slot_count, capacity, feature_width + lane_count),
        "expert",
        split_axis=0,
        concat_axis=0,
        tiled=True,
    ).reshape(buffer_rows, feature_width + lane_count)
    pieces, back = lax.optimization_barrier((pieces, back))
    input_grad = jnp.einsum(
        "tb,bd->td", token_dest, back[:, :feature_width], preferred_element_type=jnp.float32
    ).astype(jnp.bfloat16)
    gate_sum = jnp.einsum(
        "ab,bl->al", assign_dest, back[:, feature_width:], preferred_element_type=jnp.float32
    )[:, 0].reshape(tok_count, top_count)
    gate_grad = (gate_sum / gates.astype(jnp.float32)).astype(jnp.bfloat16)

    returned = lax.all_to_all(pieces, "expert", split_axis=0, concat_axis=0, tiled=True)
    new_first, new_second, leaving = adam_update(
        new_place, old_place, returned, weights, first_moment, second_moment
    )
    landed = lax.all_to_all(leaving, "expert", split_axis=0, concat_axis=0, tiled=True)
    slot_weights = jnp.transpose(landed, (1, 0, 2, 3)).reshape(
        3, 1, slot_count * block_rows, hidden
    )
    return (input_grad, gate_grad, slot_weights, new_first, new_second)


def solution(mesh):
    placed = (
        P(("dp", "expert"), None),
        P(("dp", "expert"), None),
        P(("dp", "expert"), None),
        P(("dp", "expert"), None),
        P(),
        P(),
        P(None, None, ("dp", "expert"), None),
        P(None, None, ("dp", "expert"), None),
        P(None, None, ("dp", "expert"), None),
    )
    return jax.shard_map(
        body,
        mesh=mesh,
        in_specs=placed,
        out_specs=(
            P(("dp", "expert"), None),
            P(("dp", "expert"), None),
            P(None, "expert", "dp", None),
            P(None, None, ("dp", "expert"), None),
            P(None, None, ("dp", "expert"), None),
        ),
        check_vma=False,
    )
```

time: 336 us -> 327 us (0.973)
  blocking collectives: 38.6 us -> 140 us
  waiting for transfers between devices: 186 us -> 102 us
  matrix products: 24.4 us -> 7.74 us
  starting transfers between devices: 33.2 us -> 20.6 us
  Pallas kernels: 22.8 us -> 31.9 us
  local copies, waits for them, and re-layouts: 13 us -> 7.93 us
    all_to_all x0 -> x1, blocking collectives: none -> 101 us  [body(): lax.all_to_all(packed, 'expert', split_axis=0, concat_axis=0, tiled=True)]
    all_to_all x2 -> x0, waiting for transfers between devices: 88.8 us -> none  [dispatch(): lax.all_to_all(packed, 'expert', split_axis=0, concat_axis=0, tiled=True)]
    dot_general x6 -> x1, matrix products: 18.5 us -> 3.64 us  [body(): jnp.einsum('tb,td->bd', both_dest, jnp.concatenate([tokens, cotangent]),...]
    all_to_all x2 -> x0, starting transfers between devices: 11.3 us -> none  [dispatch(): lax.all_to_all(packed, 'expert', split_axis=0, concat_axis=0, tiled=True)]
    pallas_call x0 -> x1, Pallas kernels: none -> 5.76 us  [adam_update(): pl.pallas_call(adam_kernel, grid=(matrices,), in_specs=[scalars, scalars,...]
    all_to_all x1, waiting for transfers between devices: 20 us -> 25.4 us  [body(): lax.all_to_all(leaving, 'expert', split_axis=0, concat_axis=0, tiled=True)]
  transfers between devices with their start and end apart: 9 -> 5, of which waited for: 6 -> 4; matrix products, arithmetic and copies ran while one was open for 9% -> 4% of each run, Pallas kernels for 2% -> 2%
where the time goes in v6:
time: 327 us; the launch traced here: 326 us
  blocking collectives  140 us (43%)
  waiting for transfers between devices  102 us (31%)
  Pallas kernels  31.9 us (10%)
  starting transfers between devices  20.6 us (6%)
  between operations  14.2 us (4%)
  local copies, waits for them, and re-layouts  7.93 us (2%)
  matrix products  7.74 us (2%)
    all_to_all x1, blocking collectives, body(): lax.all_to_all(packed, 'expert', split_axis=0, concat_axis=0, tiled=True)  101 us
    reduce_scatter x1, waiting for transfers between devices, body(): lax.psum_scatter(weight_grads, 'dp', scatter_dimension=1, tiled=True)  41.1 us
    all_to_all x1, blocking collectives, body(): lax.all_to_all(pieces, 'expert', split_axis=0, concat_axis=0, tiled=True)  38.6 us
    all_to_all x1, waiting for transfers between devices, body(): lax.all_to_all(leaving, 'expert', split_axis=0, concat_axis=0, tiled=True)  25.4 us
    all_to_all x1, waiting for transfers between devices, body(): lax.all_to_all(outgoing, 'expert', split_axis=0, concat_axis=0, tiled=True)  25.3 us
    pallas_call x1, Pallas kernels, unit_and_weight_grads(): pl.pallas_call(lambda *refs: grad_kernel(steps, *refs), grid=(2 * steps,)...  18 us
    all_to_all x1, starting transfers between devices, body(): lax.all_to_all(outgoing, 'expert', split_axis=0, concat_axis=0, tiled=True)  11.6 us
    all_to_all x1, waiting for transfers between devices, body(): lax.all_to_all(input_part.reshape(slot_count, capacity, feature_width + l...  9.79 us
  transfers between devices with their start and end apart: 5, of which 4 were waited for; matrix products, arithmetic and copies ran while one was open for 4% of the time, Pallas kernels for 2%

profile of v6, /device:TPU:2, one launch (start us, length us, event | category | flops | bytes accessed | tf_op | source)
XLA Modules:
  0.0 326.3 jit_solution(13316691949637372811)
XLA Ops:
  7.2 1.7 convolution_convert_fusion.2
  8.8 1.7 copy.62
  10.5 0.0 copy-start.1
  10.5 0.0 copy-start
  10.5 0.0 copy-start.2
  10.5 0.0 copy-start.3
  10.5 0.0 copy-start.4
  10.5 11.6 %all-to-all-start = ((bf16[32,3,8,768]{3,2,1,0:T(8,128)(2,1)}), bf16[32,3,8,768]{3,2,1,0:T(8,128)(2,1)S(1)}, u32[]{:S(2)}, u32[]{:S(2)}) async-start(bf16[32,3,8,768]{3,2,1,0:T(8,128)(2,1)} %copy.62), calls=%async_computation | async-start | bytes 2359296 | tf_op jit(solution)/shard_map/all_to_all | solution.py:260
  22.2 0.0 all-gather.2.cloned.1.call-start
  22.2 0.0 copy-done.1
  22.2 0.1 copy.56
  22.3 0.1 eq.131
  22.5 0.1 eq.120
  22.6 0.6 reduce-window.6
  23.2 0.2 slice_reduce_fusion
  23.5 0.1 broadcast_add_fusion.1
  23.6 0.0 copy-done
  23.6 0.1 fusion.26
  23.7 0.1 reduce_window_sum.26
  23.7 0.2 fusion.23
  23.9 0.1 and_select_fusion
  24.0 0.1 fusion.25
  24.1 0.1 select_reduce_fusion
  24.2 0.1 add.41
  24.4 0.1 copy.63
  24.5 0.1 copy.64
  24.5 0.0 copy-done.2
  24.6 0.0 copy-done.3
  24.6 0.0 copy-done.4
  24.6 3.6 %convolution_convert_fusion = bf16[1024,2048]{1,0:T(8,128)(2,1)} fusion(bf16[128,2048]{1,0:T(8,128)(2,1)S(1)} %copy-done.3, bf16[128,2048]{1,0:T(8,128)(2,1)S(1)} %copy-done.4, s32[256]{0:T(256)S(1)} %bitcast.46, s32[256]{0:T(256)S(1)} %bitcast.45, bf16[256]{0:T(256)(128)(2,1)S(1)} %get-tuple-element.48, bf16[256]{0:T(256)(128)(2,1)S(1)} %get-tuple-element.47), kind=kOutput, calls=%fused_computation | convolution fusion | flops 1080033280 | bytes 5245952 | tf_op jit(solution)/shard_map/tb,td->bd/dot_general | solution.py:288
  28.3 25.3 %all-to-all-done = bf16[32,3,8,768]{3,2,1,0:T(8,128)(2,1)S(1)} async-done(((bf16[32,3,8,768]{3,2,1,0:T(8,128)(2,1)}), bf16[32,3,8,768]{3,2,1,0:T(8,128)(2,1)S(1)}, u32[]{:S(2)}, u32[]{:S(2)}) %all-to-all-start) | async-done | bytes 1179680 | tf_op jit(solution)/shard_map/all_to_all | solution.py:260
  53.5 1.1 copy.79
  54.6 0.0 all-gather.2.cloned.1.call-update
  54.6 0.0 reduce-scatter.2.cloned.1.call-start
  54.7 101.0 %all_to_all.25 = bf16[32,32,2048]{2,1,0:T(8,128)(2,1)} all-to-all(bf16[32,32,2048]{2,1,0:T(8,128)(2,1)} %bitcast.40), channel_id=1, replica_groups=mesh['dp'=8,'expert'=32] {'expert'}, dimensions={0} | all-to-all | bytes 8388608 | tf_op jit(solution)/shard_map/all_to_all | solution.py:303
  155.7 0.0 all-gather.2.cloned.1.call-done.refs_2_.refs_3_.refs_4_.gate_w_ref.up_w_ref
  155.7 18.0 %shard_map.128 = (bf16[3,2048,768]{2,1,0:T(8,128)(2,1)}, bf16[512,2304]{1,0:T(8,128)(2,1)}, bf16[512,128]{1,0:T(8,128)(2,1)}) custom-call(bf16[32,2,16,2048]{3,2,1,0:T(8,128)(2,1)} %bitcast.36, bf16[32,2,16,2048]{3,2,1,0:T(8,128)(2,1)} %bitcast.37, bf16[8,3,256,768]{3,2,1,0:T(8,128)(2,1)} %all-gather.2.cloned.1.call-done.refs_2_.refs_3_.refs_4_.gate_w_ref.up_w_ref, ...), custom_call_target="tpu_custom_call" | custom-call | flops 9663676416 | bytes 30000000 | tf_op jit(solution)/shard_map/pallas_call | solution.py:106
  173.7 0.0 reduce-scatter.2.cloned.1.call-update
  173.7 8.1 %shard_map.129 = bf16[512,2176]{1,0:T(8,128)(2,1)} custom-call(bf16[512,2304]{1,0:T(8,128)(2,1)} %get-tuple-element.18.units_ref, bf16[8,3,256,768]{3,2,1,0:T(8,128)(2,1)} %all-gather.2.cloned.1.call-done.refs_2_.refs_3_.refs_4_.gate_w_ref.up_w_ref, bf16[8,3,256,768]{3,2,1,0:T(8,128)(2,1)} %all-gather.2.cloned.1.call-done.refs_2_.refs_3_.refs_4_.gate_w_ref.up_w_ref, ...), custom_call_target="tpu_custom_call" | custom-call | flops 3221225472 | bytes 10000000 | tf_op jit(solution)/shard_map/pallas_call | solution.py:160
  181.8 4.9 %all-to-all-start.2 = ((bf16[32,16,2176]{2,1,0:T(8,128)(2,1)}), bf16[32,16,2176]{2,1,0:T(8,128)(2,1)S(1)}, u32[]{:S(2)}, u32[]{:S(2)}) async-start(bf16[32,16,2176]{2,1,0:T(8,128)(2,1)} %bitcast.38), calls=%async_computation.3 | async-start | bytes 4456448 | tf_op jit(solution)/shard_map/all_to_all | solution.py:310
  186.7 41.1 %reduce-scatter.2.cloned.1.call-done = bf16[3,256,768]{2,1,0:T(8,128)(2,1)} async-done(((bf16[3,2048,768]{2,1,0:T(8,128)(2,1)}), bf16[3,256,768]{2,1,0:T(8,128)(2,1)}) %reduce-scatter.2.cloned.1.call-update) | async-done | bytes 1179664 | tf_op jit(solution)/shard_map/reduce_scatter | solution.py:307
  227.8 1.3 copy_bitcast_fusion.1
  229.2 9.8 %all-to-all-done.2 = bf16[32,16,2176]{2,1,0:T(8,128)(2,1)S(1)} async-done(((bf16[32,16,2176]{2,1,0:T(8,128)(2,1)}), bf16[32,16,2176]{2,1,0:T(8,128)(2,1)S(1)}, u32[]{:S(2)}, u32[]{:S(2)}) %all-to-all-start.2) | async-done | bytes 2228256 | tf_op jit(solution)/shard_map/all_to_all | solution.py:310
  239.0 38.6 %all_to_all.26.returned_ref = bf16[32,3,8,768]{3,2,1,0:T(8,128)(2,1)} all-to-all(bf16[32,3,8,768]{3,2,1,0:T(8,128)(2,1)S(1)} %copy_bitcast_fusion.1), channel_id=1, replica_groups=mesh['dp'=8,'expert'=32] {'expert'}, dimensions={0} | all-to-all | bytes 2359296 | tf_op jit(solution)/shard_map/all_to_all | solution.py:326
  277.5 5.8 %shard_map.130 = (f32[3,20,8,768]{3,2,1,0:T(8,128)}, f32[3,20,8,768]{3,2,1,0:T(8,128)}, bf16[32,3,8,768]{3,2,1,0:T(8,128)(2,1)}) custom-call(s32[32]{0:T(128)} %new_place_ref.1, s32[20]{0:T(128)} %old_place_ref.1, bf16[32,3,8,768]{3,2,1,0:T(8,128)(2,1)} %all_to_all.26.returned_ref, bf16[3,20,8,768]{3,2,1,0:T(8,128)(2,1)} %stored_ref.1, ...), custom_call_target="tpu_custom_call" | custom-call | flops 7372800 | bytes 9000000 | tf_op jit(solution)/shard_map/pallas_call | solution.py:219
  283.3 3.9 %all-to-all-start.4 = ((bf16[32,3,8,768]{3,2,1,0:T(8,128)(2,1)}), bf16[32,3,8,768]{3,2,1,0:T(8,128)(2,1)S(1)}, u32[]{:S(2)}, u32[]{:S(2)}) async-start(bf16[32,3,8,768]{3,2,1,0:T(8,128)(2,1)} %get-tuple-element.22), calls=%async_computation.5 | async-start | bytes 2359296 | tf_op jit(solution)/shard_map/all_to_all | solution.py:330
  287.3 0.1 copy.67
  287.4 0.1 add.39
  287.5 0.1 copy.59
  287.6 0.8 fusion.13
  288.4 0.3 convolution_reduce_fusion
  288.6 0.1 reshape_squeeze.3
  288.8 0.6 divide_convert_fusion
  289.4 1.3 copy.69
  290.8 2.2 convolution_convert_fusion.1
  292.9 25.4 %all-to-all-done.4 = bf16[32,3,8,768]{3,2,1,0:T(8,128)(2,1)S(1)} async-done(((bf16[32,3,8,768]{3,2,1,0:T(8,128)(2,1)}), bf16[32,3,8,768]{3,2,1,0:T(8,128)(2,1)S(1)}, u32[]{:S(2)}, u32[]{:S(2)}) %all-to-all-start.4) | async-done | bytes 1179680 | tf_op jit(solution)/shard_map/all_to_all | solution.py:330
  318.3 1.1 copy_bitcast_fusion
  (10 shorter events, 0.1 us)
Async XLA Ops:
  10.5 11.7 %copy-start.1 = (s32[128,2]{0,1:T(2,128)S(1)}, s32[128,2]{0,1:T(2,128)}, u32[]{:S(2)}) copy-start(s32[128,2]{0,1:T(2,128)} %param.11) | copy-start | bytes 3076
  10.5 13.1 %copy-start = (s32[32]{0:T(128)S(1)}, s32[32]{0:T(128)}, u32[]{:S(2)}) copy-start(s32[32]{0:T(128)} %new_place_ref.1) | copy-start | bytes 388
  10.5 14.0 %copy-start.2 = (bf16[128,2]{0,1:T(2,128)(2,1)S(1)}, bf16[128,2]{0,1:T(2,128)(2,1)}, u32[]{:S(2)}) copy-start(bf16[128,2]{0,1:T(2,128)(2,1)} %param.12) | copy-start | bytes 1540
  10.5 14.1 %copy-start.3 = (bf16[128,2048]{1,0:T(8,128)(2,1)S(1)}, bf16[128,2048]{1,0:T(8,128)(2,1)}, u32[]{:S(2)}) copy-start(bf16[128,2048]{1,0:T(8,128)(2,1)} %param.10) | copy-start | bytes 1572868
  10.5 14.1 %copy-start.4 = (bf16[128,2048]{1,0:T(8,128)(2,1)S(1)}, bf16[128,2048]{1,0:T(8,128)(2,1)}, u32[]{:S(2)}) copy-start(bf16[128,2048]{1,0:T(8,128)(2,1)} %param.9) | copy-start | bytes 1572868
  10.5 43.0 %all-to-all-start = ((bf16[32,3,8,768]{3,2,1,0:T(8,128)(2,1)}), bf16[32,3,8,768]{3,2,1,0:T(8,128)(2,1)S(1)}, u32[]{:S(2)}, u32[]{:S(2)}) async-start(bf16[32,3,8,768]{3,2,1,0:T(8,128)(2,1)} %copy.62), calls=%async_computation | async-start | bytes 2359296 | tf_op jit(solution)/shard_map/all_to_all | solution.py:260
  22.2 133.5 %all-gather.2.cloned.1.call-start = ((), (), s32[]{:S(2)}) async-start(), calls=%async_computation.6 | async-start | bytes 10616832 | tf_op jit(solution)/shard_map/all_gather | solution.py:298
  54.6 173.2 %reduce-scatter.2.cloned.1.call-start = ((), (), s32[]{:S(2)}) async-start(), calls=%async_computation.7 | async-start | bytes 10616832 | tf_op jit(solution)/shard_map/reduce_scatter | solution.py:307
  181.8 57.1 %all-to-all-start.2 = ((bf16[32,16,2176]{2,1,0:T(8,128)(2,1)}), bf16[32,16,2176]{2,1,0:T(8,128)(2,1)S(1)}, u32[]{:S(2)}, u32[]{:S(2)}) async-start(bf16[32,16,2176]{2,1,0:T(8,128)(2,1)} %bitcast.38), calls=%async_computation.3 | async-start | bytes 4456448 | tf_op jit(solution)/shard_map/all_to_all | solution.py:310
  283.3 35.0 %all-to-all-start.4 = ((bf16[32,3,8,768]{3,2,1,0:T(8,128)(2,1)}), bf16[32,3,8,768]{3,2,1,0:T(8,128)(2,1)S(1)}, u32[]{:S(2)}, u32[]{:S(2)}) async-start(bf16[32,3,8,768]{3,2,1,0:T(8,128)(2,1)} %get-tuple-element.22), calls=%async_computation.5 | async-start | bytes 2359296 | tf_op jit(solution)/shard_map/all_to_all | solution.py:330
Sparse Core Ops, SparseCore 0:
  54.7 52.5 all-gather.1
  173.8 53.9 reduce-scatter.1

commit v7 on v6

--- a/solution.py
+++ b/solution.py
@@ -32,15 +32,16 @@
     up_w_ref,
     down_w_ref,
     dw_ref,
-    units_ref,
-    gate_ref,
+    part_ref,
     first_ref,
     second_ref,
     u_ref,
+    units_ref,
 ):
     step = pl.program_id(0)
     rows, hidden = u_ref.shape
-    part = 128
+    span_rows = 128
+    width = part_ref.shape[1] - lane_count
     products = ((first_ref, x_ref, gate_w_ref), (second_ref, x_ref, up_w_ref), (u_ref, y_ref, down_w_ref))
 
     @pl.when(step == 0)
@@ -59,8 +60,8 @@
 
     @pl.when(step == steps - 1)
     def _():
-        for start in range(0, rows, part):
-            span = pl.ds(start, part)
+        for start in range(0, rows, span_rows):
+            span = pl.ds(start, span_rows)
             weighted = u_ref[span]
             first_pre = first_ref[span]
             second_pre = second_ref[span]
@@ -72,7 +73,9 @@
             units_ref[span, :hidden] = grad_first.astype(jnp.bfloat16)
             units_ref[span, hidden : 2 * hidden] = (weighted * gated).astype(jnp.bfloat16)
             units_ref[span, 2 * hidden :] = activated.astype(jnp.bfloat16)
-            gate_ref[span] = jnp.broadcast_to(total, (part, lane_count)).astype(jnp.bfloat16)
+            part_ref[span, width:] = jnp.broadcast_to(total, (span_rows, lane_count)).astype(
+                jnp.bfloat16
+            )
 
     @pl.when(step >= steps)
     def _():
@@ -84,16 +87,25 @@
         dw_ref[2] = jnp.dot(
             flat_rows(y_ref).T, units_ref[:, 2 * hidden :], preferred_element_type=jnp.float32
         ).astype(jnp.bfloat16)
-
-
-def weight_block(stacked, matrix, depth, block_of):
-    _, _, rows, hidden = stacked.shape
-    return pl.BlockSpec((depth // rows, 1, rows, hidden), lambda i: (block_of(i), matrix, 0, 0))
-
-
-def unit_and_weight_grads(received, stacked):
+        over_hidden = (((1,), (1,)), ((), ()))
+        gate_w = flat_rows(gate_w_ref)
+        depth = gate_w.shape[0]
+        part_ref[:, pl.ds(pl.multiple_of((step - steps) * depth, depth), depth)] = (
+            lax.dot_general(
+                units_ref[:, :hidden], gate_w, over_hidden, preferred_element_type=jnp.float32
+            )
+            + lax.dot_general(
+                units_ref[:, hidden : 2 * hidden],
+                flat_rows(up_w_ref),
+                over_hidden,
+                preferred_element_type=jnp.float32,
+            )
+        ).astype(jnp.bfloat16)
+
+
+def expert_rows(received, stacked):
     sources, _, capacity, width = received.shape
-    hidden = stacked.shape[3]
+    _, _, stored_rows, hidden = stacked.shape
     rows = sources * capacity
     depth = 512
     steps = width // depth
@@ -103,76 +115,38 @@
             (sources, 1, capacity, depth), lambda i: (0, which, 0, lax.rem(i, steps))
         )
 
+    def weight_block(matrix, block_of):
+        return pl.BlockSpec(
+            (depth // stored_rows, 1, stored_rows, hidden), lambda i: (block_of(i), matrix, 0, 0)
+        )
+
     return pl.pallas_call(
         lambda *refs: grad_kernel(steps, *refs),
         grid=(2 * steps,),
-        in_specs=[row_block(0), row_block(1)]
-        + [weight_block(stacked, c, depth, lambda i: jnp.minimum(i, steps - 1)) for c in range(3)],
+        in_specs=[
+            row_block(0),
+            row_block(1),
+            weight_block(0, lambda i: lax.rem(i, steps)),
+            weight_block(1, lambda i: lax.rem(i, steps)),
+            weight_block(2, lambda i: jnp.minimum(i, steps - 1)),
+        ],
         out_specs=[
             pl.BlockSpec((3, depth, hidden), lambda i: (0, jnp.maximum(i - steps, 0), 0)),
-            whole((rows, 3 * hidden)),
-            whole((rows, lane_count)),
+            whole((rows, width + lane_count)),
         ],
         out_shape=[
             jax.ShapeDtypeStruct((3, width, hidden), jnp.bfloat16),
-            jax.ShapeDtypeStruct((rows, 3 * hidden), jnp.bfloat16),
-            jax.ShapeDtypeStruct((rows, lane_count), jnp.bfloat16),
-        ],
-        scratch_shapes=[pltpu.VMEM((rows, hidden), jnp.float32)] * 3,
+            jax.ShapeDtypeStruct((rows, width + lane_count), jnp.bfloat16),
+        ],
+        scratch_shapes=[pltpu.VMEM((rows, hidden), jnp.float32)] * 3
+        + [pltpu.VMEM((rows, 3 * hidden), jnp.bfloat16)],
         compiler_params=pltpu.CompilerParams(vmem_limit_bytes=vmem_bytes),
         cost_estimate=pl.CostEstimate(
-            flops=12 * rows * width * hidden,
-            bytes_accessed=30_000_000,
+            flops=16 * rows * width * hidden,
+            bytes_accessed=36_000_000,
             transcendentals=rows * hidden,
         ),
     )(received, received, stacked, stacked, stacked)
-
-
-def part_kernel(units_ref, gate_w_ref, up_w_ref, gate_ref, out_ref):
-    step = pl.program_id(0)
-    hidden = gate_w_ref.shape[-1]
-    over_hidden = (((1,), (1,)), ((), ()))
-
-    @pl.when(step == 0)
-    def _():
-        out_ref[:, pl.ds(out_ref.shape[1] - lane_count, lane_count)] = gate_ref[...]
-
-    gate_w = flat_rows(gate_w_ref)
-    depth = gate_w.shape[0]
-    out_ref[:, pl.ds(pl.multiple_of(step * depth, depth), depth)] = (
-        lax.dot_general(
-            units_ref[:, :hidden], gate_w, over_hidden, preferred_element_type=jnp.float32
-        )
-        + lax.dot_general(
-            units_ref[:, hidden : 2 * hidden],
-            flat_rows(up_w_ref),
-            over_hidden,
-            preferred_element_type=jnp.float32,
-        )
-    ).astype(jnp.bfloat16)
-
-
-def input_parts(units, stacked, gate_part):
-    rows = units.shape[0]
-    hidden = stacked.shape[3]
-    width = stacked.shape[0] * stacked.shape[2]
-    depth = 512
-    return pl.pallas_call(
-        part_kernel,
-        grid=(width // depth,),
-        in_specs=[
-            whole((rows, 3 * hidden)),
-            weight_block(stacked, 0, depth, lambda i: i),
-            weight_block(stacked, 1, depth, lambda i: i),
-            whole((rows, lane_count)),
-        ],
-        out_specs=whole((rows, width + lane_count)),
-        out_shape=jax.ShapeDtypeStruct((rows, width + lane_count), jnp.bfloat16),
-        compiler_params=pltpu.CompilerParams(vmem_limit_bytes=vmem_bytes),
-        cost_estimate=pl.CostEstimate(
-            flops=4 * rows * width * hidden, bytes_accessed=10_000_000, transcendentals=0
-        ),
-    )(units, stacked, stacked, gate_part)
 
 
 def adam_kernel(
@@ -303,10 +277,9 @@
     received = lax.all_to_all(packed, "expert", split_axis=0, concat_axis=0, tiled=True).reshape(
         slot_count, 2, capacity, feature_width
     )
-    weight_grads, units, gate_part = unit_and_weight_grads(received, stacked)
+    weight_grads, input_part = expert_rows(received, stacked)
     summed = lax.psum_scatter(weight_grads, "dp", scatter_dimension=1, tiled=True)
     pieces = jnp.transpose(summed.reshape(3, slot_count, block_rows, hidden), (1, 0, 2, 3))
-    input_part = input_parts(units, stacked, gate_part)
     back = lax.all_to_all(
         input_part.reshape(slot_count, capacity, feature_width + lane_count),
         "expert",

time: 327 us -> 326 us (level)
  Pallas kernels: 31.9 us -> 26.6 us
    all_to_all x1, waiting for transfers between devices: 9.79 us -> 1.72 us  [body(): lax.all_to_all(input_part.reshape(slot_count, capacity, feature_width + l...]
    reduce_scatter x1, waiting for transfers between devices: 41.1 us -> 49.2 us  [body(): lax.psum_scatter(weight_grads, 'dp', scatter_dimension=1, tiled=True)]
    pallas_call x2 -> x1, Pallas kernels: 26.1 us -> 20.8 us  [expert_rows(): pl.pallas_call(lambda *refs: grad_kernel(steps, *refs), grid=(2 * steps,)...]
  transfers between devices with their start and end apart: 5 -> 5, of which waited for: 4 -> 4; matrix products, arithmetic and copies ran while one was open for 4% -> 4% of each run, Pallas kernels for 2% -> 0%
where the time goes in v7:
time: 326 us; the launch traced here: 325 us
  blocking collectives  143 us (44%)
  waiting for transfers between devices  102 us (31%)
  Pallas kernels  26.6 us (8%)
  starting transfers between devices  21 us (6%)
  between operations  14.2 us (4%)
  local copies, waits for them, and re-layouts  7.93 us (2%)
  matrix products  7.74 us (2%)
    all_to_all x1, blocking collectives, body(): lax.all_to_all(packed, 'expert', split_axis=0, concat_axis=0, tiled=True)  101 us
    reduce_scatter x1, waiting for transfers between devices, body(): lax.psum_scatter(weight_grads, 'dp', scatter_dimension=1, tiled=True)  49.2 us
    all_to_all x1, blocking collectives, body(): lax.all_to_all(pieces, 'expert', split_axis=0, concat_axis=0, tiled=True)  41.7 us
    all_to_all x1, waiting for transfers between devices, body(): lax.all_to_all(leaving, 'expert', split_axis=0, concat_axis=0, tiled=True)  25.9 us
    all_to_all x1, waiting for transfers between devices, body(): lax.all_to_all(outgoing, 'expert', split_axis=0, concat_axis=0, tiled=True)  25.3 us
    pallas_call x1, Pallas kernels, expert_rows(): pl.pallas_call(lambda *refs: grad_kernel(steps, *refs), grid=(2 * steps,)...  20.8 us
    all_to_all x1, starting transfers between devices, body(): lax.all_to_all(outgoing, 'expert', split_axis=0, concat_axis=0, tiled=True)  11.6 us
  transfers between devices with their start and end apart: 5, of which 4 were waited for; matrix products, arithmetic and copies ran while one was open for 4% of the time, Pallas kernels for 0%

profile of v7, /device:TPU:2, one launch (start us, length us, event | category | flops | bytes accessed | tf_op | source)
XLA Modules:
  0.0 325.1 jit_solution(6386497690004360815)
XLA Ops:
  7.2 1.7 convolution_convert_fusion.2
  8.8 1.7 copy.62
  10.5 0.0 copy-start.1
  10.5 0.0 copy-start
  10.5 0.0 copy-start.2
  10.5 0.0 copy-start.3
  10.5 0.0 copy-start.4
  10.5 11.6 %all-to-all-start = ((bf16[32,3,8,768]{3,2,1,0:T(8,128)(2,1)}), bf16[32,3,8,768]{3,2,1,0:T(8,128)(2,1)S(1)}, u32[]{:S(2)}, u32[]{:S(2)}) async-start(bf16[32,3,8,768]{3,2,1,0:T(8,128)(2,1)} %copy.62), calls=%async_computation | async-start | bytes 2359296 | tf_op jit(solution)/shard_map/all_to_all | solution.py:234
  22.2 0.0 all-gather.2.cloned.1.call-start
  22.2 0.0 copy-done.1
  22.2 0.1 copy.56
  22.3 0.1 eq.131
  22.5 0.1 eq.120
  22.6 0.6 reduce-window.6
  23.2 0.2 slice_reduce_fusion
  23.5 0.1 broadcast_add_fusion.1
  23.6 0.0 copy-done
  23.6 0.1 fusion.26
  23.7 0.1 reduce_window_sum.26
  23.7 0.2 fusion.23
  23.9 0.1 and_select_fusion
  24.0 0.1 fusion.25
  24.1 0.1 select_reduce_fusion
  24.2 0.1 add.41
  24.4 0.1 copy.63
  24.5 0.1 copy.64
  24.5 0.0 copy-done.2
  24.6 0.0 copy-done.3
  24.6 0.0 copy-done.4
  24.6 3.6 %convolution_convert_fusion = bf16[1024,2048]{1,0:T(8,128)(2,1)} fusion(bf16[128,2048]{1,0:T(8,128)(2,1)S(1)} %copy-done.3, bf16[128,2048]{1,0:T(8,128)(2,1)S(1)} %copy-done.4, s32[256]{0:T(256)S(1)} %bitcast.46, s32[256]{0:T(256)S(1)} %bitcast.45, bf16[256]{0:T(256)(128)(2,1)S(1)} %get-tuple-element.46, bf16[256]{0:T(256)(128)(2,1)S(1)} %get-tuple-element.45), kind=kOutput, calls=%fused_computation | convolution fusion | flops 1080033280 | bytes 5245952 | tf_op jit(solution)/shard_map/tb,td->bd/dot_general | solution.py:262
  28.3 25.3 %all-to-all-done = bf16[32,3,8,768]{3,2,1,0:T(8,128)(2,1)S(1)} async-done(((bf16[32,3,8,768]{3,2,1,0:T(8,128)(2,1)}), bf16[32,3,8,768]{3,2,1,0:T(8,128)(2,1)S(1)}, u32[]{:S(2)}, u32[]{:S(2)}) %all-to-all-start) | async-done | bytes 1179680 | tf_op jit(solution)/shard_map/all_to_all | solution.py:234
  53.5 1.1 copy.79
  54.6 0.0 all-gather.2.cloned.1.call-update
  54.6 0.0 reduce-scatter.2.cloned.1.call-start
  54.7 101.0 %all_to_all.25 = bf16[32,32,2048]{2,1,0:T(8,128)(2,1)} all-to-all(bf16[32,32,2048]{2,1,0:T(8,128)(2,1)} %bitcast.37), channel_id=1, replica_groups=mesh['dp'=8,'expert'=32] {'expert'}, dimensions={0} | all-to-all | bytes 8388608 | tf_op jit(solution)/shard_map/all_to_all | solution.py:277
  155.7 0.0 all-gather.2.cloned.1.call-done.refs_2_.refs_3_.refs_4_
  155.7 20.8 %shard_map.128 = (bf16[3,2048,768]{2,1,0:T(8,128)(2,1)}, bf16[512,2176]{1,0:T(8,128)(2,1)}) custom-call(bf16[32,2,16,2048]{3,2,1,0:T(8,128)(2,1)} %bitcast.38, bf16[32,2,16,2048]{3,2,1,0:T(8,128)(2,1)} %bitcast.39, bf16[8,3,256,768]{3,2,1,0:T(8,128)(2,1)} %all-gather.2.cloned.1.call-done.refs_2_.refs_3_.refs_4_, ...), custom_call_target="tpu_custom_call" | custom-call | flops 12884901888 | bytes 36000000 | tf_op jit(solution)/shard_map/pallas_call | solution.py:123
  176.5 0.0 reduce-scatter.2.cloned.1.call-update
  176.5 4.9 %all-to-all-start.2 = ((bf16[32,16,2176]{2,1,0:T(8,128)(2,1)}), bf16[32,16,2176]{2,1,0:T(8,128)(2,1)S(1)}, u32[]{:S(2)}, u32[]{:S(2)}) async-start(bf16[32,16,2176]{2,1,0:T(8,128)(2,1)} %bitcast.42), calls=%async_computation.3 | async-start | bytes 4456448 | tf_op jit(solution)/shard_map/all_to_all | solution.py:283
  181.4 49.2 %reduce-scatter.2.cloned.1.call-done = bf16[3,256,768]{2,1,0:T(8,128)(2,1)} async-done(((bf16[3,2048,768]{2,1,0:T(8,128)(2,1)}), bf16[3,256,768]{2,1,0:T(8,128)(2,1)}) %reduce-scatter.2.cloned.1.call-update) | async-done | bytes 1179664 | tf_op jit(solution)/shard_map/reduce_scatter | solution.py:281
  230.6 1.3 copy_bitcast_fusion.1
  232.0 1.7 all-to-all-done.2
  233.7 41.7 %all_to_all.26.returned_ref = bf16[32,3,8,768]{3,2,1,0:T(8,128)(2,1)} all-to-all(bf16[32,3,8,768]{3,2,1,0:T(8,128)(2,1)S(1)} %copy_bitcast_fusion.1), channel_id=1, replica_groups=mesh['dp'=8,'expert'=32] {'expert'}, dimensions={0} | all-to-all | bytes 2359296 | tf_op jit(solution)/shard_map/all_to_all | solution.py:299
  275.4 5.8 %shard_map.129 = (f32[3,20,8,768]{3,2,1,0:T(8,128)}, f32[3,20,8,768]{3,2,1,0:T(8,128)}, bf16[32,3,8,768]{3,2,1,0:T(8,128)(2,1)}) custom-call(s32[32]{0:T(128)} %new_place_ref.1, s32[20]{0:T(128)} %old_place_ref.1, bf16[32,3,8,768]{3,2,1,0:T(8,128)(2,1)} %all_to_all.26.returned_ref, bf16[3,20,8,768]{3,2,1,0:T(8,128)(2,1)} %stored_ref.1, ...), custom_call_target="tpu_custom_call" | custom-call | flops 7372800 | bytes 9000000 | tf_op jit(solution)/shard_map/pallas_call | solution.py:193
  281.2 4.4 %all-to-all-start.4 = ((bf16[32,3,8,768]{3,2,1,0:T(8,128)(2,1)}), bf16[32,3,8,768]{3,2,1,0:T(8,128)(2,1)S(1)}, u32[]{:S(2)}, u32[]{:S(2)}) async-start(bf16[32,3,8,768]{3,2,1,0:T(8,128)(2,1)} %get-tuple-element.20), calls=%async_computation.5 | async-start | bytes 2359296 | tf_op jit(solution)/shard_map/all_to_all | solution.py:303
  285.5 0.1 copy.67
  285.7 0.1 add.39
  285.8 0.1 copy.59
  285.9 0.8 fusion.13
  286.6 0.3 convolution_reduce_fusion
  286.9 0.1 reshape_squeeze.3
  287.1 0.6 divide_convert_fusion
  287.7 1.3 copy.69
  289.1 2.2 convolution_convert_fusion.1
  291.2 25.9 %all-to-all-done.4 = bf16[32,3,8,768]{3,2,1,0:T(8,128)(2,1)S(1)} async-done(((bf16[32,3,8,768]{3,2,1,0:T(8,128)(2,1)}), bf16[32,3,8,768]{3,2,1,0:T(8,128)(2,1)S(1)}, u32[]{:S(2)}, u32[]{:S(2)}) %all-to-all-start.4) | async-done | bytes 1179680 | tf_op jit(solution)/shard_map/all_to_all | solution.py:303
  317.1 1.1 copy_bitcast_fusion
  (10 shorter events, 0.1 us)
Async XLA Ops:
  10.5 11.7 %copy-start.1 = (s32[128,2]{0,1:T(2,128)S(1)}, s32[128,2]{0,1:T(2,128)}, u32[]{:S(2)}) copy-start(s32[128,2]{0,1:T(2,128)} %param.11) | copy-start | bytes 3076
  10.5 13.1 %copy-start = (s32[32]{0:T(128)S(1)}, s32[32]{0:T(128)}, u32[]{:S(2)}) copy-start(s32[32]{0:T(128)} %new_place_ref.1) | copy-start | bytes 388
  10.5 14.0 %copy-start.2 = (bf16[128,2]{0,1:T(2,128)(2,1)S(1)}, bf16[128,2]{0,1:T(2,128)(2,1)}, u32[]{:S(2)}) copy-start(bf16[128,2]{0,1:T(2,128)(2,1)} %param.12) | copy-start | bytes 1540
  10.5 14.1 %copy-start.3 = (bf16[128,2048]{1,0:T(8,128)(2,1)S(1)}, bf16[128,2048]{1,0:T(8,128)(2,1)}, u32[]{:S(2)}) copy-start(bf16[128,2048]{1,0:T(8,128)(2,1)} %param.10) | copy-start | bytes 1572868
  10.5 14.1 %copy-start.4 = (bf16[128,2048]{1,0:T(8,128)(2,1)S(1)}, bf16[128,2048]{1,0:T(8,128)(2,1)}, u32[]{:S(2)}) copy-start(bf16[128,2048]{1,0:T(8,128)(2,1)} %param.9) | copy-start | bytes 1572868
  10.5 43.0 %all-to-all-start = ((bf16[32,3,8,768]{3,2,1,0:T(8,128)(2,1)}), bf16[32,3,8,768]{3,2,1,0:T(8,128)(2,1)S(1)}, u32[]{:S(2)}, u32[]{:S(2)}) async-start(bf16[32,3,8,768]{3,2,1,0:T(8,128)(2,1)} %copy.62), calls=%async_computation | async-start | bytes 2359296 | tf_op jit(solution)/shard_map/all_to_all | solution.py:234
  22.2 133.5 %all-gather.2.cloned.1.call-start = ((), (), s32[]{:S(2)}) async-start(), calls=%async_computation.6 | async-start | bytes 10616832 | tf_op jit(solution)/shard_map/all_gather | solution.py:272
  54.6 176.0 %reduce-scatter.2.cloned.1.call-start = ((), (), s32[]{:S(2)}) async-start(), calls=%async_computation.7 | async-start | bytes 10616832 | tf_op jit(solution)/shard_map/reduce_scatter | solution.py:281
  176.5 57.2 %all-to-all-start.2 = ((bf16[32,16,2176]{2,1,0:T(8,128)(2,1)}), bf16[32,16,2176]{2,1,0:T(8,128)(2,1)S(1)}, u32[]{:S(2)}, u32[]{:S(2)}) async-start(bf16[32,16,2176]{2,1,0:T(8,128)(2,1)} %bitcast.42), calls=%async_computation.3 | async-start | bytes 4456448 | tf_op jit(solution)/shard_map/all_to_all | solution.py:283
  281.2 36.0 %all-to-all-start.4 = ((bf16[32,3,8,768]{3,2,1,0:T(8,128)(2,1)}), bf16[32,3,8,768]{3,2,1,0:T(8,128)(2,1)S(1)}, u32[]{:S(2)}, u32[]{:S(2)}) async-start(bf16[32,3,8,768]{3,2,1,0:T(8,128)(2,1)} %get-tuple-element.20), calls=%async_computation.5 | async-start | bytes 2359296 | tf_op jit(solution)/shard_map/all_to_all | solution.py:303
Sparse Core Ops, SparseCore 0:
  54.7 52.5 all-gather.1
  176.6 53.9 reduce-scatter.1

commit v8 on v7

--- a/solution.py
+++ b/solution.py
@@ -204,11 +204,37 @@
             pltpu.SMEM((experts,), jnp.int32),
             pltpu.VMEM((experts, rows, hidden), jnp.float32),
         ],
-        compiler_params=pltpu.CompilerParams(vmem_limit_bytes=vmem_bytes),
+        compiler_params=pltpu.CompilerParams(vmem_limit_bytes=vmem_bytes // 3),
         cost_estimate=pl.CostEstimate(
             flops=20 * first.size, bytes_accessed=9_000_000, transcendentals=2 * first.size
         ),
     )(new_place, old_place, returned, stored, first, second)
+
+
+def slot_kernel(new_place_ref, old_place_ref, stored_ref, leaving_ref, row_ref):
+    slots = leaving_ref.shape[0]
+    for row in range(stored_ref.shape[1]):
+        row_ref[old_place_ref[row]] = row
+    for slot in range(slots):
+        row = row_ref[new_place_ref[pl.program_id(0) * slots + slot]]
+        leaving_ref[slot] = stored_ref[:, row]
+
+
+def slot_rows(new_place, old_place, stored):
+    slots = new_place.shape[0]
+    matrices, experts, rows, hidden = stored.shape
+    block = slots // 4
+    scalars = pl.BlockSpec(memory_space=pltpu.SMEM)
+    return pl.pallas_call(
+        slot_kernel,
+        grid=(slots // block,),
+        in_specs=[scalars, scalars, whole(stored.shape)],
+        out_specs=pl.BlockSpec((block, matrices, rows, hidden), lambda i: (i, 0, 0, 0)),
+        out_shape=jax.ShapeDtypeStruct((slots, matrices, rows, hidden), jnp.bfloat16),
+        scratch_shapes=[pltpu.SMEM((experts,), jnp.int32)],
+        compiler_params=pltpu.CompilerParams(vmem_limit_bytes=vmem_bytes),
+        cost_estimate=pl.CostEstimate(flops=0, bytes_accessed=2_000_000, transcendentals=0),
+    )(new_place, old_place, stored)
 
 
 def body(
@@ -226,11 +252,8 @@
     expert_ids = jnp.arange(expert_count, dtype=jnp.int32)
     slot_ids = jnp.arange(slot_count, dtype=jnp.int32)
     place_hot = (new_place[:, None] == expert_ids[None, :]).astype(jnp.int32)
-    slot_state = (new_place[:, None] == old_place[None, :]).astype(jnp.bfloat16)
-
-    outgoing = jnp.einsum(
-        "se,cerh->scrh", slot_state, weights, preferred_element_type=jnp.float32
-    ).astype(jnp.bfloat16)
+
+    outgoing = slot_rows(new_place, old_place, weights)
     arrived = lax.all_to_all(outgoing, "expert", split_axis=0, concat_axis=0, tiled=True)
 
     replica_count = jnp.sum(place_hot, axis=0)

time: 326 us -> 324 us (level)
  no operation moved by 1% of the time
where the time goes in v8:
time: 324 us
  blocking collectives  143 us (44%)
  waiting for transfers between devices  103 us (32%)
  Pallas kernels  27.1 us (8%)
  starting transfers between devices  21.1 us (7%)
  between operations  14.3 us (4%)
  matrix products  7.53 us (2%)
  local copies, waits for them, and re-layouts  6.9 us (2%)
    all_to_all x1, blocking collectives, body(): lax.all_to_all(packed, 'expert', split_axis=0, concat_axis=0, tiled=True)  101 us
    reduce_scatter x1, waiting for transfers between devices, body(): lax.psum_scatter(weight_grads, 'dp', scatter_dimension=1, tiled=True)  49.1 us
    all_to_all x1, blocking collectives, body(): lax.all_to_all(pieces, 'expert', split_axis=0, concat_axis=0, tiled=True)  41.7 us
    all_to_all x1, waiting for transfers between devices, body(): lax.all_to_all(leaving, 'expert', split_axis=0, concat_axis=0, tiled=True)  26.3 us
    all_to_all x1, waiting for transfers between devices, body(): lax.all_to_all(outgoing, 'expert', split_axis=0, concat_axis=0, tiled=True)  25.4 us
    pallas_call x1, Pallas kernels, expert_rows(): pl.pallas_call(lambda *refs: grad_kernel(steps, *refs), grid=(2 * steps,)...  20.8 us
    all_to_all x1, starting transfers between devices, body(): lax.all_to_all(outgoing, 'expert', split_axis=0, concat_axis=0, tiled=True)  11.6 us
  transfers between devices with their start and end apart: 5, of which 4 were waited for; matrix products, arithmetic and copies ran while one was open for 4% of the time, Pallas kernels for 0%

profile of v8, /device:TPU:2, one launch (start us, length us, event | category | flops | bytes accessed | tf_op | source)
XLA Modules:
  0.0 323.7 jit_solution(2540801478012058401)
XLA Ops:
  7.2 2.8 shard_map.128
  10.0 0.0 copy-start.5
  10.0 0.0 copy-start.3
  10.0 0.0 copy-start.6
  10.0 0.0 copy-start.7
  10.0 0.0 copy-start.8
  10.0 11.6 %all-to-all-start = ((bf16[32,3,8,768]{3,2,1,0:T(8,128)(2,1)}), bf16[32,3,8,768]{3,2,1,0:T(8,128)(2,1)S(1)}, u32[]{:S(2)}, u32[]{:S(2)}) async-start(bf16[32,3,8,768]{3,2,1,0:T(8,128)(2,1)} %shard_map.128), calls=%async_computation | async-start | bytes 2359296 | tf_op jit(solution)/shard_map/all_to_all | solution.py:257
  21.6 0.0 all-gather.2.cloned.1.call-start
  21.7 0.0 copy-done.5
  21.7 0.1 copy.46
  21.8 0.1 eq.120
  21.9 0.1 eq.109
  22.1 0.6 reduce-window.6
  22.7 0.2 slice_reduce_fusion
  22.9 0.1 broadcast_add_fusion.1
  23.1 0.0 copy-done.3
  23.1 0.1 fusion.25
  23.1 0.1 reduce_window_sum.26
  23.2 0.2 fusion.22
  23.4 0.1 and_select_fusion
  23.5 0.1 fusion.24
  23.6 0.1 select_reduce_fusion
  23.7 0.1 add.41
  23.8 0.1 copy.50
  23.9 0.1 copy.51
  24.0 0.0 copy-done.6
  24.1 0.0 copy-done.7
  24.1 0.0 copy-done.8
  24.1 3.5 %convolution_convert_fusion = bf16[1024,2048]{1,0:T(8,128)(2,1)} fusion(bf16[128,2048]{1,0:T(8,128)(2,1)S(1)} %copy-done.7, bf16[128,2048]{1,0:T(8,128)(2,1)S(1)} %copy-done.8, s32[256]{0:T(256)S(1)} %bitcast.39, s32[256]{0:T(256)S(1)} %bitcast.38, bf16[256]{0:T(256)(128)(2,1)S(1)} %get-tuple-element.46, bf16[256]{0:T(256)(128)(2,1)S(1)} %get-tuple-element.45), kind=kOutput, calls=%fused_computation | convolution fusion | flops 1080033280 | bytes 5245952 | tf_op jit(solution)/shard_map/tb,td->bd/dot_general | solution.py:285
  27.6 25.4 %all-to-all-done = bf16[32,3,8,768]{3,2,1,0:T(8,128)(2,1)S(1)} async-done(((bf16[32,3,8,768]{3,2,1,0:T(8,128)(2,1)}), bf16[32,3,8,768]{3,2,1,0:T(8,128)(2,1)S(1)}, u32[]{:S(2)}, u32[]{:S(2)}) %all-to-all-start) | async-done | bytes 1179680 | tf_op jit(solution)/shard_map/all_to_all | solution.py:257
  53.0 1.1 copy_bitcast_fusion.2
  54.1 0.0 all-gather.2.cloned.1.call-update
  54.1 0.0 reduce-scatter.2.cloned.1.call-start
  54.1 101.0 %all_to_all.25 = bf16[32,32,2048]{2,1,0:T(8,128)(2,1)} all-to-all(bf16[32,32,2048]{2,1,0:T(8,128)(2,1)} %bitcast.33), channel_id=1, replica_groups=mesh['dp'=8,'expert'=32] {'expert'}, dimensions={0} | all-to-all | bytes 8388608 | tf_op jit(solution)/shard_map/all_to_all | solution.py:300
  155.1 0.0 all-gather.2.cloned.1.call-done.refs_2_.refs_3_.refs_4_
  155.1 20.8 %shard_map.129 = (bf16[3,2048,768]{2,1,0:T(8,128)(2,1)}, bf16[512,2176]{1,0:T(8,128)(2,1)}) custom-call(bf16[32,2,16,2048]{3,2,1,0:T(8,128)(2,1)} %bitcast.34, bf16[32,2,16,2048]{3,2,1,0:T(8,128)(2,1)} %bitcast.35, bf16[8,3,256,768]{3,2,1,0:T(8,128)(2,1)} %all-gather.2.cloned.1.call-done.refs_2_.refs_3_.refs_4_, ...), custom_call_target="tpu_custom_call" | custom-call | flops 12884901888 | bytes 36000000 | tf_op jit(solution)/shard_map/pallas_call | solution.py:123
  176.0 0.0 reduce-scatter.2.cloned.1.call-update
  176.0 5.0 %all-to-all-start.2 = ((bf16[32,16,2176]{2,1,0:T(8,128)(2,1)}), bf16[32,16,2176]{2,1,0:T(8,128)(2,1)}, u32[]{:S(2)}, u32[]{:S(2)}) async-start(bf16[32,16,2176]{2,1,0:T(8,128)(2,1)} %bitcast.9), calls=%async_computation.3 | async-start | bytes 4456448 | tf_op jit(solution)/shard_map/all_to_all | solution.py:306
  181.0 49.1 %reduce-scatter.2.cloned.1.call-done = bf16[3,256,768]{2,1,0:T(8,128)(2,1)} async-done(((bf16[3,2048,768]{2,1,0:T(8,128)(2,1)}), bf16[3,256,768]{2,1,0:T(8,128)(2,1)}) %reduce-scatter.2.cloned.1.call-update) | async-done | bytes 1179664 | tf_op jit(solution)/shard_map/reduce_scatter | solution.py:304
  230.1 1.3 copy_bitcast_fusion.1
  231.4 0.0 copy-start
  231.4 0.0 copy-start.1
  231.4 0.0 copy-start.4
  231.5 1.8 all-to-all-done.2
  233.2 41.7 %all_to_all.26.returned_ref = bf16[32,3,8,768]{3,2,1,0:T(8,128)(2,1)S(1)} all-to-all(bf16[32,3,8,768]{3,2,1,0:T(8,128)(2,1)S(1)} %copy_bitcast_fusion.1), channel_id=1, replica_groups=mesh['dp'=8,'expert'=32] {'expert'}, dimensions={0} | all-to-all | bytes 2359296 | tf_op jit(solution)/shard_map/all_to_all | solution.py:322
  274.9 0.0 copy-done
  274.9 0.0 copy-done.1
  274.9 0.0 copy-done.4
  275.0 0.0 copy-start.2
  275.0 1.4 copy-done.2
  276.3 3.5 %shard_map.130 = (f32[3,20,8,768]{3,2,1,0:T(8,128)}, f32[3,20,8,768]{3,2,1,0:T(8,128)}, bf16[32,3,8,768]{3,2,1,0:T(8,128)(2,1)}) custom-call(s32[32]{0:T(128)S(1)} %copy-done.3, s32[20]{0:T(128)S(1)} %copy-done.4, bf16[32,3,8,768]{3,2,1,0:T(8,128)(2,1)S(1)} %all_to_all.26.returned_ref, bf16[3,20,8,768]{3,2,1,0:T(8,128)(2,1)S(1)} %copy-done, ...), custom_call_target="tpu_custom_call" | custom-call | flops 7372800 | bytes 9000000 | tf_op jit(solution)/shard_map/pallas_call | solution.py:193
  279.9 4.4 %all-to-all-start.4 = ((bf16[32,3,8,768]{3,2,1,0:T(8,128)(2,1)}), bf16[32,3,8,768]{3,2,1,0:T(8,128)(2,1)S(1)}, u32[]{:S(2)}, u32[]{:S(2)}) async-start(bf16[32,3,8,768]{3,2,1,0:T(8,128)(2,1)} %get-tuple-element.20), calls=%async_computation.5 | async-start | bytes 2359296 | tf_op jit(solution)/shard_map/all_to_all | solution.py:326
  284.2 0.1 copy.54
  284.3 0.1 add.39
  284.5 0.1 copy.49
  284.5 0.1 fusion.12
  284.7 1.2 convolution_reduce_fusion
  285.9 0.1 reshape_squeeze.3
  286.0 0.6 copy.56
  286.6 2.9 convolution_convert_fusion.1
  289.5 26.3 %all-to-all-done.4 = bf16[32,3,8,768]{3,2,1,0:T(8,128)(2,1)S(1)} async-done(((bf16[32,3,8,768]{3,2,1,0:T(8,128)(2,1)}), bf16[32,3,8,768]{3,2,1,0:T(8,128)(2,1)S(1)}, u32[]{:S(2)}, u32[]{:S(2)}) %all-to-all-start.4) | async-done | bytes 1179680 | tf_op jit(solution)/shard_map/all_to_all | solution.py:326
  315.8 1.1 copy_bitcast_fusion
  (11 shorter events, 0.2 us)
Async XLA Ops:
  10.0 11.7 %copy-start.5 = (s32[128,2]{0,1:T(2,128)S(1)}, s32[128,2]{0,1:T(2,128)}, u32[]{:S(2)}) copy-start(s32[128,2]{0,1:T(2,128)} %param.11) | copy-start | bytes 3076
  10.0 13.1 %copy-start.3 = (s32[32]{0:T(128)S(1)}, s32[32]{0:T(128)}, u32[]{:S(2)}) copy-start(s32[32]{0:T(128)} %new_place_ref.3) | copy-start | bytes 388
  10.0 14.0 %copy-start.6 = (bf16[128,2]{0,1:T(2,128)(2,1)S(1)}, bf16[128,2]{0,1:T(2,128)(2,1)}, u32[]{:S(2)}) copy-start(bf16[128,2]{0,1:T(2,128)(2,1)} %param.12) | copy-start | bytes 1540
  10.0 14.1 %copy-start.7 = (bf16[128,2048]{1,0:T(8,128)(2,1)S(1)}, bf16[128,2048]{1,0:T(8,128)(2,1)}, u32[]{:S(2)}) copy-start(bf16[128,2048]{1,0:T(8,128)(2,1)} %param.10) | copy-start | bytes 1572868
  10.0 14.1 %copy-start.8 = (bf16[128,2048]{1,0:T(8,128)(2,1)S(1)}, bf16[128,2048]{1,0:T(8,128)(2,1)}, u32[]{:S(2)}) copy-start(bf16[128,2048]{1,0:T(8,128)(2,1)} %param.9) | copy-start | bytes 1572868
  10.0 43.0 %all-to-all-start = ((bf16[32,3,8,768]{3,2,1,0:T(8,128)(2,1)}), bf16[32,3,8,768]{3,2,1,0:T(8,128)(2,1)S(1)}, u32[]{:S(2)}, u32[]{:S(2)}) async-start(bf16[32,3,8,768]{3,2,1,0:T(8,128)(2,1)} %shard_map.128), calls=%async_computation | async-start | bytes 2359296 | tf_op jit(solution)/shard_map/all_to_all | solution.py:257
  21.6 133.5 %all-gather.2.cloned.1.call-start = ((), (), s32[]{:S(2)}) async-start(), calls=%async_computation.6 | async-start | bytes 10616832 | tf_op jit(solution)/shard_map/all_gather | solution.py:295
  54.1 176.0 %reduce-scatter.2.cloned.1.call-start = ((), (), s32[]{:S(2)}) async-start(), calls=%async_computation.7 | async-start | bytes 10616832 | tf_op jit(solution)/shard_map/reduce_scatter | solution.py:304
  176.0 57.3 %all-to-all-start.2 = ((bf16[32,16,2176]{2,1,0:T(8,128)(2,1)}), bf16[32,16,2176]{2,1,0:T(8,128)(2,1)}, u32[]{:S(2)}, u32[]{:S(2)}) async-start(bf16[32,16,2176]{2,1,0:T(8,128)(2,1)} %bitcast.9), calls=%async_computation.3 | async-start | bytes 4456448 | tf_op jit(solution)/shard_map/all_to_all | solution.py:306
  231.4 43.5 %copy-start = (bf16[3,20,8,768]{3,2,1,0:T(8,128)(2,1)S(1)}, bf16[3,20,8,768]{3,2,1,0:T(8,128)(2,1)}, u32[]{:S(2)}) copy-start(bf16[3,20,8,768]{3,2,1,0:T(8,128)(2,1)} %stored_ref.3) | copy-start | bytes 2211844
  231.4 43.5 %copy-start.1 = (f32[3,20,8,768]{3,2,1,0:T(8,128)S(1)}, f32[3,20,8,768]{3,2,1,0:T(8,128)}, u32[]{:S(2)}) copy-start(f32[3,20,8,768]{3,2,1,0:T(8,128)} %first_ref.1) | copy-start | bytes 4423684
  231.4 43.5 %copy-start.4 = (s32[20]{0:T(128)S(1)}, s32[20]{0:T(128)}, u32[]{:S(2)}) copy-start(s32[20]{0:T(128)} %old_place_ref.3) | copy-start | bytes 244
  275.0 1.4 copy-start.2
  279.9 36.0 %all-to-all-start.4 = ((bf16[32,3,8,768]{3,2,1,0:T(8,128)(2,1)}), bf16[32,3,8,768]{3,2,1,0:T(8,128)(2,1)S(1)}, u32[]{:S(2)}, u32[]{:S(2)}) async-start(bf16[32,3,8,768]{3,2,1,0:T(8,128)(2,1)} %get-tuple-element.20), calls=%async_computation.5 | async-start | bytes 2359296 | tf_op jit(solution)/shard_map/all_to_all | solution.py:326
Sparse Core Ops, SparseCore 0:
  54.2 52.5 all-gather.1
  176.1 53.9 reduce-scatter.1

commit v9 on v8

--- a/solution.py
+++ b/solution.py
@@ -140,7 +140,7 @@
         ],
         scratch_shapes=[pltpu.VMEM((rows, hidden), jnp.float32)] * 3
         + [pltpu.VMEM((rows, 3 * hidden), jnp.bfloat16)],
-        compiler_params=pltpu.CompilerParams(vmem_limit_bytes=vmem_bytes),
+        compiler_params=pltpu.CompilerParams(vmem_limit_bytes=vmem_bytes * 3 // 4),
         cost_estimate=pl.CostEstimate(
             flops=16 * rows * width * hidden,
             bytes_accessed=36_000_000,

time: 324 us -> 326 us (level)
  no operation moved by 1% of the time
where the time goes in v9:
time: 326 us; the launch traced here: 325 us
  blocking collectives  143 us (44%)
  waiting for transfers between devices  102 us (31%)
  Pallas kernels  26.6 us (8%)
  starting transfers between devices  21.1 us (6%)
  between operations  14.3 us (4%)
  local copies, waits for them, and re-layouts  9.09 us (3%)
  matrix products  7.68 us (2%)
    all_to_all x1, blocking collectives, body(): lax.all_to_all(packed, 'expert', split_axis=0, concat_axis=0, tiled=True)  101 us
    reduce_scatter x1, waiting for transfers between devices, body(): lax.psum_scatter(weight_grads, 'dp', scatter_dimension=1, tiled=True)  49.1 us
    all_to_all x1, blocking collectives, body(): lax.all_to_all(pieces, 'expert', split_axis=0, concat_axis=0, tiled=True)  41.7 us
    all_to_all x1, waiting for transfers between devices, body(): lax.all_to_all(leaving, 'expert', split_axis=0, concat_axis=0, tiled=True)  26.3 us
    all_to_all x1, waiting for transfers between devices, body(): lax.all_to_all(outgoing, 'expert', split_axis=0, concat_axis=0, tiled=True)  25.3 us
    pallas_call x1, Pallas kernels, expert_rows(): pl.pallas_call(lambda *refs: grad_kernel(steps, *refs), grid=(2 * steps,)...  20.3 us
    all_to_all x1, starting transfers between devices, body(): lax.all_to_all(outgoing, 'expert', split_axis=0, concat_axis=0, tiled=True)  11.6 us
  transfers between devices with their start and end apart: 5, of which 4 were waited for; matrix products, arithmetic and copies ran while one was open for 4% of the time, Pallas kernels for 0%

profile of v9, /device:TPU:2, one launch (start us, length us, event | category | flops | bytes accessed | tf_op | source)
XLA Modules:
  0.0 325.4 jit_solution(1858075107837802044)
XLA Ops:
  7.2 2.8 shard_map.128
  10.0 0.0 copy-start.6
  10.0 0.0 copy-start.4
  10.0 0.0 copy-start.7
  10.0 0.0 copy-start.8
  10.0 0.0 copy-start.9
  10.0 11.6 %all-to-all-start = ((bf16[32,3,8,768]{3,2,1,0:T(8,128)(2,1)}), bf16[32,3,8,768]{3,2,1,0:T(8,128)(2,1)S(1)}, u32[]{:S(2)}, u32[]{:S(2)}) async-start(bf16[32,3,8,768]{3,2,1,0:T(8,128)(2,1)} %shard_map.128), calls=%async_computation | async-start | bytes 2359296 | tf_op jit(solution)/shard_map/all_to_all | solution.py:257
  21.6 0.0 all-gather.2.cloned.1.call-start
  21.7 0.0 copy-done.6
  21.7 0.1 copy.46
  21.8 0.1 eq.120
  21.9 0.1 eq.109
  22.1 0.6 reduce-window.6
  22.7 0.2 slice_reduce_fusion
  22.9 0.1 broadcast_add_fusion.1
  23.1 0.0 copy-done.4
  23.1 0.1 fusion.25
  23.1 0.1 reduce_window_sum.26
  23.2 0.2 fusion.22
  23.4 0.1 and_select_fusion
  23.5 0.1 fusion.24
  23.6 0.1 select_reduce_fusion
  23.7 0.1 add.41
  23.8 0.1 copy.50
  23.9 0.1 copy.51
  24.0 0.0 copy-done.7
  24.1 0.0 copy-done.8
  24.1 0.0 copy-done.9
  24.1 3.6 %convolution_convert_fusion = bf16[1024,2048]{1,0:T(8,128)(2,1)} fusion(bf16[128,2048]{1,0:T(8,128)(2,1)S(1)} %copy-done.8, bf16[128,2048]{1,0:T(8,128)(2,1)S(1)} %copy-done.9, s32[256]{0:T(256)S(1)} %bitcast.39, s32[256]{0:T(256)S(1)} %bitcast.38, bf16[256]{0:T(256)(128)(2,1)S(1)} %get-tuple-element.46, bf16[256]{0:T(256)(128)(2,1)S(1)} %get-tuple-element.45), kind=kOutput, calls=%fused_computation | convolution fusion | flops 1080033280 | bytes 5245952 | tf_op jit(solution)/shard_map/tb,td->bd/dot_general | solution.py:285
  27.7 25.3 %all-to-all-done = bf16[32,3,8,768]{3,2,1,0:T(8,128)(2,1)S(1)} async-done(((bf16[32,3,8,768]{3,2,1,0:T(8,128)(2,1)}), bf16[32,3,8,768]{3,2,1,0:T(8,128)(2,1)S(1)}, u32[]{:S(2)}, u32[]{:S(2)}) %all-to-all-start) | async-done | bytes 1179680 | tf_op jit(solution)/shard_map/all_to_all | solution.py:257
  53.0 1.1 copy_bitcast_fusion.2
  54.1 0.0 all-gather.2.cloned.1.call-update
  54.1 0.0 reduce-scatter.2.cloned.1.call-start
  54.1 101.0 %all_to_all.25 = bf16[32,32,2048]{2,1,0:T(8,128)(2,1)} all-to-all(bf16[32,32,2048]{2,1,0:T(8,128)(2,1)} %bitcast.35), channel_id=1, replica_groups=mesh['dp'=8,'expert'=32] {'expert'}, dimensions={0} | all-to-all | bytes 8388608 | tf_op jit(solution)/shard_map/all_to_all | solution.py:300
  155.1 0.0 all-gather.2.cloned.1.call-done.refs_2_.refs_3_.refs_4_
  155.1 0.0 copy-start
  155.1 2.2 copy-done
  157.3 20.3 %shard_map.129 = (bf16[3,2048,768]{2,1,0:T(8,128)(2,1)}, bf16[512,2176]{1,0:T(8,128)(2,1)}) custom-call(bf16[32,2,16,2048]{3,2,1,0:T(8,128)(2,1)S(1)} %bitcast.33, bf16[32,2,16,2048]{3,2,1,0:T(8,128)(2,1)S(1)} %bitcast.34, bf16[8,3,256,768]{3,2,1,0:T(8,128)(2,1)} %all-gather.2.cloned.1.call-done.refs_2_.refs_3_.refs_4_, ...), custom_call_target="tpu_custom_call" | custom-call | flops 12884901888 | bytes 36000000 | tf_op jit(solution)/shard_map/pallas_call | solution.py:123
  177.6 0.0 reduce-scatter.2.cloned.1.call-update
  177.6 5.0 %all-to-all-start.2 = ((bf16[32,16,2176]{2,1,0:T(8,128)(2,1)}), bf16[32,16,2176]{2,1,0:T(8,128)(2,1)}, u32[]{:S(2)}, u32[]{:S(2)}) async-start(bf16[32,16,2176]{2,1,0:T(8,128)(2,1)} %bitcast.9), calls=%async_computation.3 | async-start | bytes 4456448 | tf_op jit(solution)/shard_map/all_to_all | solution.py:306
  182.7 49.1 %reduce-scatter.2.cloned.1.call-done = bf16[3,256,768]{2,1,0:T(8,128)(2,1)} async-done(((bf16[3,2048,768]{2,1,0:T(8,128)(2,1)}), bf16[3,256,768]{2,1,0:T(8,128)(2,1)}) %reduce-scatter.2.cloned.1.call-update) | async-done | bytes 1179664 | tf_op jit(solution)/shard_map/reduce_scatter | solution.py:304
  231.7 1.3 copy_bitcast_fusion.1
  233.1 0.0 copy-start.1
  233.1 0.0 copy-start.2
  233.1 0.0 copy-start.5
  233.1 1.8 all-to-all-done.2
  234.9 41.7 %all_to_all.26.returned_ref = bf16[32,3,8,768]{3,2,1,0:T(8,128)(2,1)S(1)} all-to-all(bf16[32,3,8,768]{3,2,1,0:T(8,128)(2,1)S(1)} %copy_bitcast_fusion.1), channel_id=1, replica_groups=mesh['dp'=8,'expert'=32] {'expert'}, dimensions={0} | all-to-all | bytes 2359296 | tf_op jit(solution)/shard_map/all_to_all | solution.py:322
  276.6 0.0 copy-done.1
  276.6 0.0 copy-done.2
  276.6 0.0 copy-done.5
  276.6 0.0 copy-start.3
  276.6 1.4 copy-done.3
  278.0 3.5 %shard_map.130 = (f32[3,20,8,768]{3,2,1,0:T(8,128)}, f32[3,20,8,768]{3,2,1,0:T(8,128)}, bf16[32,3,8,768]{3,2,1,0:T(8,128)(2,1)}) custom-call(s32[32]{0:T(128)S(1)} %copy-done.4, s32[20]{0:T(128)S(1)} %copy-done.5, bf16[32,3,8,768]{3,2,1,0:T(8,128)(2,1)S(1)} %all_to_all.26.returned_ref, bf16[3,20,8,768]{3,2,1,0:T(8,128)(2,1)S(1)} %copy-done.1, ...), custom_call_target="tpu_custom_call" | custom-call | flops 7372800 | bytes 9000000 | tf_op jit(solution)/shard_map/pallas_call | solution.py:193
  281.5 4.4 %all-to-all-start.4 = ((bf16[32,3,8,768]{3,2,1,0:T(8,128)(2,1)}), bf16[32,3,8,768]{3,2,1,0:T(8,128)(2,1)S(1)}, u32[]{:S(2)}, u32[]{:S(2)}) async-start(bf16[32,3,8,768]{3,2,1,0:T(8,128)(2,1)} %get-tuple-element.20), calls=%async_computation.5 | async-start | bytes 2359296 | tf_op jit(solution)/shard_map/all_to_all | solution.py:326
  285.9 0.1 copy.54
  286.0 0.1 add.39
  286.1 0.1 copy.49
  286.2 0.1 fusion.12
  286.3 1.2 convolution_reduce_fusion
  287.5 0.1 reshape_squeeze.3
  287.7 0.6 copy.56
  288.3 2.9 convolution_convert_fusion.1
  291.2 26.3 %all-to-all-done.4 = bf16[32,3,8,768]{3,2,1,0:T(8,128)(2,1)S(1)} async-done(((bf16[32,3,8,768]{3,2,1,0:T(8,128)(2,1)}), bf16[32,3,8,768]{3,2,1,0:T(8,128)(2,1)S(1)}, u32[]{:S(2)}, u32[]{:S(2)}) %all-to-all-start.4) | async-done | bytes 1179680 | tf_op jit(solution)/shard_map/all_to_all | solution.py:326
  317.5 1.1 copy_bitcast_fusion
  (11 shorter events, 0.2 us)
Async XLA Ops:
  10.0 11.7 %copy-start.6 = (s32[128,2]{0,1:T(2,128)S(1)}, s32[128,2]{0,1:T(2,128)}, u32[]{:S(2)}) copy-start(s32[128,2]{0,1:T(2,128)} %param.11) | copy-start | bytes 3076
  10.0 13.1 %copy-start.4 = (s32[32]{0:T(128)S(1)}, s32[32]{0:T(128)}, u32[]{:S(2)}) copy-start(s32[32]{0:T(128)} %new_place_ref.3) | copy-start | bytes 388
  10.0 14.0 %copy-start.7 = (bf16[128,2]{0,1:T(2,128)(2,1)S(1)}, bf16[128,2]{0,1:T(2,128)(2,1)}, u32[]{:S(2)}) copy-start(bf16[128,2]{0,1:T(2,128)(2,1)} %param.12) | copy-start | bytes 1540
  10.0 14.1 %copy-start.8 = (bf16[128,2048]{1,0:T(8,128)(2,1)S(1)}, bf16[128,2048]{1,0:T(8,128)(2,1)}, u32[]{:S(2)}) copy-start(bf16[128,2048]{1,0:T(8,128)(2,1)} %param.10) | copy-start | bytes 1572868
  10.0 14.1 %copy-start.9 = (bf16[128,2048]{1,0:T(8,128)(2,1)S(1)}, bf16[128,2048]{1,0:T(8,128)(2,1)}, u32[]{:S(2)}) copy-start(bf16[128,2048]{1,0:T(8,128)(2,1)} %param.9) | copy-start | bytes 1572868
  10.0 43.0 %all-to-all-start = ((bf16[32,3,8,768]{3,2,1,0:T(8,128)(2,1)}), bf16[32,3,8,768]{3,2,1,0:T(8,128)(2,1)S(1)}, u32[]{:S(2)}, u32[]{:S(2)}) async-start(bf16[32,3,8,768]{3,2,1,0:T(8,128)(2,1)} %shard_map.128), calls=%async_computation | async-start | bytes 2359296 | tf_op jit(solution)/shard_map/all_to_all | solution.py:257
  21.6 133.5 %all-gather.2.cloned.1.call-start = ((), (), s32[]{:S(2)}) async-start(), calls=%async_computation.6 | async-start | bytes 10616832 | tf_op jit(solution)/shard_map/all_gather | solution.py:295
  54.1 177.6 %reduce-scatter.2.cloned.1.call-start = ((), (), s32[]{:S(2)}) async-start(), calls=%async_computation.7 | async-start | bytes 10616832 | tf_op jit(solution)/shard_map/reduce_scatter | solution.py:304
  155.1 2.2 copy-start
  177.6 57.3 %all-to-all-start.2 = ((bf16[32,16,2176]{2,1,0:T(8,128)(2,1)}), bf16[32,16,2176]{2,1,0:T(8,128)(2,1)}, u32[]{:S(2)}, u32[]{:S(2)}) async-start(bf16[32,16,2176]{2,1,0:T(8,128)(2,1)} %bitcast.9), calls=%async_computation.3 | async-start | bytes 4456448 | tf_op jit(solution)/shard_map/all_to_all | solution.py:306
  233.1 43.5 %copy-start.1 = (bf16[3,20,8,768]{3,2,1,0:T(8,128)(2,1)S(1)}, bf16[3,20,8,768]{3,2,1,0:T(8,128)(2,1)}, u32[]{:S(2)}) copy-start(bf16[3,20,8,768]{3,2,1,0:T(8,128)(2,1)} %stored_ref.3) | copy-start | bytes 2211844
  233.1 43.5 %copy-start.2 = (f32[3,20,8,768]{3,2,1,0:T(8,128)S(1)}, f32[3,20,8,768]{3,2,1,0:T(8,128)}, u32[]{:S(2)}) copy-start(f32[3,20,8,768]{3,2,1,0:T(8,128)} %first_ref.1) | copy-start | bytes 4423684
  233.1 43.5 %copy-start.5 = (s32[20]{0:T(128)S(1)}, s32[20]{0:T(128)}, u32[]{:S(2)}) copy-start(s32[20]{0:T(128)} %old_place_ref.3) | copy-start | bytes 244
  276.6 1.4 copy-start.3
  281.5 36.0 %all-to-all-start.4 = ((bf16[32,3,8,768]{3,2,1,0:T(8,128)(2,1)}), bf16[32,3,8,768]{3,2,1,0:T(8,128)(2,1)S(1)}, u32[]{:S(2)}, u32[]{:S(2)}) async-start(bf16[32,3,8,768]{3,2,1,0:T(8,128)(2,1)} %get-tuple-element.20), calls=%async_computation.5 | async-start | bytes 2359296 | tf_op jit(solution)/shard_map/all_to_all | solution.py:326
Sparse Core Ops, SparseCore 0:
  54.2 52.5 all-gather.1
  177.7 53.9 reduce-scatter.1
